TPU v7x, 128 devices: a whole 4x4x4 slice. The times are simulated.
128 devices in a mesh: rows: 16 (over z, x_hi, core), kern: 8 (over y, x_lo).
Axes of the slice: x: 4 (x_hi: 2, x_lo: 2; x = x_hi * 2 + x_lo), y: 4, z: 4, core: 2. Of those that a mesh axis runs over, the one named last changes fastest.
Arguments:
- mask_params: float32 [16384, 16384], P(('rows', 'kern')), may hold values from -6 to 6
- pupil_kernels: float32 [16, 2, 2, 256, 256], P('kern'), may hold values from -0.005859375 to 0.005859375
- target_pattern: int32 [4096, 4096], P('rows', 'kern'), may hold values 0 or 1
Outputs:
- stepped_params: float32 [16384, 16384], P(('rows', 'kern'))
All inputs are finite; a program needn't handle non-finite values. No bound on the sum of `target_pattern` on one device may be relied on, other than what follows from the above.
Results may differ from a plain program's by a relative error of at most 0.0081.
Values may be sent and summed in bfloat16 or wider, within the bound.
No kernel may reach another device: no remote copies, remote signals or barrier semaphores. Data moves between devices by JAX's collectives and lax.ppermute only.
A program may use at most 256 MiB of HBM per device.

v0:
```python
import math

import jax
import jax.numpy as jnp
from jax import lax
from jax.sharding import PartitionSpec as P

MASK = 16384
GRID = 4096
BAND = 256


steepness = 4.0
threshold = 0.75
step_size = 1.0
dose_levels = (1.0, 1.15)


def band_table(positions, period, band_size):
    frequency = (jnp.arange(band_size, dtype=jnp.int32) - band_size // 2) % period
    product = positions[:, None] * frequency[None, :] % period
    angles = product.astype(jnp.float32) * (2.0 * math.pi / period)
    return (jnp.cos(angles), jnp.sin(angles))


def column_table():
    cosine, sine = band_table(jnp.arange(MASK, dtype=jnp.int32), MASK, BAND)
    return (jnp.concatenate([cosine, -sine], 1) * (1.0 / MASK)).astype(jnp.bfloat16)


def grid_tables(row_positions):
    cosine, sine = band_table(row_positions, GRID, BAND)
    rows_table = jnp.concatenate([cosine, sine], 1).astype(jnp.bfloat16)
    all_cos, all_sin = band_table(jnp.arange(GRID, dtype=jnp.int32), GRID, BAND)
    upper = jnp.concatenate([all_cos.T, all_sin.T], 1)
    lower = jnp.concatenate([-all_sin.T, all_cos.T], 1)
    column_map = jnp.concatenate([upper, lower], 0).astype(jnp.bfloat16)
    return (rows_table, column_map)


def hdot(left, right):
    return jnp.dot(left, right, precision=lax.Precision.HIGHEST, preferred_element_type=jnp.float32)


def field_of(spec_re, spec_im, kernel_re, kernel_im, rows_table, column_map):
    amp_re = kernel_re * spec_re - kernel_im * spec_im
    amp_im = kernel_re * spec_im + kernel_im * spec_re
    block = jnp.concatenate(
        [jnp.concatenate([amp_re, amp_im], 1), jnp.concatenate([-amp_im, amp_re], 1)], 0
    ).astype(jnp.bfloat16)
    partial_value = jnp.dot(rows_table, block, preferred_element_type=jnp.float32).astype(
        jnp.bfloat16
    )
    return jnp.dot(partial_value, column_map, preferred_element_type=jnp.float32)


def spectrum_adjoint(field, adjoint, kernel_re, kernel_im, rows_table, column_map):
    row_count = field.shape[0]
    grid_size = adjoint.shape[1]
    weighted = (
        (2.0 * field.reshape(row_count, 2, grid_size) * adjoint.astype(jnp.float32)[:, None, :])
        .reshape(row_count, 2 * grid_size)
        .astype(jnp.bfloat16)
    )
    back = jnp.dot(weighted, column_map.T, preferred_element_type=jnp.float32).astype(jnp.bfloat16)
    grads = jnp.dot(rows_table.T, back, preferred_element_type=jnp.float32)
    band_size = kernel_re.shape[0]
    grad_re = grads[:band_size, :band_size] + grads[band_size:, band_size:]
    grad_im = grads[:band_size, band_size:] - grads[band_size:, :band_size]
    return (kernel_re * grad_re + kernel_im * grad_im, kernel_re * grad_im - kernel_im * grad_re)


def resist_adjoint(intensity, target):
    dose = jnp.array(dose_levels, jnp.float32)[:, None, None]
    resist = jax.nn.sigmoid(steepness * (dose * intensity - threshold))
    wanted = target.astype(jnp.float32)[None]
    return (2.0 * (resist - wanted) * resist * (1.0 - resist) * steepness * dose).astype(
        jnp.bfloat16
    )


def local(mask_params, pupil_kernels, target_pattern):
    mask_rows = mask_params.shape[0]
    mask_start = lax.axis_index(("rows", "kern")) * mask_rows
    transmit = jnp.tanh(mask_params)
    table = column_table()
    column_spec = jnp.dot(transmit.astype(jnp.bfloat16), table, preferred_element_type=jnp.float32)
    row_cos, row_sin = band_table(mask_start + jnp.arange(mask_rows, dtype=jnp.int32), MASK, BAND)
    col_re = column_spec[:, :BAND]
    col_im = column_spec[:, BAND:]
    local_re = hdot(row_cos.T, col_re) + hdot(row_sin.T, col_im)
    local_im = hdot(row_cos.T, col_im) - hdot(row_sin.T, col_re)
    spec_re, spec_im = lax.psum((local_re, local_im), ("rows", "kern"))
    grid_rows = GRID // lax.axis_size("rows")
    grid_start = lax.axis_index("rows") * grid_rows
    rows_table, column_map = grid_tables(grid_start + jnp.arange(grid_rows, dtype=jnp.int32))
    members = pupil_kernels.shape[0]
    fields = []
    powers = [jnp.zeros((grid_rows, GRID), jnp.float32), jnp.zeros((grid_rows, GRID), jnp.float32)]
    for member in range(members):
        for corner in range(2):
            field = field_of(
                spec_re,
                spec_im,
                pupil_kernels[member, corner, 0],
                pupil_kernels[member, corner, 1],
                rows_table,
                column_map,
            )
            fields.append(field)
            powers[corner] = (
                powers[corner]
                + field[:, :GRID] * field[:, :GRID]
                + field[:, GRID:] * field[:, GRID:]
            )
    partial_power = jnp.stack(powers)
    slab_cols = GRID // lax.axis_size("kern")
    total_power = lax.psum(partial_power.astype(jnp.bfloat16), "kern").astype(jnp.float32)
    slab_power = lax.dynamic_slice_in_dim(
        total_power, lax.axis_index("kern") * slab_cols, slab_cols, 2
    )
    slab_adjoint = resist_adjoint(slab_power, target_pattern)
    adjoint = lax.all_gather(slab_adjoint, "kern", axis=2, tiled=True)
    total_re = jnp.zeros((BAND, BAND), jnp.float32)
    total_im = jnp.zeros((BAND, BAND), jnp.float32)
    for member in range(members):
        for corner in range(2):
            grad_re, grad_im = spectrum_adjoint(
                fields[2 * member + corner],
                adjoint[corner],
                pupil_kernels[member, corner, 0],
                pupil_kernels[member, corner, 1],
                rows_table,
                column_map,
            )
            total_re = total_re + grad_re
            total_im = total_im + grad_im
    spec_grad_re, spec_grad_im = lax.psum((total_re, total_im), ("rows", "kern"))
    col_grad_re = hdot(row_cos, spec_grad_re) - hdot(row_sin, spec_grad_im)
    col_grad_im = hdot(row_sin, spec_grad_re) + hdot(row_cos, spec_grad_im)
    col_grad = jnp.concatenate([col_grad_re, col_grad_im], 1).astype(jnp.bfloat16)
    pixel_grad = jnp.dot(col_grad, table.T, preferred_element_type=jnp.float32)
    return mask_params - step_size * pixel_grad * (1.0 - transmit * transmit)


def solution(mesh):
    placed = (P(("rows", "kern"), None), P("kern", None, None, None, None), P("rows", "kern"))
    return jax.shard_map(
        local, mesh=mesh, in_specs=placed, out_specs=P(("rows", "kern"), None), check_vma=False
    )
```

profile of v0, /device:TPU:1, one launch (start us, length us, event | category | flops | bytes accessed | tf_op | source)
XLA Modules:
  0.0 858.1 jit_solution(7653969498916827332)
XLA Ops:
  6.6 68.2 %fusion.8 = (f32[16384,256]{1,0:T(8,128)}, f32[16384,256]{1,0:T(8,128)}) fusion(s32[256]{0:T(256)S(1)} %and_select_fusion.1), kind=kLoop, calls=%fused_computation.19 | loop fusion | flops 62914560 | bytes 33555456 | tf_op jit(solution)/shard_map/cos | solution.py:23
  74.7 14.9 %fusion.40 = f32[128,512]{0,1:T(8,128)S(1)} fusion(f32[128,16384]{1,0:T(8,128)} %param.4, f32[16384,256]{1,0:T(8,128)} %get-tuple-element.35, f32[16384,256]{1,0:T(8,128)} %get-tuple-element.34), kind=kOutput, calls=%fused_computation.74 | convolution fusion | flops 2174746624 | bytes 42205184 | tf_op jit(solution)/shard_map/dot_general | solution.py:87
  95.2 19.5 %fusion.29 = (bf16[256,4096]{1,0:T(8,128)(2,1)}, bf16[256,4096]{1,0:T(8,128)(2,1)}, bf16[256,4096]{1,0:T(8,128)(2,1)}) fusion(s32[256]{0:T(256)S(1)} %get-tuple-element.40), kind=kLoop, calls=%fused_computation.57 | loop fusion | flops 18874368 | bytes 6292480 | tf_op jit(solution)/shard_map/convert.29
  115.9 128.0 %all-reduce.10.cloned.1.call-done = (f32[256,256]{1,0:T(8,128)}, f32[256,256]{1,0:T(8,128)}) async-done(((f32[256,256]{1,0:T(8,128)}, f32[256,256]{1,0:T(8,128)}), (f32[256,256]{1,0:T(8,128)}, f32[256,256]{1,0:T(8,128)})) %all-reduce.10.cloned.1.call-update) | async-done | bytes 524304 | tf_op jit(solution)/shard_map/psum | solution.py:93
  243.9 2.2 fusion.204
  246.8 13.4 %fusion.44 = f32[256,8192]{1,0:T(8,128)} fusion(bf16[256,256]{1,0:T(8,128)(2,1)} %get-tuple-element.25, bf16[256,256]{1,0:T(8,128)(2,1)} %get-tuple-element.38, bf16[256,256]{1,0:T(8,128)(2,1)} %get-tuple-element.9, bf16[256,256]{1,0:T(8,128)(2,1)S(1)} %get-tuple-element.30, bf16[256,256]{1,0:T(8,128)(2,1)S(1)} %get-tuple-element.29, ...), kind=kOutput, calls=%fused_computation.80 | convolution fusion | flops 2318008320 | bytes 15335424 | tf_op jit(solution)/shard_map/dot_general | solution.py:54
  260.2 12.3 %fusion.43 = f32[256,8192]{1,0:T(8,128)} fusion(bf16[256,256]{1,0:T(8,128)(2,1)S(1)} %copy-done.7, bf16[256,256]{1,0:T(8,128)(2,1)S(1)} %copy-done.8, bf16[256,256]{1,0:T(8,128)(2,1)S(1)} %copy-done.6, bf16[256,256]{1,0:T(8,128)(2,1)S(1)} %get-tuple-element.30, bf16[256,256]{1,0:T(8,128)(2,1)S(1)} %get-tuple-element.29, ...), kind=kOutput, calls=%fused_computation.79 | convolution fusion | flops 2318008320 | bytes 15335424 | tf_op jit(solution)/shard_map/dot_general | solution.py:54
  272.5 8.0 fusion.30
  280.6 12.7 %fusion.45 = f32[256,8192]{1,0:T(8,128)} fusion(bf16[256,256]{1,0:T(8,128)(2,1)S(1)} %copy-done.5, bf16[256,256]{1,0:T(8,128)(2,1)S(1)} %get-tuple-element.37, bf16[256,256]{1,0:T(8,128)(2,1)S(1)} %copy-done.4, bf16[256,256]{1,0:T(8,128)(2,1)S(1)} %get-tuple-element.30, bf16[256,256]{1,0:T(8,128)(2,1)S(1)} %get-tuple-element.29, ...), kind=kOutput, calls=%fused_computation.81 | convolution fusion | flops 2318008320 | bytes 15335424 | tf_op jit(solution)/shard_map/dot_general | solution.py:54
  293.3 12.3 %fusion.46 = f32[256,8192]{1,0:T(8,128)} fusion(bf16[256,256]{1,0:T(8,128)(2,1)S(1)} %copy-done.3, bf16[256,256]{1,0:T(8,128)(2,1)S(1)} %get-tuple-element.36, bf16[256,256]{1,0:T(8,128)(2,1)S(1)} %get-tuple-element.19, bf16[256,256]{1,0:T(8,128)(2,1)S(1)} %get-tuple-element.30, bf16[256,256]{1,0:T(8,128)(2,1)S(1)} %get-tuple-element.29, ...), kind=kOutput, calls=%fused_computation.82 | convolution fusion | flops 2318008320 | bytes 15335424 | tf_op jit(solution)/shard_map/dot_general | solution.py:54
  305.6 6.7 fusion.31
  312.4 2.4 pad_maximum_fusion
  314.9 181.2 %all-reduce.6.cloned.1.call-done = bf16[2,256,4096]{2,1,0:T(8,128)(2,1)} async-done(((bf16[2,256,4096]{2,1,0:T(8,128)(2,1)}), bf16[2,256,4096]{2,1,0:T(8,128)(2,1)}) %all-reduce.6.cloned.1.call-update) | async-done | bytes 4194320 | tf_op jit(solution)/shard_map/psum | solution.py:118
  496.1 2.4 multiply_convert_fusion.24
  498.6 10.6 %maximum_maximum_fusion = bf16[512,8192]{1,0:T(8,128)(2,1)} fusion(bf16[256,4096]{1,0:T(8,128)(2,1)} %get-tuple-element.33, bf16[256,4096]{1,0:T(8,128)(2,1)} %get-tuple-element.32, bf16[256,4096]{1,0:T(8,128)(2,1)} %get-tuple-element.31), kind=kLoop, calls=%fused_computation.14 | loop fusion | flops 33554432 | bytes 14680064 | tf_op jit(solution)/shard_map/concatenate | solution.py:37
  509.2 80.2 %all-gather.2.cloned.1.call-done = bf16[2,256,4096]{2,1,0:T(8,128)(2,1)} async-done(((bf16[2,256,512]{2,1,0:T(8,128)(2,1)}), bf16[2,256,4096]{2,1,0:T(8,128)(2,1)}) %all-gather.2.cloned.1.call-update) | async-done | bytes 4194320 | tf_op jit(solution)/shard_map/all_gather | solution.py:123
  589.4 5.0 multiply_bitcast_fusion
  594.4 4.8 mul.413
  599.1 10.9 %copy.6 = f32[32,8,2,4096]{3,1,2,0:T(8,128)} copy(f32[32,8,2,4096]{3,2,1,0:T(2,128)S(1)} %bitcast.170) | data formatting | bytes 16777216
  610.0 10.8 %fusion.33 = f32[512,512]{1,0:T(8,128)S(1)} fusion(bf16[512,8192]{1,0:T(8,128)(2,1)} %maximum_maximum_fusion, f32[256,8192]{1,0:T(8,128)} %fusion.46, f32[256,8192]{1,0:T(8,128)} %bitcast.168, bf16[256,256]{1,0:T(8,128)(2,1)S(1)} %get-tuple-element.30, bf16[256,256]{1,0:T(8,128)(2,1)S(1)} %get-tuple-element.29), kind=kOutput, calls=%fused_computation.61 | convolution fusion | flops 2286551040 | bytes 26476544 | tf_op jit(solution)/shard_map/dot_general | solution.py:66
  620.8 12.0 %fusion.37 = f32[512,512]{1,0:T(8,128)} fusion(bf16[512,8192]{1,0:T(8,128)(2,1)} %maximum_maximum_fusion, f32[256,8192]{1,0:T(8,128)} %fusion.45, f32[256,8192]{1,0:T(8,128)} %bitcast.169, bf16[256,256]{1,0:T(8,128)(2,1)S(1)} %get-tuple-element.30, bf16[256,256]{1,0:T(8,128)(2,1)S(1)} %get-tuple-element.29), kind=kOutput, calls=%fused_computation.65 | convolution fusion | flops 2286551040 | bytes 26476544 | tf_op jit(solution)/shard_map/dot_general | solution.py:66
  632.8 5.7 mul.406
  638.6 10.9 %copy.5 = f32[32,8,2,4096]{3,1,2,0:T(8,128)} copy(f32[32,8,2,4096]{3,2,1,0:T(2,128)S(1)} %bitcast.171) | data formatting | bytes 16777216
  649.5 11.8 %fusion.35 = f32[512,512]{1,0:T(8,128)} fusion(bf16[512,8192]{1,0:T(8,128)(2,1)} %maximum_maximum_fusion, f32[256,8192]{1,0:T(8,128)} %fusion.44, f32[256,8192]{1,0:T(8,128)} %bitcast.166, bf16[256,256]{1,0:T(8,128)(2,1)S(1)} %get-tuple-element.30, bf16[256,256]{1,0:T(8,128)(2,1)S(1)} %get-tuple-element.29), kind=kOutput, calls=%fused_computation.63 | convolution fusion | flops 2286551040 | bytes 26476544 | tf_op jit(solution)/shard_map/dot_general | solution.py:66
  661.3 12.0 %fusion.39 = f32[512,512]{1,0:T(8,128)} fusion(bf16[512,8192]{1,0:T(8,128)(2,1)} %maximum_maximum_fusion, f32[256,8192]{1,0:T(8,128)} %fusion.43, f32[256,8192]{1,0:T(8,128)} %bitcast.167, bf16[256,256]{1,0:T(8,128)(2,1)S(1)} %get-tuple-element.30, bf16[256,256]{1,0:T(8,128)(2,1)S(1)} %get-tuple-element.29), kind=kOutput, calls=%fused_computation.67 | convolution fusion | flops 2286551040 | bytes 26476544 | tf_op jit(solution)/shard_map/dot_general | solution.py:66
  673.3 2.9 fusion.114
  676.3 2.9 fusion.112
  679.2 145.9 %all-reduce.8.cloned.1.call-done = (f32[256,256]{1,0:T(8,128)}, f32[256,256]{1,0:T(8,128)}) async-done(((f32[256,256]{1,0:T(8,128)}, f32[256,256]{1,0:T(8,128)}), (f32[256,256]{1,0:T(8,128)}, f32[256,256]{1,0:T(8,128)})) %all-reduce.8.cloned.1.call-update) | async-done | bytes 524304 | tf_op jit(solution)/shard_map/psum | solution.py:138
  826.9 1.8 fusion.153
  828.7 1.8 fusion.41
  830.5 1.8 fusion.42
  832.3 18.8 %fusion.1 = f32[128,16384]{1,0:T(8,128)} fusion(f32[128,16384]{1,0:T(8,128)} %param.4, f32[16384,256]{1,0:T(8,128)} %get-tuple-element.35, f32[16384,256]{1,0:T(8,128)} %get-tuple-element.34, bf16[128,256]{1,0:T(8,128)(2,1)S(1)} %fusion.42, bf16[128,256]{1,0:T(8,128)(2,1)S(1)} %fusion.41), kind=kOutput, calls=%fused_computation.6 | convolution fusion | flops 2181300224 | bytes 50462720 | tf_op jit(solution)/shard_map/dot_general | solution.py:142
  (42 shorter events, 9.5 us)
Async XLA Ops:
  6.5 237.3 %all-reduce.10.cloned.1.call-start = ((), (), s32[]{:S(2)}) async-start(), calls=%async_computation.3 | async-start | bytes 1048576 | tf_op jit(solution)/shard_map/psum | solution.py:93
  89.7 154.2 %copy-start = (f32[2,2,2,256,256]{4,3,2,1,0:T(8,128)S(1)}, f32[2,2,2,256,256]{4,3,2,1,0:T(8,128)}, u32[]{:S(2)}) copy-start(f32[2,2,2,256,256]{4,3,2,1,0:T(8,128)} %param.5) | copy-start | bytes 6291460
  94.9 401.2 %all-reduce.6.cloned.1.call-start = ((), (), s32[]{:S(2)}) async-start(), calls=%async_computation | async-start | bytes 8388608 | tf_op jit(solution)/shard_map/psum | solution.py:118
  246.8 13.4 %copy-start.6 = (bf16[256,256]{1,0:T(8,128)(2,1)S(1)}, bf16[256,256]{1,0:T(8,128)(2,1)}, u32[]{:S(2)}) copy-start(bf16[256,256]{1,0:T(8,128)(2,1)} %get-tuple-element.26) | copy-start | bytes 393220
  246.8 13.4 %copy-start.7 = (bf16[256,256]{1,0:T(8,128)(2,1)S(1)}, bf16[256,256]{1,0:T(8,128)(2,1)}, u32[]{:S(2)}) copy-start(bf16[256,256]{1,0:T(8,128)(2,1)} %get-tuple-element.28) | copy-start | bytes 393220
  246.8 13.4 %copy-start.8 = (bf16[256,256]{1,0:T(8,128)(2,1)S(1)}, bf16[256,256]{1,0:T(8,128)(2,1)}, u32[]{:S(2)}) copy-start(bf16[256,256]{1,0:T(8,128)(2,1)} %get-tuple-element.39) | copy-start | bytes 393220
  272.5 8.0 copy-start.4
  272.5 8.0 copy-start.5
  280.5 12.7 %copy-start.3 = (bf16[256,256]{1,0:T(8,128)(2,1)S(1)}, bf16[256,256]{1,0:T(8,128)(2,1)}, u32[]{:S(2)}) copy-start(bf16[256,256]{1,0:T(8,128)(2,1)} %get-tuple-element.21) | copy-start | bytes 393220
  305.6 6.8 copy-start.1
  312.3 2.5 copy-start.2
  312.3 183.8 %copy-start.9 = (f32[2]{0:T(128)S(1)}, f32[2]{0:T(128)}, u32[]{:S(2)}) copy-start(f32[2]{0:T(128)} %constant.106.clone) | copy-start | bytes 28
  312.4 183.8 %copy-start.10 = (f32[2]{0:T(128)S(1)}, f32[2]{0:T(128)}, u32[]{:S(2)}) copy-start(f32[2]{0:T(128)} %constant.108) | copy-start | bytes 28
  314.8 274.6 %all-gather.2.cloned.1.call-start = ((), (), s32[]{:S(2)}) async-start(), calls=%async_computation.1 | async-start | bytes 4718592 | tf_op jit(solution)/shard_map/all_gather | solution.py:123
  498.5 326.6 %all-reduce.8.cloned.1.call-start = ((), (), s32[]{:S(2)}) async-start(), calls=%async_computation.2 | async-start | bytes 1048576 | tf_op jit(solution)/shard_map/psum | solution.py:138
Sparse Core Ops, SparseCore 0:
  95.0 148.8 all-reduce.9
  314.9 181.1 all-reduce.5
  498.7 90.6 all-gather.1
  679.4 145.7 all-reduce.7
where the time goes:
time: 864 us; the launch traced here: 858 us
  waiting for transfers between devices  535 us (62%)
  matrix products  143 us (17%)
  other arithmetic  133 us (15%)
  local copies, waits for them, and re-layouts  32.4 us (4%)
  between operations  13.8 us (2%)
    psum x1, waiting for transfers between devices, local(): lax.psum(partial_power.astype(jnp.bfloat16), 'kern').astype(jnp.float32)  181 us
    psum x1, waiting for transfers between devices, local(): lax.psum((total_re, total_im), ('rows', 'kern'))  146 us
    psum x1, waiting for transfers between devices, local(): spec_re, spec_im = lax.psum((local_re, local_im), ('rows', 'kern'))  128 us
    all_gather x1, waiting for transfers between devices, local(): adjoint = lax.all_gather(slab_adjoint, 'kern', axis=2, tiled=True)  80.2 us
    cos x1, other arithmetic, band_table(): return (jnp.cos(angles), jnp.sin(angles))  68.2 us
    dot_general x4, matrix products, field_of(): jnp.dot(partial_value, column_map, preferred_element_type=jnp.float32)  50.6 us
    dot_general x4, matrix products, spectrum_adjoint(): grads = jnp.dot(rows_table.T, back, preferred_element_type=jnp.float32)  46.6 us
    another operation x5, other arithmetic  23.7 us
  transfers between devices with their start and end apart: 4, of which 4 were waited for; matrix products, arithmetic and copies ran while one was open for 4% of the time, Pallas kernels for 0%

commit v1 on v0

v1 whole, which is shorter than its diff:
```python
import math

import jax
import jax.numpy as jnp
import numpy as np
from jax import lax
from jax.experimental import pallas as pl
from jax.experimental.pallas import tpu as pltpu
from jax.sharding import PartitionSpec as P

MASK = 16384
GRID = 4096
BAND = 256
COARSE = 512
STEP = 256
STEPS = MASK // STEP
ROWS = 16
KERN = 8
DEVICES = ROWS * KERN

steepness = 4.0
threshold = 0.75
step_size = 1.0
dose_levels = (1.0, 1.15)

VMEM_LIMIT = 56 * 1024 * 1024
HIGHEST = lax.Precision.HIGHEST


def tables(positions, period):
    frequency = np.arange(BAND) - BAND // 2
    angles = (np.outer(positions, frequency) % period) * (2.0 * math.pi / period)
    return np.cos(angles), np.sin(angles)


def bfloat(values):
    return np.asarray(values, np.float32).astype(jnp.bfloat16)


def wide_table(positions, period):
    return np.concatenate(tables(positions, period), 1).astype(np.float32)


def step_table():
    cosine, sine = tables(np.arange(STEP), MASK)
    return bfloat(np.concatenate([cosine, -sine], 1) / MASK)


def step_phases():
    return wide_table(np.arange(STEPS) * STEP, MASK)


def coarse_map():
    cosine, sine = tables(np.arange(COARSE), COARSE)
    upper = np.concatenate([cosine.T, sine.T], 1)
    lower = np.concatenate([-sine.T, cosine.T], 1)
    return bfloat(np.concatenate([upper, lower], 0))


def interpolation():
    ratio = GRID // COARSE
    frequency = np.arange(1, COARSE // 2)
    offset = np.arange(GRID)
    profile = 1.0 + 2.0 * np.cos(2.0 * math.pi * (np.outer(offset, frequency) % GRID) / GRID).sum(1)
    profile = (profile + np.cos(math.pi * offset / ratio)) / COARSE
    matrix = profile[(offset[None, :] - ratio * np.arange(COARSE)[:, None]) % GRID]
    high = bfloat(matrix)
    low = bfloat(matrix - high.astype(np.float64))
    return high, low


def shifted_table(base, shift):
    cosine = base[:, :BAND] * shift[:, :BAND] - base[:, BAND:] * shift[:, BAND:]
    sine = base[:, BAND:] * shift[:, :BAND] + base[:, :BAND] * shift[:, BAND:]
    return jnp.concatenate([cosine, sine], 1)


def whole_spec(shape):
    return pl.BlockSpec(shape, lambda i: (0,) * len(shape))


def params():
    return pltpu.CompilerParams(vmem_limit_bytes=VMEM_LIMIT)


def store_tiles(out_ref, value, row, column):
    for i in range(value.shape[0] // 8):
        for j in range(value.shape[1] // 128):
            out_ref[(row // 8 + i) * 4 + column // 128 + j] = value[8 * i : 8 * i + 8, 128 * j : 128 * j + 128]


def load_tiles(tiles_ref, held_ref):
    for i in range(32):
        for j in range(4):
            held_ref[8 * i : 8 * i + 8, 128 * j : 128 * j + 128] = tiles_ref[4 * i + j]


def spectrum_kernel(mask_ref, step_ref, phase_ref, rows_ref, out_ref, acc_ref):
    index = pl.program_id(0)
    per = mask_ref.shape[1] // STEP

    @pl.when(index == 0)
    def _():
        acc_ref[...] = jnp.zeros_like(acc_ref)

    for part in range(per):
        transmit = jnp.tanh(mask_ref[:, part * STEP : (part + 1) * STEP]).astype(jnp.bfloat16)
        product = jnp.dot(transmit, step_ref[...], preferred_element_type=jnp.float32)
        first = product[:, :BAND]
        second = product[:, BAND:]
        phase = phase_ref[pl.ds(index * per + part, 1), :]
        cosine = phase[:, :BAND]
        sine = phase[:, BAND:]
        acc_ref[:, :BAND] += first * cosine + second * sine
        acc_ref[:, BAND:] += second * cosine - first * sine

    @pl.when(index == pl.num_programs(0) - 1)
    def _():
        product = lax.dot_general(
            rows_ref[...],
            acc_ref[...],
            (((0,), (0,)), ((), ())),
            precision=HIGHEST,
            preferred_element_type=jnp.float32,
        )
        store_tiles(out_ref, product[:BAND, :BAND] + product[BAND:, BAND:], 0, 0)
        store_tiles(out_ref, product[:BAND, BAND:] - product[BAND:, :BAND], 0, BAND)


def mask_spectrum(mask_params, step_value, phases, mask_rows):
    rows = mask_params.shape[0]
    width = 2048
    return pl.pallas_call(
        spectrum_kernel,
        grid=(MASK // width,),
        in_specs=[
            pl.BlockSpec((rows, width), lambda i: (0, i)),
            whole_spec(step_value.shape),
            whole_spec(phases.shape),
            whole_spec(mask_rows.shape),
        ],
        out_specs=whole_spec((DEVICES, 8, 128)),
        out_shape=jax.ShapeDtypeStruct((DEVICES, 8, 128), jnp.float32),
        scratch_shapes=[pltpu.VMEM((rows, 2 * BAND), jnp.float32)],
        compiler_params=params(),
        name="mask_spectrum",
    )(mask_params, step_value, phases, mask_rows)


def field_kernel(tiles_ref, pupil_ref, rows_ref, map_ref, field_ref, power_ref, spec_ref, sum_ref):
    index = pl.program_id(0)

    @pl.when(index == 0)
    def _():
        load_tiles(tiles_ref, spec_ref)

    spec_re = spec_ref[:, :BAND]
    spec_im = spec_ref[:, BAND:]
    kernel_re = pupil_ref[0, 0]
    kernel_im = pupil_ref[0, 1]
    amp_re = kernel_re * spec_re - kernel_im * spec_im
    amp_im = kernel_re * spec_im + kernel_im * spec_re
    block = jnp.concatenate(
        [jnp.concatenate([amp_re, amp_im], 1), jnp.concatenate([-amp_im, amp_re], 1)], 0
    ).astype(jnp.bfloat16)
    partial = jnp.dot(rows_ref[...], block, preferred_element_type=jnp.float32).astype(jnp.bfloat16)
    field = jnp.dot(partial, map_ref[...], preferred_element_type=jnp.float32)
    field_ref[0] = field
    power = field[:, :COARSE] * field[:, :COARSE] + field[:, COARSE:] * field[:, COARSE:]
    corner = index % 2

    @pl.when(index < 2)
    def _():
        sum_ref[corner] = power

    @pl.when(index >= 2)
    def _():
        total = (sum_ref[corner] + power).astype(jnp.bfloat16)
        slab = total.shape[0] // KERN
        for owner in range(KERN):
            power_ref[owner, corner] = total[owner * slab : (owner + 1) * slab]


def coarse_fields(tiles, pupils, rows_table, column_map):
    pairs = pupils.shape[0]
    rows = rows_table.shape[0]
    return pl.pallas_call(
        field_kernel,
        grid=(pairs,),
        in_specs=[
            whole_spec(tiles.shape),
            pl.BlockSpec((1, 2, BAND, BAND), lambda i: (i, 0, 0, 0)),
            whole_spec(rows_table.shape),
            whole_spec(column_map.shape),
        ],
        out_specs=[
            pl.BlockSpec((1, rows, 2 * COARSE), lambda i: (i, 0, 0)),
            whole_spec((KERN, 2, rows // KERN, COARSE)),
        ],
        out_shape=[
            jax.ShapeDtypeStruct((pairs, rows, 2 * COARSE), jnp.float32),
            jax.ShapeDtypeStruct((KERN, 2, rows // KERN, COARSE), jnp.bfloat16),
        ],
        scratch_shapes=[
            pltpu.VMEM((BAND, 2 * BAND), jnp.float32),
            pltpu.VMEM((2, rows, COARSE), jnp.float32),
        ],
        compiler_params=params(),
        name="coarse_fields",
    )(tiles, pupils, rows_table, column_map)


def adjoint_kernel(parts_ref, target_ref, high_ref, low_ref, out_ref, power_ref, acc_ref):
    index = pl.program_id(0)
    rows = parts_ref.shape[2]

    @pl.when(index == 0)
    def _():
        total = parts_ref[0].astype(jnp.float32)
        for owner in range(1, KERN):
            total = total + parts_ref[owner].astype(jnp.float32)
        total = total.reshape(2 * rows, COARSE)
        high = total.astype(jnp.bfloat16)
        power_ref[: 2 * rows] = high
        power_ref[2 * rows :] = (total - high.astype(jnp.float32)).astype(jnp.bfloat16)
        acc_ref[...] = jnp.zeros_like(acc_ref)

    both = jnp.dot(power_ref[...], high_ref[...], preferred_element_type=jnp.float32)
    rest = jnp.dot(power_ref[: 2 * rows], low_ref[...], preferred_element_type=jnp.float32)
    fine = both[: 2 * rows] + (both[2 * rows :] + rest)
    wanted = target_ref[...].astype(jnp.float32)
    corners = []
    for corner in range(2):
        dose = dose_levels[corner]
        resist = jax.nn.sigmoid(steepness * (dose * fine[corner * rows : (corner + 1) * rows] - threshold))
        corners.append(
            (2.0 * (resist - wanted) * resist * (1.0 - resist) * steepness * dose).astype(jnp.bfloat16)
        )
    adjoint = jnp.concatenate(corners, 0)
    contract = (((1,), (1,)), ((), ()))
    acc_ref[...] += lax.dot_general(
        adjoint, high_ref[...], contract, preferred_element_type=jnp.float32
    ) + lax.dot_general(adjoint, low_ref[...], contract, preferred_element_type=jnp.float32)

    @pl.when(index == pl.num_programs(0) - 1)
    def _():
        out_ref[...] = acc_ref[...].reshape(2, rows, COARSE).astype(jnp.bfloat16)


def coarse_adjoint(parts, target, high, low):
    rows = target.shape[0]
    width = 512
    return pl.pallas_call(
        adjoint_kernel,
        grid=(GRID // width,),
        in_specs=[
            whole_spec(parts.shape),
            pl.BlockSpec((rows, width), lambda i: (0, i)),
            pl.BlockSpec((COARSE, width), lambda i: (0, i)),
            pl.BlockSpec((COARSE, width), lambda i: (0, i)),
        ],
        out_specs=whole_spec((2, rows, COARSE)),
        out_shape=jax.ShapeDtypeStruct((2, rows, COARSE), jnp.bfloat16),
        scratch_shapes=[
            pltpu.VMEM((4 * rows, COARSE), jnp.bfloat16),
            pltpu.VMEM((2 * rows, COARSE), jnp.float32),
        ],
        compiler_params=params(),
        name="coarse_adjoint",
    )(parts, target, high, low)


def gradient_kernel(field_ref, adjoint_ref, pupil_ref, rows_ref, map_ref, out_ref, acc_ref):
    index = pl.program_id(0)
    corner = index % 2

    @pl.when(index == 0)
    def _():
        acc_ref[...] = jnp.zeros_like(acc_ref)

    adjoint = jnp.concatenate([adjoint_ref[owner, corner] for owner in range(KERN)], 0)
    adjoint = 2.0 * adjoint.astype(jnp.float32)
    field = field_ref[0]
    weighted = jnp.concatenate(
        [field[:, :COARSE] * adjoint, field[:, COARSE:] * adjoint], 1
    ).astype(jnp.bfloat16)
    back = lax.dot_general(
        weighted, map_ref[...], (((1,), (1,)), ((), ())), preferred_element_type=jnp.float32
    ).astype(jnp.bfloat16)
    grads = lax.dot_general(
        rows_ref[...], back, (((0,), (0,)), ((), ())), preferred_element_type=jnp.float32
    )
    grad_re = grads[:BAND, :BAND] + grads[BAND:, BAND:]
    grad_im = grads[:BAND, BAND:] - grads[BAND:, :BAND]
    kernel_re = pupil_ref[0, 0]
    kernel_im = pupil_ref[0, 1]
    acc_ref[:, :BAND] += kernel_re * grad_re + kernel_im * grad_im
    acc_ref[:, BAND:] += kernel_re * grad_im - kernel_im * grad_re

    @pl.when(index == pl.num_programs(0) - 1)
    def _():
        store_tiles(out_ref, acc_ref[...], 0, 0)


def spectrum_gradient(fields, adjoint, pupils, rows_table, column_map):
    pairs, rows, _ = fields.shape
    return pl.pallas_call(
        gradient_kernel,
        grid=(pairs,),
        in_specs=[
            pl.BlockSpec((1, rows, 2 * COARSE), lambda i: (i, 0, 0)),
            whole_spec(adjoint.shape),
            pl.BlockSpec((1, 2, BAND, BAND), lambda i: (i, 0, 0, 0)),
            whole_spec(rows_table.shape),
            whole_spec(column_map.shape),
        ],
        out_specs=whole_spec((DEVICES, 8, 128)),
        out_shape=jax.ShapeDtypeStruct((DEVICES, 8, 128), jnp.float32),
        scratch_shapes=[pltpu.VMEM((BAND, 2 * BAND), jnp.float32)],
        compiler_params=params(),
        name="spectrum_gradient",
    )(fields, adjoint, pupils, rows_table, column_map)


def update_kernel(tiles_ref, rows_ref, mask_ref, step_ref, phase_ref, out_ref, held_ref, column_ref):
    index = pl.program_id(0)
    per = mask_ref.shape[1] // STEP

    @pl.when(index == 0)
    def _():
        load_tiles(tiles_ref, held_ref)
        rows = rows_ref[...]
        product_cos = jnp.dot(
            rows[:, :BAND], held_ref[...], precision=HIGHEST, preferred_element_type=jnp.float32
        )
        product_sin = jnp.dot(
            rows[:, BAND:], held_ref[...], precision=HIGHEST, preferred_element_type=jnp.float32
        )
        column_ref[:, :BAND] = product_cos[:, :BAND] - product_sin[:, BAND:]
        column_ref[:, BAND:] = product_sin[:, :BAND] + product_cos[:, BAND:]

    for part in range(per):
        phase = phase_ref[pl.ds(index * per + part, 1), :]
        cosine = phase[:, :BAND]
        sine = phase[:, BAND:]
        col_re = column_ref[:, :BAND]
        col_im = column_ref[:, BAND:]
        turned = jnp.concatenate(
            [
                (col_re * cosine - col_im * sine).astype(jnp.bfloat16),
                (col_re * sine + col_im * cosine).astype(jnp.bfloat16),
            ],
            1,
        )
        pixel_grad = lax.dot_general(
            turned, step_ref[...], (((1,), (1,)), ((), ())), preferred_element_type=jnp.float32
        )
        mask = mask_ref[:, part * STEP : (part + 1) * STEP]
        transmit = jnp.tanh(mask)
        out_ref[:, part * STEP : (part + 1) * STEP] = mask - step_size * pixel_grad * (
            1.0 - transmit * transmit
        )


def mask_update(tiles, mask_rows, mask_params, step_value, phases):
    rows = mask_params.shape[0]
    width = 2048
    return pl.pallas_call(
        update_kernel,
        grid=(MASK // width,),
        in_specs=[
            whole_spec(tiles.shape),
            whole_spec(mask_rows.shape),
            pl.BlockSpec((rows, width), lambda i: (0, i)),
            whole_spec(step_value.shape),
            whole_spec(phases.shape),
        ],
        out_specs=pl.BlockSpec((rows, width), lambda i: (0, i)),
        out_shape=jax.ShapeDtypeStruct((rows, MASK), jnp.float32),
        scratch_shapes=[
            pltpu.VMEM((BAND, 2 * BAND), jnp.float32),
            pltpu.VMEM((rows, 2 * BAND), jnp.float32),
        ],
        compiler_params=params(),
        name="mask_update",
    )(tiles, mask_rows, mask_params, step_value, phases)


def exchange(values, axes):
    return lax.all_to_all(values, axes, 0, 0, tiled=True)


def sum_tiles(tiles):
    everyone = ("rows", "kern")
    own = jnp.sum(exchange(tiles, everyone), 0, keepdims=True)
    return exchange(jnp.broadcast_to(own, tiles.shape), everyone)


def local(mask_params, pupil_kernels, target_pattern):
    rows = mask_params.shape[0]
    device = lax.axis_index(("rows", "kern"))
    grid_rows, slab_cols = target_pattern.shape
    slab_rows = grid_rows // KERN
    target = exchange(target_pattern.astype(jnp.bfloat16).reshape(KERN, slab_rows, slab_cols), "kern")
    target = jnp.transpose(target, (1, 0, 2)).reshape(slab_rows, GRID)

    step_value = jnp.asarray(step_table())
    phases = jnp.asarray(step_phases())
    mask_rows = shifted_table(
        jnp.asarray(wide_table(np.arange(rows), MASK)),
        lax.dynamic_slice_in_dim(jnp.asarray(wide_table(np.arange(DEVICES) * rows, MASK)), device, 1, 0),
    )
    rows_table = shifted_table(
        jnp.asarray(wide_table(np.arange(grid_rows), GRID)),
        lax.dynamic_slice_in_dim(
            jnp.asarray(wide_table(np.arange(ROWS) * grid_rows, GRID)), lax.axis_index("rows"), 1, 0
        ),
    ).astype(jnp.bfloat16)
    column_map = jnp.asarray(coarse_map())
    high, low = interpolation()

    spectrum = sum_tiles(mask_spectrum(mask_params, step_value, phases, mask_rows))
    pupils = pupil_kernels.reshape(-1, 2, BAND, BAND)
    fields, powers = coarse_fields(spectrum, pupils, rows_table, column_map)
    parts = exchange(powers, "kern")
    slab_adjoint = coarse_adjoint(parts, target, jnp.asarray(high), jnp.asarray(low))
    adjoint = exchange(jnp.broadcast_to(slab_adjoint[None], (KERN,) + slab_adjoint.shape), "kern")
    gradient = sum_tiles(spectrum_gradient(fields, adjoint, pupils, rows_table, column_map))
    return mask_update(gradient, mask_rows, mask_params, step_value, phases)


def solution(mesh):
    placed = (P(("rows", "kern"), None), P("kern", None, None, None, None), P("rows", "kern"))
    return jax.shard_map(
        local, mesh=mesh, in_specs=placed, out_specs=P(("rows", "kern"), None), check_vma=False
    )
```

time: 864 us -> 163 us (0.19)
  waiting for transfers between devices: 535 us -> 20.4 us
  matrix products: 143 us -> 0 us
  other arithmetic: 133 us -> 3.52 us
  blocking collectives: 0 us -> 75.1 us
  Pallas kernels: 0 us -> 45.2 us
  local copies, waits for them, and re-layouts: 32.4 us -> 4.11 us
  between operations: 13.8 us -> 0.08 us
  starting transfers between devices: 0.34 us -> 13.1 us
    psum x3 -> x0, waiting for transfers between devices: 455 us -> none  [the longest x1 181 us: local(): lax.psum(partial_power.astype(jnp.bfloat16), 'kern').astype(jnp.float32)]
    dot_general x18 -> x0, matrix products: 143 us -> none  [the longest x4 50.6 us: field_of(): jnp.dot(partial_value, column_map, preferred_element_type=jnp.float32)]
    all_gather x1 -> x0, waiting for transfers between devices: 80.2 us -> none  [local(): adjoint = lax.all_gather(slab_adjoint, 'kern', axis=2, tiled=True)]
    all_to_all x0 -> x4, blocking collectives: none -> 75.1 us  [exchange(): return lax.all_to_all(values, axes, 0, 0, tiled=True)]
    cos x1 -> x0, other arithmetic: 68.2 us -> none  [band_table(): return (jnp.cos(angles), jnp.sin(angles))]
    pallas_call x0 -> x5, Pallas kernels: none -> 45.2 us  [the longest x1 12.6 us: mask_update(): pl.pallas_call(update_kernel, grid=(MASK // width,), in_specs=[whole_spec...]
    another operation x8 -> x1, other arithmetic: 40.8 us -> 0.07 us
    unnamed x24 -> x10, local copies, waits for them, and re-layouts: 21.9 us -> 0.81 us
  transfers between devices with their start and end apart: 4 -> 3, of which waited for: 4 -> 2; matrix products, arithmetic and copies ran while one was open for 4% -> 1% of each run, Pallas kernels for 0% -> 4%
where the time goes in v1:
time: 163 us; the launch traced here: 162 us
  blocking collectives  75.1 us (46%)
  Pallas kernels  45.2 us (28%)
  waiting for transfers between devices  20.4 us (13%)
  starting transfers between devices  13.1 us (8%)
  local copies, waits for them, and re-layouts  4.11 us (3%)
  other arithmetic  3.52 us (2%)
    all_to_all x4, blocking collectives, exchange(): return lax.all_to_all(values, axes, 0, 0, tiled=True)  75.1 us
    all_to_all x3, waiting for transfers between devices, exchange(): return lax.all_to_all(values, axes, 0, 0, tiled=True)  20.4 us
    all_to_all x3, starting transfers between devices, exchange(): return lax.all_to_all(values, axes, 0, 0, tiled=True)  13.1 us
    pallas_call x1, Pallas kernels, mask_update(): pl.pallas_call(update_kernel, grid=(MASK // width,), in_specs=[whole_spec...  12.6 us
    pallas_call x1, Pallas kernels, mask_spectrum(): pl.pallas_call(spectrum_kernel, grid=(MASK // width,), in_specs=[pl.Block...  9.82 us
    pallas_call x1, Pallas kernels, coarse_adjoint(): pl.pallas_call(adjoint_kernel, grid=(GRID // width,), in_specs=[whole_spe...  9.68 us
    pallas_call x1, Pallas kernels, spectrum_gradient(): pl.pallas_call(gradient_kernel, grid=(pairs,), in_specs=[pl.BlockSpec((1,...  6.63 us
    pallas_call x1, Pallas kernels, coarse_fields(): pl.pallas_call(field_kernel, grid=(pairs,), in_specs=[whole_spec(tiles.sh...  6.49 us
  transfers between devices with their start and end apart: 3, of which 2 were waited for; matrix products, arithmetic and copies ran while one was open for 1% of the time, Pallas kernels for 4%

profile of v1, /device:TPU:1, one launch (start us, length us, event | category | flops | bytes accessed | tf_op | source)
XLA Modules:
  0.0 161.6 jit_solution(13295719572270804886)
XLA Ops:
  0.0 0.8 constant_dynamic-slice_fusion
  0.8 1.0 multiply_subtract_fusion
  1.8 0.7 pad_maximum_fusion.rows_ref
  2.6 0.0 copy-start.2
  2.6 9.8 %mask_spectrum.1 = f32[128,8,128]{2,1,0:T(8,128)} custom-call(f32[128,16384]{1,0:T(8,128)} %mask_ref.3, bf16[256,512]{1,0:T(8,128)(2,1)} %constant.37.clone.step_ref, f32[64,512]{1,0:T(8,128)} %constant.38.clone.phase_ref, f32[128,512]{1,0:T(8,128)} %pad_maximum_fusion.rows_ref), custom_call_target="tpu_custom_call" | custom-call | tf_op jit(solution)/shard_map/mask_spectrum/pallas_call | solution.py:133
  12.4 24.9 %all_to_all.35 = f32[128,8,128]{2,1,0:T(8,128)S(1)} all-to-all(f32[128,8,128]{2,1,0:T(8,128)} %mask_spectrum.1), channel_id=1, replica_groups=mesh['rows'=16,'kern'=8] {'rows','kern'}, dimensions={0} | all-to-all | bytes 1048576 | tf_op jit(solution)/shard_map/all_to_all | solution.py:390
  37.3 0.1 reduce_sum.18
  37.4 0.8 broadcast_in_dim.6
  38.3 4.6 %all-to-all-start.1 = ((f32[128,8,128]{2,1,0:T(8,128)}), f32[128,8,128]{2,1,0:T(8,128)S(1)}, u32[]{:S(2)}, u32[]{:S(2)}) async-start(f32[128,8,128]{2,1,0:T(8,128)} %broadcast_in_dim.6), calls=%async_computation.1 | async-start | bytes 1048576 | tf_op jit(solution)/shard_map/all_to_all | solution.py:390
  42.9 0.0 copy-done.2
  42.9 0.7 convert_element_type.4
  43.6 12.8 %all-to-all-done.1.tiles_ref = f32[128,8,128]{2,1,0:T(8,128)S(1)} async-done(((f32[128,8,128]{2,1,0:T(8,128)}), f32[128,8,128]{2,1,0:T(8,128)S(1)}, u32[]{:S(2)}, u32[]{:S(2)}) %all-to-all-start.1) | async-done | bytes 524320 | tf_op jit(solution)/shard_map/all_to_all | solution.py:390
  56.5 3.4 %all-to-all-start.3 = ((bf16[8,32,512]{2,1,0:T(8,128)(2,1)}), bf16[8,32,512]{2,1,0:T(8,128)(2,1)S(1)}, u32[]{:S(2)}, u32[]{:S(2)}) async-start(bf16[8,32,512]{2,1,0:T(8,128)(2,1)} %bitcast.5), calls=%async_computation.3 | async-start | bytes 524288 | tf_op jit(solution)/shard_map/all_to_all | solution.py:390
  59.9 0.0 copy-done.3
  59.9 0.0 copy-done.4
  59.9 0.1 subtract_convert_fusion
  60.0 0.7 pad_maximum_fusion.1.rows_ref
  60.7 0.0 copy-done
  60.7 6.5 %coarse_fields.1 = (f32[4,256,1024]{2,1,0:T(8,128)}, bf16[8,2,32,512]{3,2,1,0:T(8,128)(2,1)}) custom-call(f32[128,8,128]{2,1,0:T(8,128)} %copy-done, f32[4,2,256,256]{3,2,1,0:T(8,128)} %bitcast.9, bf16[256,512]{1,0:T(8,128)(2,1)} %pad_maximum_fusion.1.rows_ref, bf16[512,1024]{1,0:T(8,128)(2,1)} %constant.43.clone.map_ref), custom_call_target="tpu_custom_call" | custom-call | tf_op jit(solution)/shard_map/coarse_fields/pallas_call | solution.py:187
  67.2 0.0 all-to-all-done.3
  67.2 5.1 %all-to-all-start.2 = ((bf16[8,2,32,512]{3,2,1,0:T(8,128)(2,1)}), bf16[8,2,32,512]{3,2,1,0:T(8,128)(2,1)S(1)}, u32[]{:S(2)}, u32[]{:S(2)}) async-start(bf16[8,2,32,512]{3,2,1,0:T(8,128)(2,1)} %get-tuple-element.8), calls=%async_computation.2 | async-start | bytes 1048576 | tf_op jit(solution)/shard_map/all_to_all | solution.py:390
  72.2 0.7 copy.15
  73.0 7.6 %all-to-all-done.2.parts_ref = bf16[8,2,32,512]{3,2,1,0:T(8,128)(2,1)S(1)} async-done(((bf16[8,2,32,512]{3,2,1,0:T(8,128)(2,1)}), bf16[8,2,32,512]{3,2,1,0:T(8,128)(2,1)S(1)}, u32[]{:S(2)}, u32[]{:S(2)}) %all-to-all-start.2) | async-done | bytes 524320 | tf_op jit(solution)/shard_map/all_to_all | solution.py:390
  80.6 0.8 copy-done.1
  81.4 9.7 %coarse_adjoint.1 = bf16[2,32,512]{2,1,0:T(8,128)(2,1)} custom-call(bf16[8,2,32,512]{3,2,1,0:T(8,128)(2,1)} %copy-done.1, bf16[32,4096]{1,0:T(8,128)(2,1)} %bitcast.11, bf16[512,4096]{1,0:T(8,128)(2,1)} %constant.44.clone.high_ref, bf16[512,4096]{1,0:T(8,128)(2,1)} %constant.45.clone.low_ref), custom_call_target="tpu_custom_call" | custom-call | tf_op jit(solution)/shard_map/coarse_adjoint/pallas_call | solution.py:253
  91.1 0.9 broadcast_in_dim.7
  92.0 10.7 %all_to_all.36.adjoint_ref = bf16[8,2,32,512]{3,2,1,0:T(8,128)(2,1)} all-to-all(bf16[8,2,32,512]{3,2,1,0:T(8,128)(2,1)S(1)} %broadcast_in_dim.7), channel_id=1, replica_groups=mesh['rows'=16,'kern'=8] {'kern'}, dimensions={0} | all-to-all | bytes 1048576 | tf_op jit(solution)/shard_map/all_to_all | solution.py:390
  102.6 6.6 %spectrum_gradient.1 = f32[128,8,128]{2,1,0:T(8,128)} custom-call(f32[4,256,1024]{2,1,0:T(8,128)} %get-tuple-element.7.field_ref, bf16[8,2,32,512]{3,2,1,0:T(8,128)(2,1)} %all_to_all.36.adjoint_ref, f32[4,2,256,256]{3,2,1,0:T(8,128)} %bitcast.10, bf16[256,512]{1,0:T(8,128)(2,1)} %pad_maximum_fusion.1.rows_ref, bf16[512,1024]{1,0:T(8,128)(2,1)} %constant.43.clone.map_ref), custom_call_target="tpu_custom_call" | custom-call | tf_op jit(solution)/shard_map/spectrum_gradient/pallas_call | solution.py:307
  109.3 21.3 %all_to_all.37 = f32[128,8,128]{2,1,0:T(8,128)S(1)} all-to-all(f32[128,8,128]{2,1,0:T(8,128)} %spectrum_gradient.1), channel_id=1, replica_groups=mesh['rows'=16,'kern'=8] {'rows','kern'}, dimensions={0} | all-to-all | bytes 1048576 | tf_op jit(solution)/shard_map/all_to_all | solution.py:390
  130.6 0.1 reduce_sum.19
  130.8 18.2 %all_to_all.38.tiles_ref = f32[128,8,128]{2,1,0:T(8,128)} all-to-all(f32[128,8,128]{2,1,0:T(8,128)S(1)} %broadcast_in_dim.8), channel_id=1, replica_groups=mesh['rows'=16,'kern'=8] {'rows','kern'}, dimensions={0} | all-to-all | bytes 1048576 | tf_op jit(solution)/shard_map/all_to_all | solution.py:390
  149.0 12.6 %mask_update.1 = f32[128,16384]{1,0:T(8,128)} custom-call(f32[128,8,128]{2,1,0:T(8,128)} %all_to_all.38.tiles_ref, f32[128,512]{1,0:T(8,128)} %pad_maximum_fusion.rows_ref, f32[128,16384]{1,0:T(8,128)} %mask_ref.3, bf16[256,512]{1,0:T(8,128)(2,1)} %constant.37.clone.step_ref, f32[64,512]{1,0:T(8,128)} %constant.38.clone.phase_ref), custom_call_target="tpu_custom_call" | custom-call | tf_op jit(solution)/shard_map/mask_update/pallas_call | solution.py:368
  (5 shorter events, 0.0 us)
Async XLA Ops:
  2.6 40.3 %copy-start.2 = (s32[256,512]{1,0:T(8,128)S(1)}, s32[256,512]{1,0:T(8,128)}, u32[]{:S(2)}) copy-start(s32[256,512]{1,0:T(8,128)} %param.14) | copy-start | bytes 1572868
  12.4 47.5 %copy-start.3 = (f32[256,256]{1,0:T(8,128)S(1)}, f32[256,256]{1,0:T(8,128)}, u32[]{:S(2)}) copy-start(f32[256,256]{1,0:T(8,128)} %constant.50) | copy-start | bytes 786436
  12.4 47.5 %copy-start.4 = (f32[256,256]{1,0:T(8,128)S(1)}, f32[256,256]{1,0:T(8,128)}, u32[]{:S(2)}) copy-start(f32[256,256]{1,0:T(8,128)} %constant.49) | copy-start | bytes 786436
  38.3 18.2 %all-to-all-start.1 = ((f32[128,8,128]{2,1,0:T(8,128)}), f32[128,8,128]{2,1,0:T(8,128)S(1)}, u32[]{:S(2)}, u32[]{:S(2)}) async-start(f32[128,8,128]{2,1,0:T(8,128)} %broadcast_in_dim.6), calls=%async_computation.1 | async-start | bytes 1048576 | tf_op jit(solution)/shard_map/all_to_all | solution.py:390
  56.5 4.2 %copy-start = (f32[128,8,128]{2,1,0:T(8,128)}, f32[128,8,128]{2,1,0:T(8,128)S(1)}, u32[]{:S(2)}) copy-start(f32[128,8,128]{2,1,0:T(8,128)S(1)} %all-to-all-done.1.tiles_ref) | copy-start | bytes 1572868
  56.5 10.7 %all-to-all-start.3 = ((bf16[8,32,512]{2,1,0:T(8,128)(2,1)}), bf16[8,32,512]{2,1,0:T(8,128)(2,1)S(1)}, u32[]{:S(2)}, u32[]{:S(2)}) async-start(bf16[8,32,512]{2,1,0:T(8,128)(2,1)} %bitcast.5), calls=%async_computation.3 | async-start | bytes 524288 | tf_op jit(solution)/shard_map/all_to_all | solution.py:390
  67.2 13.4 %all-to-all-start.2 = ((bf16[8,2,32,512]{3,2,1,0:T(8,128)(2,1)}), bf16[8,2,32,512]{3,2,1,0:T(8,128)(2,1)S(1)}, u32[]{:S(2)}, u32[]{:S(2)}) async-start(bf16[8,2,32,512]{3,2,1,0:T(8,128)(2,1)} %get-tuple-element.8), calls=%async_computation.2 | async-start | bytes 1048576 | tf_op jit(solution)/shard_map/all_to_all | solution.py:390
  80.6 0.8 copy-start.1

commit v2 on v1

v2 whole, which is shorter than its diff:
```python
import math

import jax
import jax.numpy as jnp
import numpy as np
from jax import lax
from jax.experimental import pallas as pl
from jax.experimental.pallas import tpu as pltpu
from jax.sharding import PartitionSpec as P

MASK = 16384
GRID = 4096
BAND = 256
COARSE = 512
STEP = 256
STEPS = MASK // STEP
ROWS = 16
KERN = 8
DEVICES = ROWS * KERN

steepness = 4.0
threshold = 0.75
step_size = 1.0
dose_levels = (1.0, 1.15)

VMEM_LIMIT = 24 * 1024 * 1024
STREAM_LIMIT = 60 * 1024 * 1024
HIGHEST = lax.Precision.HIGHEST


def tables(positions, period):
    frequency = np.arange(BAND) - BAND // 2
    angles = (np.outer(positions, frequency) % period) * (2.0 * math.pi / period)
    return np.cos(angles), np.sin(angles)


def bfloat(values):
    return np.asarray(values, np.float32).astype(jnp.bfloat16)


def wide_table(positions, period):
    return np.concatenate(tables(positions, period), 1).astype(np.float32)


def step_table():
    cosine, sine = tables(np.arange(STEP), MASK)
    return bfloat(np.concatenate([cosine, -sine], 1) / MASK)


def step_phases():
    return wide_table(np.arange(STEPS) * STEP, MASK)


def coarse_map():
    cosine, sine = tables(np.arange(COARSE), COARSE)
    upper = np.concatenate([cosine.T, sine.T], 1)
    lower = np.concatenate([-sine.T, cosine.T], 1)
    return bfloat(np.concatenate([upper, lower], 0))


def interpolation():
    ratio = GRID // COARSE
    frequency = np.arange(1, COARSE // 2)
    offset = np.arange(GRID)
    profile = 1.0 + 2.0 * np.cos(2.0 * math.pi * (np.outer(offset, frequency) % GRID) / GRID).sum(1)
    profile = (profile + np.cos(math.pi * offset / ratio)) / COARSE
    matrix = profile[(offset[None, :] - ratio * np.arange(COARSE)[:, None]) % GRID]
    return bfloat(matrix)


def shifted_table(base_ref, shift):
    cosine = base_ref[:, :BAND] * shift[:, :BAND] - base_ref[:, BAND:] * shift[:, BAND:]
    sine = base_ref[:, BAND:] * shift[:, :BAND] + base_ref[:, :BAND] * shift[:, BAND:]
    return cosine, sine


def mask_table(base_ref, shift_ref):
    device = lax.axis_index("rows") * KERN + lax.axis_index("kern")
    return shifted_table(base_ref, shift_ref[pl.ds(device, 1), :])


def grid_table(base_ref, shift_ref):
    cosine, sine = shifted_table(base_ref, shift_ref[pl.ds(lax.axis_index("rows"), 1), :])
    return jnp.concatenate([cosine, sine], 1).astype(jnp.bfloat16)


def whole_spec(shape):
    return pl.BlockSpec(shape, lambda i: (0,) * len(shape))


def params(limit=VMEM_LIMIT):
    return pltpu.CompilerParams(vmem_limit_bytes=limit)


def kern_place(shift):
    return lax.rem(lax.axis_index("kern") + (shift + KERN), KERN)


def float_dot(left, right):
    return jnp.dot(left, right, preferred_element_type=jnp.float32)


def split(values):
    high = values.astype(jnp.bfloat16)
    return high, (values - high.astype(jnp.float32)).astype(jnp.bfloat16)


def store_tiles(out_ref, value, row, column):
    for i in range(value.shape[0] // 8):
        for j in range(value.shape[1] // 128):
            out_ref[(row // 8 + i) * 4 + column // 128 + j] = value[
                8 * i : 8 * i + 8, 128 * j : 128 * j + 128
            ].astype(out_ref.dtype)


def load_tiles(tiles_ref, held_ref):
    for i in range(BAND // 8):
        for j in range(4):
            held_ref[8 * i : 8 * i + 8, 128 * j : 128 * j + 128] = tiles_ref[4 * i + j].astype(jnp.float32)


def spectrum_kernel(mask_ref, step_ref, phase_ref, base_ref, shift_ref, target_ref, out_ref, *refs):
    wanted_refs = refs[:KERN]
    stack_ref, product_ref, acc_ref = refs[KERN:]
    index = pl.program_id(0)
    rows = mask_ref.shape[0]
    per = mask_ref.shape[1] // STEP

    @pl.when(index == 0)
    def _():
        acc_ref[...] = jnp.zeros_like(acc_ref)
        slab = target_ref.shape[0] // KERN
        for shift in range(KERN):
            at = pl.multiple_of(kern_place(shift) * slab, slab)
            wanted_refs[shift][...] = target_ref[pl.ds(at, slab), :].astype(jnp.float32).astype(jnp.bfloat16)

    for part in range(per):
        stack_ref[part * rows : (part + 1) * rows] = jnp.tanh(
            mask_ref[:, part * STEP : (part + 1) * STEP]
        ).astype(jnp.bfloat16)
    product_ref[...] = float_dot(stack_ref[...], step_ref[...])
    chunk = 32
    for start in range(0, rows, chunk):
        total_re = acc_ref[start : start + chunk, :BAND]
        total_im = acc_ref[start : start + chunk, BAND:]
        for part in range(per):
            phase = phase_ref[pl.ds(index * per + part, 1), :]
            cosine = phase[:, :BAND]
            sine = phase[:, BAND:]
            at = part * rows + start
            first = product_ref[at : at + chunk, :BAND]
            second = product_ref[at : at + chunk, BAND:]
            total_re = total_re + (first * cosine + second * sine)
            total_im = total_im + (second * cosine - first * sine)
        acc_ref[start : start + chunk, :BAND] = total_re
        acc_ref[start : start + chunk, BAND:] = total_im

    @pl.when(index == pl.num_programs(0) - 1)
    def _():
        table = jnp.concatenate(mask_table(base_ref, shift_ref), 1)
        product = lax.dot_general(
            table,
            acc_ref[...],
            (((0,), (0,)), ((), ())),
            precision=HIGHEST,
            preferred_element_type=jnp.float32,
        )
        store_tiles(out_ref, product[:BAND, :BAND] + product[BAND:, BAND:], 0, 0)
        store_tiles(out_ref, product[:BAND, BAND:] - product[BAND:, :BAND], 0, BAND)


def mask_spectrum(mask_params, step_value, phases, base, shifts, target):
    rows = mask_params.shape[0]
    chunk = (target.shape[0] // KERN, target.shape[1])
    width = 2048
    stacked = rows * (width // STEP)
    return pl.pallas_call(
        spectrum_kernel,
        grid=(MASK // width,),
        in_specs=[
            pl.BlockSpec((rows, width), lambda i: (0, i)),
            whole_spec(step_value.shape),
            whole_spec(phases.shape),
            whole_spec(base.shape),
            whole_spec(shifts.shape),
            whole_spec(target.shape),
        ],
        out_specs=[whole_spec((DEVICES, 8, 128))] + [whole_spec(chunk)] * KERN,
        out_shape=[jax.ShapeDtypeStruct((DEVICES, 8, 128), jnp.bfloat16)]
        + [jax.ShapeDtypeStruct(chunk, jnp.bfloat16)] * KERN,
        scratch_shapes=[
            pltpu.VMEM((stacked, STEP), jnp.bfloat16),
            pltpu.VMEM((stacked, 2 * BAND), jnp.float32),
            pltpu.VMEM((rows, 2 * BAND), jnp.float32),
        ],
        compiler_params=params(STREAM_LIMIT),
        name="mask_spectrum",
    )(mask_params, step_value, phases, base, shifts, target)


def field_kernel(
    tiles_ref, pupil_ref, base_ref, shift_ref, map_ref, field_ref, power_ref,
    spec_ref, rows_ref, partial_ref, sum_ref,
):
    index = pl.program_id(0)
    rows = base_ref.shape[0]
    slab = rows // KERN

    @pl.when(index == 0)
    def _():
        load_tiles(tiles_ref, spec_ref)
        rows_ref[...] = grid_table(base_ref, shift_ref)

    spec_re = spec_ref[:, :BAND]
    spec_im = spec_ref[:, BAND:]
    for corner in range(2):
        kernel_re = pupil_ref[0, corner, 0]
        kernel_im = pupil_ref[0, corner, 1]
        amp_re = (kernel_re * spec_re - kernel_im * spec_im).astype(jnp.bfloat16)
        amp_im = (kernel_re * spec_im + kernel_im * spec_re).astype(jnp.bfloat16)
        block = jnp.concatenate(
            [jnp.concatenate([amp_re, amp_im], 1), jnp.concatenate([-amp_im, amp_re], 1)], 0
        )
        partial_ref[corner * rows : (corner + 1) * rows] = float_dot(rows_ref[...], block).astype(
            jnp.bfloat16
        )
    field_ref[0] = float_dot(partial_ref[...], map_ref[...])

    for corner in range(2):
        for owner in range(KERN):
            at = corner * rows + owner * slab
            real = field_ref[0, at : at + slab, :COARSE]
            imag = field_ref[0, at : at + slab, COARSE:]
            power = real * real + imag * imag

            @pl.when(index == 0)
            def _():
                sum_ref[at : at + slab] = power

            @pl.when(index == 1)
            def _():
                power_ref[owner, corner] = (sum_ref[at : at + slab] + power).astype(jnp.bfloat16)


def coarse_fields(tiles, pupils, base, shifts, column_map):
    members = pupils.shape[0]
    rows = base.shape[0]
    return pl.pallas_call(
        field_kernel,
        grid=(members,),
        in_specs=[
            whole_spec(tiles.shape),
            pl.BlockSpec((1, 2, 2, BAND, BAND), lambda i: (i, 0, 0, 0, 0)),
            whole_spec(base.shape),
            whole_spec(shifts.shape),
            whole_spec(column_map.shape),
        ],
        out_specs=[
            pl.BlockSpec((1, 2 * rows, 2 * COARSE), lambda i: (i, 0, 0)),
            whole_spec((KERN, 2, rows // KERN, COARSE)),
        ],
        out_shape=[
            jax.ShapeDtypeStruct((members, 2 * rows, 2 * COARSE), jnp.float32),
            jax.ShapeDtypeStruct((KERN, 2, rows // KERN, COARSE), jnp.bfloat16),
        ],
        scratch_shapes=[
            pltpu.VMEM((BAND, 2 * BAND), jnp.float32),
            pltpu.VMEM((rows, 2 * BAND), jnp.bfloat16),
            pltpu.VMEM((2 * rows, 2 * BAND), jnp.bfloat16),
            pltpu.VMEM((2 * rows, COARSE), jnp.float32),
        ],
        compiler_params=params(),
        name="coarse_fields",
    )(tiles, pupils, base, shifts, column_map)


def adjoint_kernel(parts_ref, matrix_ref, *refs):
    wanted_refs = refs[:KERN]
    out_ref, power_ref, acc_ref, wanted_ref = refs[KERN:]
    index = pl.program_id(0)
    rows = parts_ref.shape[2]

    @pl.when(index == 0)
    def _():
        for shift in range(KERN):
            wanted_ref[kern_place(-shift)] = wanted_refs[shift][...]
        for corner in range(2):
            total = parts_ref[0, corner].astype(jnp.float32)
            for owner in range(1, KERN):
                total = total + parts_ref[owner, corner].astype(jnp.float32)
            power_ref[corner * rows : (corner + 1) * rows] = total.astype(jnp.bfloat16)
        acc_ref[...] = jnp.zeros_like(acc_ref)

    fine = float_dot(power_ref[...], matrix_ref[...])
    wanted = wanted_ref[index].astype(jnp.float32)
    corners = []
    for corner in range(2):
        dose = dose_levels[corner]
        resist = jax.nn.sigmoid(steepness * (dose * fine[corner * rows : (corner + 1) * rows] - threshold))
        corners.append(
            (2.0 * (resist - wanted) * resist * (1.0 - resist) * steepness * dose).astype(jnp.bfloat16)
        )
    acc_ref[...] += lax.dot_general(
        jnp.concatenate(corners, 0),
        matrix_ref[...],
        (((1,), (1,)), ((), ())),
        preferred_element_type=jnp.float32,
    )

    @pl.when(index == pl.num_programs(0) - 1)
    def _():
        out_ref[...] = acc_ref[...].reshape(2, rows, COARSE).astype(jnp.bfloat16)


def coarse_adjoint(parts, matrix, wanted):
    rows = parts.shape[2]
    width = GRID // KERN
    return pl.pallas_call(
        adjoint_kernel,
        grid=(KERN,),
        in_specs=[
            whole_spec(parts.shape),
            pl.BlockSpec((COARSE, width), lambda i: (0, i)),
        ]
        + [whole_spec(wanted[0].shape)] * KERN,
        out_specs=whole_spec((2, rows, COARSE)),
        out_shape=jax.ShapeDtypeStruct((2, rows, COARSE), jnp.bfloat16),
        scratch_shapes=[
            pltpu.VMEM((2 * rows, COARSE), jnp.bfloat16),
            pltpu.VMEM((2 * rows, COARSE), jnp.float32),
            pltpu.VMEM((KERN,) + wanted[0].shape, jnp.bfloat16),
        ],
        compiler_params=params(),
        name="coarse_adjoint",
    )(parts, matrix, *wanted)


def gradient_kernel(field_ref, pupil_ref, base_ref, shift_ref, map_ref, *refs):
    adjoint_refs = refs[:KERN]
    out_ref, rows_ref, weighted_ref, back_ref, acc_ref, adjoint_ref = refs[KERN:]
    index = pl.program_id(0)
    slab = adjoint_ref.shape[2]
    rows = slab * KERN

    @pl.when(index == 0)
    def _():
        acc_ref[...] = jnp.zeros_like(acc_ref)
        rows_ref[...] = grid_table(base_ref, shift_ref)
        for shift in range(KERN):
            adjoint_ref[kern_place(-shift)] = adjoint_refs[shift][...]

    for corner in range(2):
        for owner in range(KERN):
            at = corner * rows + owner * slab
            adjoint = 2.0 * adjoint_ref[owner, corner].astype(jnp.float32)
            for half in range(2):
                columns = slice(half * COARSE, (half + 1) * COARSE)
                weighted_ref[at : at + slab, columns] = (field_ref[0, at : at + slab, columns] * adjoint).astype(
                    jnp.bfloat16
                )
    back_ref[...] = lax.dot_general(
        weighted_ref[...], map_ref[...], (((1,), (1,)), ((), ())), preferred_element_type=jnp.float32
    ).astype(jnp.bfloat16)
    for corner in range(2):
        grads = lax.dot_general(
            rows_ref[...],
            back_ref[corner * rows : (corner + 1) * rows],
            (((0,), (0,)), ((), ())),
            preferred_element_type=jnp.float32,
        )
        grad_re = grads[:BAND, :BAND] + grads[BAND:, BAND:]
        grad_im = grads[:BAND, BAND:] - grads[BAND:, :BAND]
        kernel_re = pupil_ref[0, corner, 0]
        kernel_im = pupil_ref[0, corner, 1]
        acc_ref[:, :BAND] += kernel_re * grad_re + kernel_im * grad_im
        acc_ref[:, BAND:] += kernel_re * grad_im - kernel_im * grad_re

    @pl.when(index == pl.num_programs(0) - 1)
    def _():
        store_tiles(out_ref, acc_ref[...], 0, 0)


def spectrum_gradient(fields, adjoint, pupils, base, shifts, column_map):
    members = pupils.shape[0]
    slab = adjoint[0].shape
    rows = slab[1] * KERN
    return pl.pallas_call(
        gradient_kernel,
        grid=(members,),
        in_specs=[
            pl.BlockSpec((1, 2 * rows, 2 * COARSE), lambda i: (i, 0, 0)),
            pl.BlockSpec((1, 2, 2, BAND, BAND), lambda i: (i, 0, 0, 0, 0)),
            whole_spec(base.shape),
            whole_spec(shifts.shape),
            whole_spec(column_map.shape),
        ]
        + [whole_spec(slab)] * KERN,
        out_specs=whole_spec((DEVICES, 8, 128)),
        out_shape=jax.ShapeDtypeStruct((DEVICES, 8, 128), jnp.bfloat16),
        scratch_shapes=[
            pltpu.VMEM((rows, 2 * BAND), jnp.bfloat16),
            pltpu.VMEM((2 * rows, 2 * COARSE), jnp.bfloat16),
            pltpu.VMEM((2 * rows, 2 * BAND), jnp.bfloat16),
            pltpu.VMEM((BAND, 2 * BAND), jnp.float32),
            pltpu.VMEM((KERN,) + slab, jnp.bfloat16),
        ],
        compiler_params=params(),
        name="spectrum_gradient",
    )(fields, pupils, base, shifts, column_map, *adjoint)


def update_kernel(
    tiles_ref, base_ref, shift_ref, mask_ref, step_ref, phase_ref, out_ref, held_ref, column_ref, stack_ref, product_ref
):
    index = pl.program_id(0)
    rows = mask_ref.shape[0]
    per = mask_ref.shape[1] // STEP

    @pl.when(index == 0)
    def _():
        cosine, sine = mask_table(base_ref, shift_ref)
        table = jnp.concatenate(split(cosine) + split(sine), 0)
        load_tiles(tiles_ref, held_ref)
        product = float_dot(table, held_ref[...].astype(jnp.bfloat16))
        by_cos = product[:rows] + product[rows : 2 * rows]
        by_sin = product[2 * rows : 3 * rows] + product[3 * rows :]
        column_ref[:, :BAND] = by_cos[:, :BAND] - by_sin[:, BAND:]
        column_ref[:, BAND:] = by_sin[:, :BAND] + by_cos[:, BAND:]

    chunk = 32
    for start in range(0, rows, chunk):
        col_re = column_ref[start : start + chunk, :BAND]
        col_im = column_ref[start : start + chunk, BAND:]
        for part in range(per):
            phase = phase_ref[pl.ds(index * per + part, 1), :]
            cosine = phase[:, :BAND]
            sine = phase[:, BAND:]
            at = part * rows + start
            stack_ref[at : at + chunk, :BAND] = (col_re * cosine - col_im * sine).astype(jnp.bfloat16)
            stack_ref[at : at + chunk, BAND:] = (col_re * sine + col_im * cosine).astype(jnp.bfloat16)
    product_ref[...] = float_dot(stack_ref[...], step_ref[...])
    for part in range(per):
        columns = slice(part * STEP, (part + 1) * STEP)
        mask = mask_ref[:, columns]
        transmit = jnp.tanh(mask)
        out_ref[:, columns] = mask - step_size * product_ref[part * rows : (part + 1) * rows] * (
            1.0 - transmit * transmit
        )


def mask_update(gradient, base, shifts, mask_params, step_value, phases):
    rows = mask_params.shape[0]
    width = 2048
    stacked = rows * (width // STEP)
    return pl.pallas_call(
        update_kernel,
        grid=(MASK // width,),
        in_specs=[
            whole_spec(gradient.shape),
            whole_spec(base.shape),
            whole_spec(shifts.shape),
            pl.BlockSpec((rows, width), lambda i: (0, i)),
            whole_spec(step_value.shape),
            whole_spec(phases.shape),
        ],
        out_specs=pl.BlockSpec((rows, width), lambda i: (0, i)),
        out_shape=jax.ShapeDtypeStruct((rows, MASK), jnp.float32),
        scratch_shapes=[
            pltpu.VMEM((BAND, 2 * BAND), jnp.float32),
            pltpu.VMEM((rows, 2 * BAND), jnp.float32),
            pltpu.VMEM((stacked, 2 * BAND), jnp.bfloat16),
            pltpu.VMEM((stacked, STEP), jnp.float32),
        ],
        compiler_params=params(STREAM_LIMIT),
        name="mask_update",
    )(gradient, base, shifts, mask_params, step_value, phases)


def exchange(values, axes):
    return lax.all_to_all(values, axes, 0, 0, tiled=True)


def summed(parts, copies, dtype):
    total = jnp.sum(parts.astype(jnp.float32), 0).astype(dtype)
    return jnp.broadcast_to(total[None], (copies,) + total.shape)


def sum_tiles(tiles):
    everyone = ("rows", "kern")
    return exchange(summed(exchange(tiles, everyone), DEVICES, jnp.bfloat16), everyone)


def shifted(values, shift):
    return lax.ppermute(values, "kern", [(place, (place + shift) % KERN) for place in range(KERN)])


def local(mask_params, pupil_kernels, target_pattern):
    rows = mask_params.shape[0]
    grid_rows = target_pattern.shape[0]
    step_value = step_table()
    phases = jnp.asarray(step_phases())
    mask_base = jnp.asarray(wide_table(np.arange(rows), MASK))
    mask_shifts = jnp.asarray(wide_table(np.arange(DEVICES) * rows, MASK))
    grid_base = jnp.asarray(wide_table(np.arange(grid_rows), GRID))
    grid_shifts = jnp.asarray(wide_table(np.arange(ROWS) * grid_rows, GRID))
    column_map = jnp.asarray(coarse_map())

    tiles, *wanted = mask_spectrum(
        mask_params, jnp.asarray(step_value), phases, mask_base, mask_shifts, target_pattern
    )
    wanted = wanted[:1] + [shifted(wanted[shift], shift) for shift in range(1, KERN)]
    spectrum = sum_tiles(tiles)
    fields, powers = coarse_fields(spectrum, pupil_kernels, grid_base, grid_shifts, column_map)
    slab = coarse_adjoint(exchange(powers, "kern"), jnp.asarray(interpolation()), wanted)
    adjoint = [slab] + [shifted(slab, shift) for shift in range(1, KERN)]
    gradient = sum_tiles(spectrum_gradient(fields, adjoint, pupil_kernels, grid_base, grid_shifts, column_map))
    return mask_update(gradient, mask_base, mask_shifts, mask_params, jnp.asarray(step_value.T), phases)


def solution(mesh):
    placed = (P(("rows", "kern"), None), P("kern", None, None, None, None), P("rows", "kern"))
    return jax.shard_map(
        local, mesh=mesh, in_specs=placed, out_specs=P(("rows", "kern"), None), check_vma=False
    )
```

time: 163 us -> 144 us (0.88)
  Pallas kernels: 45.2 us -> 31.9 us
  waiting for transfers between devices: 20.4 us -> 7.84 us
  starting transfers between devices: 13.1 us -> 23.5 us
  other arithmetic: 3.52 us -> 0.28 us
  local copies, waits for them, and re-layouts: 4.11 us -> 6.16 us
    all_to_all x3 -> x1, waiting for transfers between devices: 20.4 us -> 0.01 us  [exchange(): return lax.all_to_all(values, axes, 0, 0, tiled=True)]
    ppermute x0 -> x14, starting transfers between devices: none -> 19.4 us  [shifted(): lax.ppermute(values, 'kern', [(place, (place + shift) % KERN) for place i...]
    pallas_call x3, Pallas kernels: 22.8 us -> 10.3 us  [the longest x1 5.07 us: coarse_adjoint(): pl.pallas_call(adjoint_kernel, grid=(KERN,), in_specs=[whole_spec(parts.s...]
    all_to_all x3 -> x1, starting transfers between devices: 13.1 us -> 4.14 us  [exchange(): return lax.all_to_all(values, axes, 0, 0, tiled=True)]
    ppermute x0 -> x14, waiting for transfers between devices: none -> 7.84 us  [shifted(): lax.ppermute(values, 'kern', [(place, (place + shift) % KERN) for place i...]
    unnamed x10 -> x30, local copies, waits for them, and re-layouts: 0.81 us -> 6.08 us
    broadcast_in_dim x3 -> x2, local copies, waits for them, and re-layouts: 1.75 us -> 0.07 us  [summed(): return jnp.broadcast_to(total[None], (copies,) + total.shape)]
    all_to_all x4, blocking collectives: 75.1 us -> 73.5 us  [exchange(): return lax.all_to_all(values, axes, 0, 0, tiled=True)]
  transfers between devices with their start and end apart: 3 -> 15, of which waited for: 2 -> 5; matrix products, arithmetic and copies ran while one was open for 1% -> 0% of each run, Pallas kernels for 4% -> 0%
where the time goes in v2:
time: 144 us; the launch traced here: 143 us
  blocking collectives  73.5 us (51%)
  Pallas kernels  31.9 us (22%)
  starting transfers between devices  23.5 us (16%)
  waiting for transfers between devices  7.84 us (5%)
  local copies, waits for them, and re-layouts  6.16 us (4%)
    all_to_all x4, blocking collectives, exchange(): return lax.all_to_all(values, axes, 0, 0, tiled=True)  73.5 us
    ppermute x14, starting transfers between devices, shifted(): lax.ppermute(values, 'kern', [(place, (place + shift) % KERN) for place i...  19.4 us
    pallas_call x1, Pallas kernels, mask_update(): pl.pallas_call(update_kernel, grid=(MASK // width,), in_specs=[whole_spec...  11.3 us
    pallas_call x1, Pallas kernels, mask_spectrum(): pl.pallas_call(spectrum_kernel, grid=(MASK // width,), in_specs=[pl.Block...  10.2 us
    ppermute x14, waiting for transfers between devices, shifted(): lax.ppermute(values, 'kern', [(place, (place + shift) % KERN) for place i...  7.84 us
    unnamed x30, local copies, waits for them, and re-layouts  6.08 us
    pallas_call x1, Pallas kernels, coarse_adjoint(): pl.pallas_call(adjoint_kernel, grid=(KERN,), in_specs=[whole_spec(parts.s...  5.07 us
    all_to_all x1, starting transfers between devices, exchange(): return lax.all_to_all(values, axes, 0, 0, tiled=True)  4.14 us
  transfers between devices with their start and end apart: 15, of which 5 were waited for; matrix products, arithmetic and copies ran while one was open for 0% of the time, Pallas kernels for 0%

profile of v2, /device:TPU:1, one launch (start us, length us, event | category | flops | bytes accessed | tf_op | source)
XLA Modules:
  0.0 143.3 jit_solution(10724547825019257928)
XLA Ops:
  0.0 10.2 %mask_spectrum.1 = (bf16[128,8,128]{2,1,0:T(8,128)(2,1)}, bf16[32,512]{1,0:T(8,128)(2,1)}, bf16[32,512]{1,0:T(8,128)(2,1)}, bf16[32,512]{1,0:T(8,128)(2,1)}, bf1...) custom-call(f32[128,16384]{1,0:T(8,128)} %mask_ref.3, ...), custom_call_target="tpu_custom_call" | custom-call | tf_op jit(solution)/shard_map/mask_spectrum/pallas_call | solution.py:177
  10.3 22.6 %all_to_all.25 = bf16[128,8,128]{2,1,0:T(8,128)(2,1)S(1)} all-to-all(bf16[128,8,128]{2,1,0:T(8,128)(2,1)} %get-tuple-element.16), channel_id=1, replica_groups=mesh['rows'=16,'kern'=8] {'rows','kern'}, dimensions={0} | all-to-all | bytes 524288 | tf_op jit(solution)/shard_map/all_to_all | solution.py:480
  32.8 0.1 reduce_sum.24
  33.0 15.0 %all_to_all.26.tiles_ref = bf16[128,8,128]{2,1,0:T(8,128)(2,1)S(1)} all-to-all(bf16[128,8,128]{2,1,0:T(8,128)(2,1)S(1)} %broadcast_in_dim.4), channel_id=1, replica_groups=mesh['rows'=16,'kern'=8] {'rows','kern'}, dimensions={0} | all-to-all | bytes 524288 | tf_op jit(solution)/shard_map/all_to_all | solution.py:480
  48.1 1.0 copy-done.5
  49.1 2.6 %coarse_fields.1 = (f32[2,512,1024]{2,1,0:T(8,128)S(1)}, bf16[8,2,32,512]{3,2,1,0:T(8,128)(2,1)S(1)}) custom-call(bf16[128,8,128]{2,1,0:T(8,128)(2,1)S(1)} %all_to_all.26.tiles_ref, f32[2,2,2,256,256]{4,3,2,1,0:T(8,128)S(1)} %copy-done, f32[256,512]{1,0:T(8,128)S(1)} %copy-done.5, f32[16,512]{1,0:T(8,128)S(1)} %copy-done.8, bf16[512,1024]{1,0:T(8,128)(2,1)S(1)} %copy-done.4), custom_call_target="tpu_custom_call" | custom-call | tf_op jit(solution)/shard_map/coarse_fields/pallas_call | solution.py:248
  51.7 2.0 %copy-done.2 = f32[2,512,1024]{2,1,0:T(8,128)} copy-done((f32[2,512,1024]{2,1,0:T(8,128)}, f32[2,512,1024]{2,1,0:T(8,128)S(1)}, u32[]{:S(2)}) %copy-start.2) | copy-done | bytes 4194328
  53.8 0.8 copy-done.7
  54.6 4.1 %all-to-all-start.2 = ((bf16[8,2,32,512]{3,2,1,0:T(8,128)(2,1)}), bf16[8,2,32,512]{3,2,1,0:T(8,128)(2,1)}, u32[]{:S(2)}, u32[]{:S(2)}) async-start(bf16[8,2,32,512]{3,2,1,0:T(8,128)(2,1)} %copy-done.7), calls=%async_computation.2 | async-start | bytes 1048576 | tf_op jit(solution)/shard_map/all_to_all | solution.py:480
  58.7 1.3 collective-permute-start
  60.0 1.2 collective-permute-start.1
  61.2 1.8 %collective-permute-start.2 = (bf16[32,512]{1,0:T(8,128)(2,1)}, bf16[32,512]{1,0:T(8,128)(2,1)S(1)}, u32[]{:S(2)}, u32[]{:S(2)}) collective-permute-start(bf16[32,512]{1,0:T(8,128)(2,1)} %get-tuple-element.22), channel_id=1, source_target_pairs={{0,3},{1,4},{2,5},{3,6},{4,7},{5,0},{6,1},{7,2},{8,11},{9,12},{10,... | collective-permute-start | bytes 98312 | tf_op jit(solution)/shard_map/ppermute | solution.py:494
  63.0 1.8 %collective-permute-start.3 = (bf16[32,512]{1,0:T(8,128)(2,1)}, bf16[32,512]{1,0:T(8,128)(2,1)S(1)}, u32[]{:S(2)}, u32[]{:S(2)}) collective-permute-start(bf16[32,512]{1,0:T(8,128)(2,1)} %get-tuple-element.23), channel_id=1, source_target_pairs={{0,4},{1,5},{2,6},{3,7},{4,0},{5,1},{6,2},{7,3},{8,12},{9,13},{10,... | collective-permute-start | bytes 98312 | tf_op jit(solution)/shard_map/ppermute | solution.py:494
  64.8 2.7 %collective-permute-start.4 = (bf16[32,512]{1,0:T(8,128)(2,1)S(1)}, bf16[32,512]{1,0:T(8,128)(2,1)S(1)}, u32[]{:S(2)}, u32[]{:S(2)}) collective-permute-start(bf16[32,512]{1,0:T(8,128)(2,1)S(1)} %copy-done.12), channel_id=1, source_target_pairs={{0,5},{1,6},{2,7},{3,0},{4,1},{5,2},{6,3},{7,4},{8,13},{9,14},{10,... | collective-permute-start | bytes 98312 | tf_op jit(solution)/shard_map/ppermute | solution.py:494
  67.5 1.0 collective-permute-done.refs_1_
  68.5 0.9 collective-permute-start.5
  69.4 0.7 collective-permute-start.6
  70.2 1.3 collective-permute-done.5.refs_6_
  71.5 0.7 collective-permute-done.6.refs_7_
  72.2 2.2 %copy-done.1 = bf16[512,4096]{1,0:T(8,128)(2,1)S(1)} copy-done((bf16[512,4096]{1,0:T(8,128)(2,1)S(1)}, bf16[512,4096]{1,0:T(8,128)(2,1)}, u32[]{:S(2)}) %copy-start.1) | copy-done | bytes 4194328
  74.4 5.1 %coarse_adjoint.1.refs_0_ = bf16[2,32,512]{2,1,0:T(8,128)(2,1)S(1)} custom-call(bf16[8,2,32,512]{3,2,1,0:T(8,128)(2,1)} %all-to-all-done.2.parts_ref, bf16[512,4096]{1,0:T(8,128)(2,1)S(1)} %copy-done.1, bf16[32,512]{1,0:T(8,128)(2,1)S(1)} %copy-done.9, bf16[32,512]{1,0:T(8,128)(2,1)S(1)} %collective-permute-done.refs_1_, ...), custom_call_target="tpu_custom_call" | custom-call | tf_op jit(solution)/shard_map/coarse_adjoint/pallas_call | solution.py:318
  79.5 3.3 %collective-permute-start.13 = (bf16[2,32,512]{2,1,0:T(8,128)(2,1)S(1)}, bf16[2,32,512]{2,1,0:T(8,128)(2,1)S(1)}, u32[]{:S(2)}, u32[]{:S(2)}) collective-permute-start(bf16[2,32,512]{2,1,0:T(8,128)(2,1)S(1)} %coarse_adjoint.1.refs_0_), channel_id=1, source_target_pairs={{0,7},{1,0},{2,1},{3,2},{4,3},{5,4},{6,5},{7,6},{8,15},{9,8},{10,9... | collective-permute-start | bytes 196616 | tf_op jit(solution)/shard_map/ppermute | solution.py:494
  82.7 0.6 collective-permute-start.11
  83.3 2.4 %collective-permute-start.10 = (bf16[2,32,512]{2,1,0:T(8,128)(2,1)S(1)}, bf16[2,32,512]{2,1,0:T(8,128)(2,1)S(1)}, u32[]{:S(2)}, u32[]{:S(2)}) collective-permute-start(bf16[2,32,512]{2,1,0:T(8,128)(2,1)S(1)} %coarse_adjoint.1.refs_0_), channel_id=1, source_target_pairs={{0,4},{1,5},{2,6},{3,7},{4,0},{5,1},{6,2},{7,3},{8,12},{9,13},{10,... | collective-permute-start | bytes 196616 | tf_op jit(solution)/shard_map/ppermute | solution.py:494
  85.8 0.8 collective-permute-start.8
  86.6 1.8 %collective-permute-start.7 = (bf16[2,32,512]{2,1,0:T(8,128)(2,1)S(1)}, bf16[2,32,512]{2,1,0:T(8,128)(2,1)S(1)}, u32[]{:S(2)}, u32[]{:S(2)}) collective-permute-start(bf16[2,32,512]{2,1,0:T(8,128)(2,1)S(1)} %coarse_adjoint.1.refs_0_), channel_id=1, source_target_pairs={{0,1},{1,2},{2,3},{3,4},{4,5},{5,6},{6,7},{7,0},{8,9},{9,10},{10,1... | collective-permute-start | bytes 196616 | tf_op jit(solution)/shard_map/ppermute | solution.py:494
  88.4 3.2 %collective-permute-done.9.refs_3_ = bf16[2,32,512]{2,1,0:T(8,128)(2,1)S(1)} collective-permute-done((bf16[2,32,512]{2,1,0:T(8,128)(2,1)S(1)}, bf16[2,32,512]{2,1,0:T(8,128)(2,1)S(1)}, u32[]{:S(2)}, u32[]{:S(2)}) %collective-permute-start.9) | collective-permute-done | bytes 65568 | tf_op jit(solution)/shard_map/ppermute | solution.py:494
  91.6 1.6 %collective-permute-done.8.refs_2_ = bf16[2,32,512]{2,1,0:T(8,128)(2,1)S(1)} collective-permute-done((bf16[2,32,512]{2,1,0:T(8,128)(2,1)S(1)}, bf16[2,32,512]{2,1,0:T(8,128)(2,1)S(1)}, u32[]{:S(2)}, u32[]{:S(2)}) %collective-permute-start.8) | collective-permute-done | bytes 65568 | tf_op jit(solution)/shard_map/ppermute | solution.py:494
  93.2 2.6 %spectrum_gradient.1 = bf16[128,8,128]{2,1,0:T(8,128)(2,1)S(1)} custom-call(f32[2,512,1024]{2,1,0:T(8,128)S(1)} %copy-done.3, f32[2,2,2,256,256]{4,3,2,1,0:T(8,128)S(1)} %copy-done, f32[256,512]{1,0:T(8,128)S(1)} %copy-done.6, f32[16,512]{1,0:T(8,128)S(1)} %copy-done.8, bf16[512,1024]{1,0:T(8,128)(2,1)S(1)} %copy-done.4, ...), custom_call_target="tpu_custom_call" | custom-call | tf_op jit(solution)/shard_map/spectrum_gradient/pallas_call | solution.py:387
  95.9 20.5 %all_to_all.27 = bf16[128,8,128]{2,1,0:T(8,128)(2,1)S(1)} all-to-all(bf16[128,8,128]{2,1,0:T(8,128)(2,1)S(1)} %spectrum_gradient.1), channel_id=1, replica_groups=mesh['rows'=16,'kern'=8] {'rows','kern'}, dimensions={0} | all-to-all | bytes 524288 | tf_op jit(solution)/shard_map/all_to_all | solution.py:480
  116.5 15.4 %all_to_all.28.tiles_ref = bf16[128,8,128]{2,1,0:T(8,128)(2,1)} all-to-all(bf16[128,8,128]{2,1,0:T(8,128)(2,1)S(1)} %broadcast_in_dim.5), channel_id=1, replica_groups=mesh['rows'=16,'kern'=8] {'rows','kern'}, dimensions={0} | all-to-all | bytes 524288 | tf_op jit(solution)/shard_map/all_to_all | solution.py:480
  131.9 11.3 %mask_update.1 = f32[128,16384]{1,0:T(8,128)} custom-call(bf16[128,8,128]{2,1,0:T(8,128)(2,1)} %all_to_all.28.tiles_ref, f32[128,512]{1,0:T(8,128)} %constant.23.clone.base_ref, f32[128,512]{1,0:T(8,128)} %constant.24.clone.shift_ref, f32[128,16384]{1,0:T(8,128)} %mask_ref.3, bf16[512,256]{1,0:T(8,128)(2,1)} %constant.30.clone.step_ref, ...), custom_call_target="tpu_custom_call" | custom-call | tf_op jit(solution)/shard_map/mask_update/pallas_call | solution.py:455
  (41 shorter events, 0.3 us)
Async XLA Ops:
  0.0 48.1 %copy-start.4 = (bf16[512,1024]{1,0:T(8,128)(2,1)S(1)}, bf16[512,1024]{1,0:T(8,128)(2,1)}, u32[]{:S(2)}) copy-start(bf16[512,1024]{1,0:T(8,128)(2,1)} %constant.27.clone.map_ref) | copy-start | bytes 3145732
  0.0 48.1 %copy-start.8 = (f32[16,512]{1,0:T(8,128)S(1)}, f32[16,512]{1,0:T(8,128)}, u32[]{:S(2)}) copy-start(f32[16,512]{1,0:T(8,128)} %constant.26.clone.shift_ref) | copy-start | bytes 98308
  0.0 48.1 %copy-start = (f32[2,2,2,256,256]{4,3,2,1,0:T(8,128)S(1)}, f32[2,2,2,256,256]{4,3,2,1,0:T(8,128)}, u32[]{:S(2)}) copy-start(f32[2,2,2,256,256]{4,3,2,1,0:T(8,128)} %pupil_ref.3) | copy-start | bytes 6291460
  10.2 58.2 %copy-start.11 = (bf16[32,512]{1,0:T(8,128)(2,1)S(1)}, bf16[32,512]{1,0:T(8,128)(2,1)}, u32[]{:S(2)}) copy-start(bf16[32,512]{1,0:T(8,128)(2,1)} %get-tuple-element.25) | copy-start | bytes 98308
  10.3 59.2 %copy-start.10 = (bf16[32,512]{1,0:T(8,128)(2,1)S(1)}, bf16[32,512]{1,0:T(8,128)(2,1)}, u32[]{:S(2)}) copy-start(bf16[32,512]{1,0:T(8,128)(2,1)} %get-tuple-element.26) | copy-start | bytes 98308
  10.3 61.9 %copy-start.9 = (bf16[32,512]{1,0:T(8,128)(2,1)S(1)}, bf16[32,512]{1,0:T(8,128)(2,1)}, u32[]{:S(2)}) copy-start(bf16[32,512]{1,0:T(8,128)(2,1)} %get-tuple-element.19.refs_0_) | copy-start | bytes 98308
  33.0 25.7 %copy-start.14 = (bf16[32,512]{1,0:T(8,128)(2,1)S(1)}, bf16[32,512]{1,0:T(8,128)(2,1)}, u32[]{:S(2)}) copy-start(bf16[32,512]{1,0:T(8,128)(2,1)} %get-tuple-element.20) | copy-start | bytes 98308
  33.0 27.1 %copy-start.13 = (bf16[32,512]{1,0:T(8,128)(2,1)S(1)}, bf16[32,512]{1,0:T(8,128)(2,1)}, u32[]{:S(2)}) copy-start(bf16[32,512]{1,0:T(8,128)(2,1)} %get-tuple-element.21) | copy-start | bytes 98308
  33.0 31.8 %copy-start.12 = (bf16[32,512]{1,0:T(8,128)(2,1)S(1)}, bf16[32,512]{1,0:T(8,128)(2,1)}, u32[]{:S(2)}) copy-start(bf16[32,512]{1,0:T(8,128)(2,1)} %get-tuple-element.24) | copy-start | bytes 98308
  48.1 1.0 copy-start.5
  51.7 2.0 %copy-start.2 = (f32[2,512,1024]{2,1,0:T(8,128)}, f32[2,512,1024]{2,1,0:T(8,128)S(1)}, u32[]{:S(2)}) copy-start(f32[2,512,1024]{2,1,0:T(8,128)S(1)} %get-tuple-element.17.field_ref) | copy-start | bytes 12582916
  53.8 0.8 copy-start.7
  54.6 17.6 %all-to-all-start.2 = ((bf16[8,2,32,512]{3,2,1,0:T(8,128)(2,1)}), bf16[8,2,32,512]{3,2,1,0:T(8,128)(2,1)}, u32[]{:S(2)}, u32[]{:S(2)}) async-start(bf16[8,2,32,512]{3,2,1,0:T(8,128)(2,1)} %copy-done.7), calls=%async_computation.2 | async-start | bytes 1048576 | tf_op jit(solution)/shard_map/all_to_all | solution.py:480
  58.7 9.8 %collective-permute-start = (bf16[32,512]{1,0:T(8,128)(2,1)S(1)}, bf16[32,512]{1,0:T(8,128)(2,1)S(1)}, u32[]{:S(2)}, u32[]{:S(2)}) collective-permute-start(bf16[32,512]{1,0:T(8,128)(2,1)S(1)} %copy-done.14), channel_id=1, source_target_pairs={{0,1},{1,2},{2,3},{3,4},{4,5},{5,6},{6,7},{7,0},{8,9},{9,10},{10,1... | collective-permute-start | bytes 98312 | tf_op jit(solution)/shard_map/ppermute | solution.py:494
  60.0 9.4 %collective-permute-start.1 = (bf16[32,512]{1,0:T(8,128)(2,1)S(1)}, bf16[32,512]{1,0:T(8,128)(2,1)S(1)}, u32[]{:S(2)}, u32[]{:S(2)}) collective-permute-start(bf16[32,512]{1,0:T(8,128)(2,1)S(1)} %copy-done.13), channel_id=1, source_target_pairs={{0,2},{1,3},{2,4},{3,5},{4,6},{5,7},{6,0},{7,1},{8,10},{9,11},{10,... | collective-permute-start | bytes 98312 | tf_op jit(solution)/shard_map/ppermute | solution.py:494
  61.2 8.9 %collective-permute-start.2 = (bf16[32,512]{1,0:T(8,128)(2,1)}, bf16[32,512]{1,0:T(8,128)(2,1)S(1)}, u32[]{:S(2)}, u32[]{:S(2)}) collective-permute-start(bf16[32,512]{1,0:T(8,128)(2,1)} %get-tuple-element.22), channel_id=1, source_target_pairs={{0,3},{1,4},{2,5},{3,6},{4,7},{5,0},{6,1},{7,2},{8,11},{9,12},{10,... | collective-permute-start | bytes 98312 | tf_op jit(solution)/shard_map/ppermute | solution.py:494
  63.0 7.1 %collective-permute-start.3 = (bf16[32,512]{1,0:T(8,128)(2,1)}, bf16[32,512]{1,0:T(8,128)(2,1)S(1)}, u32[]{:S(2)}, u32[]{:S(2)}) collective-permute-start(bf16[32,512]{1,0:T(8,128)(2,1)} %get-tuple-element.23), channel_id=1, source_target_pairs={{0,4},{1,5},{2,6},{3,7},{4,0},{5,1},{6,2},{7,3},{8,12},{9,13},{10,... | collective-permute-start | bytes 98312 | tf_op jit(solution)/shard_map/ppermute | solution.py:494
  64.8 5.4 %collective-permute-start.4 = (bf16[32,512]{1,0:T(8,128)(2,1)S(1)}, bf16[32,512]{1,0:T(8,128)(2,1)S(1)}, u32[]{:S(2)}, u32[]{:S(2)}) collective-permute-start(bf16[32,512]{1,0:T(8,128)(2,1)S(1)} %copy-done.12), channel_id=1, source_target_pairs={{0,5},{1,6},{2,7},{3,0},{4,1},{5,2},{6,3},{7,4},{8,13},{9,14},{10,... | collective-permute-start | bytes 98312 | tf_op jit(solution)/shard_map/ppermute | solution.py:494
  68.5 3.0 %collective-permute-start.5 = (bf16[32,512]{1,0:T(8,128)(2,1)S(1)}, bf16[32,512]{1,0:T(8,128)(2,1)S(1)}, u32[]{:S(2)}, u32[]{:S(2)}) collective-permute-start(bf16[32,512]{1,0:T(8,128)(2,1)S(1)} %copy-done.11), channel_id=1, source_target_pairs={{0,6},{1,7},{2,0},{3,1},{4,2},{5,3},{6,4},{7,5},{8,14},{9,15},{10,... | collective-permute-start | bytes 98312 | tf_op jit(solution)/shard_map/ppermute | solution.py:494
  69.4 2.8 %collective-permute-start.6 = (bf16[32,512]{1,0:T(8,128)(2,1)S(1)}, bf16[32,512]{1,0:T(8,128)(2,1)S(1)}, u32[]{:S(2)}, u32[]{:S(2)}) collective-permute-start(bf16[32,512]{1,0:T(8,128)(2,1)S(1)} %copy-done.10), channel_id=1, source_target_pairs={{0,7},{1,0},{2,1},{3,2},{4,3},{5,4},{6,5},{7,6},{8,15},{9,8},{10,9... | collective-permute-start | bytes 98312 | tf_op jit(solution)/shard_map/ppermute | solution.py:494
  72.2 2.2 %copy-start.1 = (bf16[512,4096]{1,0:T(8,128)(2,1)S(1)}, bf16[512,4096]{1,0:T(8,128)(2,1)}, u32[]{:S(2)}) copy-start(bf16[512,4096]{1,0:T(8,128)(2,1)} %constant.29.clone.matrix_ref) | copy-start | bytes 12582916
  74.4 18.8 %copy-start.3 = (f32[2,512,1024]{2,1,0:T(8,128)S(1)}, f32[2,512,1024]{2,1,0:T(8,128)}, u32[]{:S(2)}) copy-start(f32[2,512,1024]{2,1,0:T(8,128)} %copy-done.2) | copy-start | bytes 12582916
  74.4 18.8 %copy-start.6 = (f32[256,512]{1,0:T(8,128)S(1)}, f32[256,512]{1,0:T(8,128)}, u32[]{:S(2)}) copy-start(f32[256,512]{1,0:T(8,128)} %constant.25.clone.base_ref) | copy-start | bytes 1572868
  79.5 6.3 %collective-permute-start.13 = (bf16[2,32,512]{2,1,0:T(8,128)(2,1)S(1)}, bf16[2,32,512]{2,1,0:T(8,128)(2,1)S(1)}, u32[]{:S(2)}, u32[]{:S(2)}) collective-permute-start(bf16[2,32,512]{2,1,0:T(8,128)(2,1)S(1)} %coarse_adjoint.1.refs_0_), channel_id=1, source_target_pairs={{0,7},{1,0},{2,1},{3,2},{4,3},{5,4},{6,5},{7,6},{8,15},{9,8},{10,9... | collective-permute-start | bytes 196616 | tf_op jit(solution)/shard_map/ppermute | solution.py:494
  82.7 3.8 %collective-permute-start.12 = (bf16[2,32,512]{2,1,0:T(8,128)(2,1)S(1)}, bf16[2,32,512]{2,1,0:T(8,128)(2,1)S(1)}, u32[]{:S(2)}, u32[]{:S(2)}) collective-permute-start(bf16[2,32,512]{2,1,0:T(8,128)(2,1)S(1)} %coarse_adjoint.1.refs_0_), channel_id=1, source_target_pairs={{0,6},{1,7},{2,0},{3,1},{4,2},{5,3},{6,4},{7,5},{8,14},{9,15},{10,... | collective-permute-start | bytes 196616 | tf_op jit(solution)/shard_map/ppermute | solution.py:494
  82.7 5.6 %collective-permute-start.11 = (bf16[2,32,512]{2,1,0:T(8,128)(2,1)S(1)}, bf16[2,32,512]{2,1,0:T(8,128)(2,1)S(1)}, u32[]{:S(2)}, u32[]{:S(2)}) collective-permute-start(bf16[2,32,512]{2,1,0:T(8,128)(2,1)S(1)} %coarse_adjoint.1.refs_0_), channel_id=1, source_target_pairs={{0,5},{1,6},{2,7},{3,0},{4,1},{5,2},{6,3},{7,4},{8,13},{9,14},{10,... | collective-permute-start | bytes 196616 | tf_op jit(solution)/shard_map/ppermute | solution.py:494
  83.3 5.0 %collective-permute-start.10 = (bf16[2,32,512]{2,1,0:T(8,128)(2,1)S(1)}, bf16[2,32,512]{2,1,0:T(8,128)(2,1)S(1)}, u32[]{:S(2)}, u32[]{:S(2)}) collective-permute-start(bf16[2,32,512]{2,1,0:T(8,128)(2,1)S(1)} %coarse_adjoint.1.refs_0_), channel_id=1, source_target_pairs={{0,4},{1,5},{2,6},{3,7},{4,0},{5,1},{6,2},{7,3},{8,12},{9,13},{10,... | collective-permute-start | bytes 196616 | tf_op jit(solution)/shard_map/ppermute | solution.py:494
  85.8 5.8 %collective-permute-start.9 = (bf16[2,32,512]{2,1,0:T(8,128)(2,1)S(1)}, bf16[2,32,512]{2,1,0:T(8,128)(2,1)S(1)}, u32[]{:S(2)}, u32[]{:S(2)}) collective-permute-start(bf16[2,32,512]{2,1,0:T(8,128)(2,1)S(1)} %coarse_adjoint.1.refs_0_), channel_id=1, source_target_pairs={{0,3},{1,4},{2,5},{3,6},{4,7},{5,0},{6,1},{7,2},{8,11},{9,12},{10,... | collective-permute-start | bytes 196616 | tf_op jit(solution)/shard_map/ppermute | solution.py:494
  85.8 7.4 %collective-permute-start.8 = (bf16[2,32,512]{2,1,0:T(8,128)(2,1)S(1)}, bf16[2,32,512]{2,1,0:T(8,128)(2,1)S(1)}, u32[]{:S(2)}, u32[]{:S(2)}) collective-permute-start(bf16[2,32,512]{2,1,0:T(8,128)(2,1)S(1)} %coarse_adjoint.1.refs_0_), channel_id=1, source_target_pairs={{0,2},{1,3},{2,4},{3,5},{4,6},{5,7},{6,0},{7,1},{8,10},{9,11},{10,... | collective-permute-start | bytes 196616 | tf_op jit(solution)/shard_map/ppermute | solution.py:494
  86.6 6.6 %collective-permute-start.7 = (bf16[2,32,512]{2,1,0:T(8,128)(2,1)S(1)}, bf16[2,32,512]{2,1,0:T(8,128)(2,1)S(1)}, u32[]{:S(2)}, u32[]{:S(2)}) collective-permute-start(bf16[2,32,512]{2,1,0:T(8,128)(2,1)S(1)} %coarse_adjoint.1.refs_0_), channel_id=1, source_target_pairs={{0,1},{1,2},{2,3},{3,4},{4,5},{5,6},{6,7},{7,0},{8,9},{9,10},{10,1... | collective-permute-start | bytes 196616 | tf_op jit(solution)/shard_map/ppermute | solution.py:494

commit v3 on v2

v3 whole, which is shorter than its diff:
```python
import math

import jax
import jax.numpy as jnp
import numpy as np
from jax import lax
from jax.experimental import pallas as pl
from jax.experimental.pallas import tpu as pltpu
from jax.sharding import PartitionSpec as P

MASK = 16384
GRID = 4096
BAND = 256
HALF = BAND // 2
COARSE = 512
STEP = 256
STEPS = MASK // STEP
ROWS = 16
KERN = 8
DEVICES = ROWS * KERN
WIDTH = 2048
CHUNKS = MASK // WIDTH
PER = WIDTH // STEP

steepness = 4.0
threshold = 0.75
step_size = 1.0
dose_levels = (1.0, 1.15)

VMEM_LIMIT = 24 * 1024 * 1024
STREAM_LIMIT = 56 * 1024 * 1024
HIGHEST = lax.Precision.HIGHEST


def tables(positions, period, count=BAND):
    frequency = np.arange(count) - BAND // 2
    angles = (np.outer(positions, frequency) % period) * (2.0 * math.pi / period)
    return np.cos(angles), np.sin(angles)


def bfloat(values):
    return np.asarray(values, np.float32).astype(jnp.bfloat16)


def wide_table(positions, period, count=BAND):
    return np.concatenate(tables(positions, period, count), 1).astype(np.float32)


def step_table():
    cosine, sine = tables(np.arange(STEP), MASK, HALF)
    return bfloat(np.concatenate([cosine, -sine], 1) / MASK)


def coarse_map():
    cosine, sine = tables(np.arange(COARSE), COARSE)
    upper = np.concatenate([cosine.T, sine.T], 1)
    lower = np.concatenate([-sine.T, cosine.T], 1)
    return bfloat(np.concatenate([upper, lower], 0))


def interpolation():
    ratio = GRID // COARSE
    frequency = np.arange(1, COARSE // 2)
    offset = np.arange(GRID)
    profile = 1.0 + 2.0 * np.cos(2.0 * math.pi * (np.outer(offset, frequency) % GRID) / GRID).sum(1)
    profile = (profile + np.cos(math.pi * offset / ratio)) / COARSE
    return bfloat(profile[(offset[None, :] - ratio * np.arange(COARSE)[:, None]) % GRID])


def device_place():
    return lax.axis_index("rows") * KERN + lax.axis_index("kern")


def turned_table(base, shift):
    cosine = base[:, :BAND] * shift[:, :BAND] - base[:, BAND:] * shift[:, BAND:]
    sine = base[:, BAND:] * shift[:, :BAND] + base[:, :BAND] * shift[:, BAND:]
    return cosine, sine


def whole_spec(shape):
    return pl.BlockSpec(shape, lambda i: (0,) * len(shape))


def params(limit=VMEM_LIMIT):
    return pltpu.CompilerParams(vmem_limit_bytes=limit)


def float_dot(left, right):
    return jnp.dot(left, right, preferred_element_type=jnp.float32)


def dot_first(left, right, precision=None):
    return lax.dot_general(
        left, right, (((0,), (0,)), ((), ())), precision=precision, preferred_element_type=jnp.float32
    )


def dot_last(left, right):
    return lax.dot_general(left, right, (((1,), (1,)), ((), ())), preferred_element_type=jnp.float32)


def split(values):
    high = values.astype(jnp.bfloat16)
    return high, (values - high.astype(jnp.float32)).astype(jnp.bfloat16)


def iotas(shape):
    return lax.broadcasted_iota(jnp.int32, shape, 0), lax.broadcasted_iota(jnp.int32, shape, 1)


def row_mirror():
    row, column = iotas((BAND, BAND))
    return jnp.where(row + column == BAND, 1.0, 0.0).astype(jnp.bfloat16)


def conjugate_mirror():
    row, column = iotas((BAND, BAND))
    real = (row + column == HALF) & (row < HALF) & (column > 0) & (column < HALF)
    imag = (row + column == 2 * HALF + HALF) & (row >= HALF) & (column > HALF)
    return (jnp.where(real, 1.0, 0.0) - jnp.where(imag, 1.0, 0.0)).astype(jnp.bfloat16)


def diagonal():
    row, column = iotas((BAND, BAND))
    return row == column


def store_tiles(out_ref, real, imag):
    for part, value in enumerate((real, imag)):
        for i in range(BAND // 8):
            for j in range(2):
                out_ref[4 * i + 2 * part + j] = value[8 * i : 8 * i + 8, 128 * j : 128 * j + 128].astype(
                    out_ref.dtype
                )


def load_tiles(tiles_ref, held_ref):
    for part in range(2):
        for i in range(BAND // 8):
            for j in range(2):
                held_ref[part, 8 * i : 8 * i + 8, 128 * j : 128 * j + 128] = tiles_ref[
                    4 * i + 2 * part + j
                ].astype(jnp.float32)


def spectrum_kernel(
    mask_ref, step_ref, phase_ref, base_ref, shift_ref, grid_base_ref, grid_shift_ref, target_ref,
    out_ref, rows_ref, wanted_ref,
    held_ref, steps_ref, phases_ref, bases_ref, shifts_ref, grid_bases_ref, grid_shifts_ref, targets_ref,
    stack_a, stack_b, product_a, product_b, re_ref, im_ref, flat_ref, sems,
):
    rows = mask_ref.shape[0]
    stacks = (stack_a, stack_b)
    products = (product_a, product_b)
    chunks = [
        pltpu.make_async_copy(mask_ref.at[:, pl.ds(i * WIDTH, WIDTH)], held_ref.at[i], sems.at[i])
        for i in range(CHUNKS)
    ]
    small = [
        pltpu.make_async_copy(source, target, sems.at[CHUNKS + i])
        for i, (source, target) in enumerate(
            (
                (step_ref, steps_ref),
                (phase_ref, phases_ref),
                (grid_base_ref, grid_bases_ref),
                (grid_shift_ref.at[lax.axis_index("rows")], grid_shifts_ref),
                (target_ref, targets_ref),
                (base_ref, bases_ref),
                (shift_ref.at[device_place()], shifts_ref),
            )
        )
    ]
    chunks[0].start()
    small[0].start()
    chunks[1].start()
    for copy in small[1:] + chunks[2:]:
        copy.start()

    def transmit(i):
        chunks[i].wait()
        total = jnp.zeros((rows, HALF), jnp.float32)
        for part in range(PER):
            value = jnp.tanh(held_ref[i, :, part * STEP : (part + 1) * STEP]).astype(jnp.bfloat16)
            stacks[i % 2][part * rows : (part + 1) * rows] = value
            wide = value.astype(jnp.float32)
            total = total + (wide[:, :HALF] + wide[:, HALF:])
        flat_ref[...] = total if i == 0 else flat_ref[...] + total

    def gather(i):
        piece = 32
        for start in range(0, rows, piece):
            total_re = None
            for part in range(PER):
                at = part * rows + start
                step = i * PER + part
                cosine = phases_ref[step : step + 1, :HALF]
                sine = phases_ref[step : step + 1, HALF:]
                first = products[i % 2][at : at + piece, :HALF]
                second = products[i % 2][at : at + piece, HALF:]
                turned_re = first * cosine + second * sine
                turned_im = second * cosine - first * sine
                total_re = turned_re if part == 0 else total_re + turned_re
                total_im = turned_im if part == 0 else total_im + turned_im
            here = slice(start, start + piece)
            re_ref[here] = total_re if i == 0 else re_ref[here] + total_re
            im_ref[here] = total_im if i == 0 else im_ref[here] + total_im

    transmit(0)
    small[0].wait()
    small[1].wait()
    for i in range(CHUNKS):
        products[i % 2][...] = float_dot(stacks[i % 2][...], steps_ref[...])
        if i + 1 < CHUNKS:
            transmit(i + 1)
        if i > 0:
            gather(i - 1)
    gather(CHUNKS - 1)
    for copy in small[2:]:
        copy.wait()
    cosine, sine = turned_table(grid_bases_ref[...], grid_shifts_ref[...])
    rows_ref[:, :BAND] = cosine.astype(jnp.bfloat16)
    rows_ref[:, BAND:] = sine.astype(jnp.bfloat16)
    wanted_ref[...] = targets_ref[...].astype(jnp.float32).astype(jnp.bfloat16)
    table = jnp.concatenate(turned_table(bases_ref[...], shifts_ref[...]), 1)
    product = dot_first(table, jnp.concatenate([re_ref[...], im_ref[...]], 1), HIGHEST)
    by_cos = product[:BAND]
    by_sin = product[BAND:]
    half_re = by_cos[:, :HALF] + by_sin[:, HALF:]
    half_im = by_cos[:, HALF:] - by_sin[:, :HALF]
    beyond_re = by_cos[:1, :HALF] - by_sin[:1, HALF:]
    beyond_im = by_cos[:1, HALF:] + by_sin[:1, :HALF]
    centre = jnp.sum(dot_first(flat_ref[...], table, HIGHEST), 0, keepdims=True) * (1.0 / MASK)
    mirror = conjugate_mirror()
    flip = row_mirror()
    row, column = iotas((BAND, HALF))
    whole = jnp.concatenate([half_re, half_im], 1)
    ends = jnp.concatenate([beyond_re, beyond_im], 1)
    other = 0.0
    for piece, end in zip(split(whole), split(jnp.concatenate([ends] * 8, 0))):
        turned = float_dot(flip, float_dot(piece, mirror).astype(jnp.bfloat16))
        other = other + jnp.where(iotas((BAND, BAND))[0] == 0, float_dot(end, mirror)[:1], turned)
    parts = []
    for part, value in enumerate((centre[:, :BAND], -centre[:, BAND:])):
        line = jnp.sum(jnp.where(diagonal(), value, 0.0), 1, keepdims=True)
        parts.append(jnp.where(column == 0, line, other[:, part * HALF : (part + 1) * HALF]))
    store_tiles(
        out_ref, jnp.concatenate([half_re, parts[0]], 1), jnp.concatenate([half_im, parts[1]], 1)
    )


def mask_spectrum(mask_params, step_value, phases, base, shifts, grid_base, grid_shifts, target):
    rows = mask_params.shape[0]
    stacked = rows * PER
    arguments = (mask_params, step_value, phases, base, shifts, grid_base, grid_shifts, target)
    grid_rows = grid_base.shape[0]
    return pl.pallas_call(
        spectrum_kernel,
        in_specs=[pl.BlockSpec(memory_space=pltpu.HBM)] * len(arguments),
        out_specs=[pl.BlockSpec(memory_space=pltpu.VMEM)] * 3,
        out_shape=[
            jax.ShapeDtypeStruct((DEVICES, 8, 128), jnp.bfloat16),
            jax.ShapeDtypeStruct((grid_rows, 2 * BAND), jnp.bfloat16),
            jax.ShapeDtypeStruct(target.shape, jnp.bfloat16),
        ],
        scratch_shapes=[
            pltpu.VMEM((CHUNKS, rows, WIDTH), jnp.float32),
            pltpu.VMEM(step_value.shape, jnp.bfloat16),
            pltpu.VMEM(phases.shape, jnp.float32),
            pltpu.VMEM(base.shape, jnp.float32),
            pltpu.VMEM((1, 2 * BAND), jnp.float32),
            pltpu.VMEM(grid_base.shape, jnp.float32),
            pltpu.VMEM((1, 2 * BAND), jnp.float32),
            pltpu.VMEM(target.shape, jnp.int32),
            pltpu.VMEM((stacked, STEP), jnp.bfloat16),
            pltpu.VMEM((stacked, STEP), jnp.bfloat16),
            pltpu.VMEM((stacked, BAND), jnp.float32),
            pltpu.VMEM((stacked, BAND), jnp.float32),
            pltpu.VMEM((rows, HALF), jnp.float32),
            pltpu.VMEM((rows, HALF), jnp.float32),
            pltpu.VMEM((rows, HALF), jnp.float32),
            pltpu.SemaphoreType.DMA((CHUNKS + 7,)),
        ],
        compiler_params=params(STREAM_LIMIT),
        name="mask_spectrum",
    )(*arguments)


def field_kernel(
    tiles_ref, pupil_ref, wanted_ref, rows_ref, map_ref, field_ref, power_ref,
    spec_ref, partial_ref, sum_ref,
):
    index = pl.program_id(0)
    rows = wanted_ref.shape[0]
    slab = rows // KERN

    @pl.when(index == 0)
    def _():
        load_tiles(tiles_ref, spec_ref)
        for owner in range(KERN):
            power_ref[owner, 2] = wanted_ref[owner * slab : (owner + 1) * slab]

    spec_re = spec_ref[0]
    spec_im = spec_ref[1]
    for corner in range(2):
        kernel_re = pupil_ref[0, corner, 0]
        kernel_im = pupil_ref[0, corner, 1]
        amp_re = (kernel_re * spec_re - kernel_im * spec_im).astype(jnp.bfloat16)
        amp_im = (kernel_re * spec_im + kernel_im * spec_re).astype(jnp.bfloat16)
        block = jnp.concatenate(
            [jnp.concatenate([amp_re, amp_im], 1), jnp.concatenate([-amp_im, amp_re], 1)], 0
        )
        partial_ref[corner * rows : (corner + 1) * rows] = float_dot(rows_ref[...], block).astype(
            jnp.bfloat16
        )
    field_ref[0] = float_dot(partial_ref[...], map_ref[...])

    for corner in range(2):
        for owner in range(KERN):
            at = corner * rows + owner * slab
            real = field_ref[0, at : at + slab, :COARSE]
            imag = field_ref[0, at : at + slab, COARSE:]
            power = real * real + imag * imag

            @pl.when(index == 0)
            def _():
                sum_ref[at : at + slab] = power

            @pl.when(index == 1)
            def _():
                power_ref[owner, corner] = (sum_ref[at : at + slab] + power).astype(jnp.bfloat16)


def coarse_fields(tiles, pupils, wanted, rows_table, column_map):
    members = pupils.shape[0]
    rows = wanted.shape[0]
    return pl.pallas_call(
        field_kernel,
        grid=(members,),
        in_specs=[
            whole_spec(tiles.shape),
            pl.BlockSpec((1, 2, 2, BAND, BAND), lambda i: (i, 0, 0, 0, 0)),
            whole_spec(wanted.shape),
            whole_spec(rows_table.shape),
            whole_spec(column_map.shape),
        ],
        out_specs=[
            pl.BlockSpec((1, 2 * rows, 2 * COARSE), lambda i: (i, 0, 0)),
            whole_spec((KERN, 3, rows // KERN, COARSE)),
        ],
        out_shape=[
            jax.ShapeDtypeStruct((members, 2 * rows, 2 * COARSE), jnp.float32),
            jax.ShapeDtypeStruct((KERN, 3, rows // KERN, COARSE), jnp.bfloat16),
        ],
        scratch_shapes=[
            pltpu.VMEM((2, BAND, BAND), jnp.float32),
            pltpu.VMEM((2 * rows, 2 * BAND), jnp.bfloat16),
            pltpu.VMEM((2 * rows, COARSE), jnp.float32),
        ],
        compiler_params=params(),
        name="coarse_fields",
    )(tiles, pupils, wanted, rows_table, column_map)


def adjoint_kernel(parts_ref, matrix_ref, out_ref, power_ref, acc_ref):
    index = pl.program_id(0)
    rows = parts_ref.shape[2]

    @pl.when(index == 0)
    def _():
        for corner in range(2):
            total = parts_ref[0, corner].astype(jnp.float32)
            for owner in range(1, KERN):
                total = total + parts_ref[owner, corner].astype(jnp.float32)
            power_ref[corner * rows : (corner + 1) * rows] = total.astype(jnp.bfloat16)
        acc_ref[...] = jnp.zeros_like(acc_ref)

    fine = float_dot(power_ref[...], matrix_ref[...])
    wanted = parts_ref[index, 2].astype(jnp.float32)
    corners = []
    for corner in range(2):
        dose = dose_levels[corner]
        resist = jax.nn.sigmoid(steepness * (dose * fine[corner * rows : (corner + 1) * rows] - threshold))
        corners.append(
            (2.0 * (resist - wanted) * resist * (1.0 - resist) * steepness * dose).astype(jnp.bfloat16)
        )
    acc_ref[...] += dot_last(jnp.concatenate(corners, 0), matrix_ref[...])

    @pl.when(index == pl.num_programs(0) - 1)
    def _():
        folded = acc_ref[...].reshape(2, rows, COARSE).astype(jnp.bfloat16)
        for owner in range(KERN):
            out_ref[owner] = folded


def coarse_adjoint(parts, matrix):
    rows = parts.shape[2]
    width = GRID // KERN
    return pl.pallas_call(
        adjoint_kernel,
        grid=(KERN,),
        in_specs=[
            whole_spec(parts.shape),
            pl.BlockSpec((COARSE, width), lambda i: (0, i)),
        ],
        out_specs=whole_spec((KERN, 2, rows, COARSE)),
        out_shape=jax.ShapeDtypeStruct((KERN, 2, rows, COARSE), jnp.bfloat16),
        scratch_shapes=[
            pltpu.VMEM((2 * rows, COARSE), jnp.bfloat16),
            pltpu.VMEM((2 * rows, COARSE), jnp.float32),
        ],
        compiler_params=params(),
        name="coarse_adjoint",
    )(parts, matrix)


def gradient_kernel(
    field_ref, adjoint_ref, pupil_ref, rows_ref, map_ref, out_ref, weighted_ref, back_ref, acc_ref
):
    index = pl.program_id(0)
    slab = adjoint_ref.shape[2]
    rows = slab * KERN

    @pl.when(index == 0)
    def _():
        acc_ref[...] = jnp.zeros_like(acc_ref)

    for corner in range(2):
        for owner in range(KERN):
            at = corner * rows + owner * slab
            adjoint = 2.0 * adjoint_ref[owner, corner].astype(jnp.float32)
            for half in range(2):
                columns = slice(half * COARSE, (half + 1) * COARSE)
                weighted_ref[at : at + slab, columns] = (field_ref[0, at : at + slab, columns] * adjoint).astype(
                    jnp.bfloat16
                )
    back_ref[...] = dot_last(weighted_ref[...], map_ref[...]).astype(jnp.bfloat16)
    for corner in range(2):
        grads = dot_first(rows_ref[...], back_ref[corner * rows : (corner + 1) * rows])
        grad_re = grads[:BAND, :BAND] + grads[BAND:, BAND:]
        grad_im = grads[:BAND, BAND:] - grads[BAND:, :BAND]
        kernel_re = pupil_ref[0, corner, 0]
        kernel_im = pupil_ref[0, corner, 1]
        acc_ref[0] += kernel_re * grad_re + kernel_im * grad_im
        acc_ref[1] += kernel_re * grad_im - kernel_im * grad_re

    @pl.when(index == pl.num_programs(0) - 1)
    def _():
        store_tiles(out_ref, acc_ref[0], acc_ref[1])


def spectrum_gradient(fields, adjoint, pupils, rows_table, column_map):
    members = pupils.shape[0]
    rows = rows_table.shape[0]
    return pl.pallas_call(
        gradient_kernel,
        grid=(members,),
        in_specs=[
            pl.BlockSpec((1, 2 * rows, 2 * COARSE), lambda i: (i, 0, 0)),
            whole_spec(adjoint.shape),
            pl.BlockSpec((1, 2, 2, BAND, BAND), lambda i: (i, 0, 0, 0, 0)),
            whole_spec(rows_table.shape),
            whole_spec(column_map.shape),
        ],
        out_specs=whole_spec((DEVICES, 8, 128)),
        out_shape=jax.ShapeDtypeStruct((DEVICES, 8, 128), jnp.bfloat16),
        scratch_shapes=[
            pltpu.VMEM((2 * rows, 2 * COARSE), jnp.bfloat16),
            pltpu.VMEM((2 * rows, 2 * BAND), jnp.bfloat16),
            pltpu.VMEM((2, BAND, BAND), jnp.float32),
        ],
        compiler_params=params(),
        name="spectrum_gradient",
    )(fields, adjoint, pupils, rows_table, column_map)


def update_kernel(
    tiles_ref, base_ref, shift_ref, mask_ref, step_ref, phase_ref, out_ref,
    spec_ref, bases_ref, shifts_ref, held_ref, steps_ref, phases_ref, re_ref, im_ref, stack_a, stack_b, product_a, product_b, sems,
):
    rows = mask_ref.shape[0]
    stacks = (stack_a, stack_b)
    products = (product_a, product_b)
    columns = [pl.ds(i * WIDTH, WIDTH) for i in range(CHUNKS)]
    chunks = [
        pltpu.make_async_copy(mask_ref.at[:, columns[i]], held_ref.at[i], sems.at[i]) for i in range(CHUNKS)
    ]
    results = [
        pltpu.make_async_copy(held_ref.at[i], out_ref.at[:, columns[i]], sems.at[CHUNKS + i])
        for i in range(CHUNKS)
    ]
    small = [
        pltpu.make_async_copy(source, target, sems.at[2 * CHUNKS + i])
        for i, (source, target) in enumerate(
            (
                (base_ref, bases_ref),
                (shift_ref.at[device_place()], shifts_ref),
                (phase_ref, phases_ref),
                (step_ref, steps_ref),
            )
        )
    ]
    for copy in small + chunks:
        copy.start()

    load_tiles(tiles_ref, spec_ref)
    left = jnp.concatenate([spec_ref[0, :, :HALF], spec_ref[1, :, :HALF]], 1)
    right = jnp.concatenate([spec_ref[0, :, HALF:], spec_ref[1, :, HALF:]], 1)
    turned = float_dot(right.astype(jnp.bfloat16), conjugate_mirror())
    half = split(left + float_dot(row_mirror(), turned.astype(jnp.bfloat16)))
    beyond_re = turned[:1, :HALF]
    beyond_im = turned[:1, HALF:]
    centres = [
        jnp.sum(jnp.where(diagonal(), spec_ref[part, :, HALF : HALF + 1], 0.0), 0, keepdims=True)
        for part in range(2)
    ]
    small[0].wait()
    small[1].wait()
    cosine, sine = turned_table(bases_ref[...], shifts_ref[...])
    high_cos, low_cos = split(cosine)
    high_sin, low_sin = split(sine)
    product = float_dot(jnp.concatenate([high_cos, low_cos, high_sin, low_sin], 0), half[0])
    rest = float_dot(jnp.concatenate([high_cos, high_sin], 0), half[1])
    by_cos = product[:rows] + (product[rows : 2 * rows] + rest[:rows])
    by_sin = product[2 * rows : 3 * rows] + (product[3 * rows :] + rest[rows:])
    edge_cos = cosine[:, :1]
    edge_sin = -sine[:, :1]
    re_ref[...] = by_cos[:, :HALF] - by_sin[:, HALF:] + (edge_cos * beyond_re - edge_sin * beyond_im)
    im_ref[...] = by_sin[:, :HALF] + by_cos[:, HALF:] + (edge_sin * beyond_re + edge_cos * beyond_im)
    centre = jnp.sum(cosine * centres[0] - sine * centres[1], 1, keepdims=True) * (1.0 / MASK)

    def turn(i):
        piece = 32
        for start in range(0, rows, piece):
            col_re = re_ref[start : start + piece]
            col_im = im_ref[start : start + piece]
            for part in range(PER):
                step = i * PER + part
                cosine = phases_ref[step : step + 1, :HALF]
                sine = phases_ref[step : step + 1, HALF:]
                at = part * rows + start
                stacks[i % 2][at : at + piece, :HALF] = (col_re * cosine - col_im * sine).astype(jnp.bfloat16)
                stacks[i % 2][at : at + piece, HALF:] = (col_re * sine + col_im * cosine).astype(jnp.bfloat16)

    def finish(i):
        for part in range(PER):
            here = slice(part * STEP, (part + 1) * STEP)
            mask = held_ref[i, :, here]
            transmit = jnp.tanh(mask)
            pixel_grad = products[i % 2][part * rows : (part + 1) * rows] + centre
            held_ref[i, :, here] = mask - step_size * pixel_grad * (1.0 - transmit * transmit)
        results[i].start()

    small[2].wait()
    turn(0)
    small[3].wait()
    for i in range(CHUNKS):
        chunks[i].wait()
        products[i % 2][...] = float_dot(stacks[i % 2][...], steps_ref[...])
        if i + 1 < CHUNKS:
            turn(i + 1)
        if i > 0:
            finish(i - 1)
    finish(CHUNKS - 1)
    for copy in results:
        copy.wait()


def mask_update(tiles, base, shifts, mask_params, step_value, phases):
    rows = mask_params.shape[0]
    stacked = rows * PER
    hbm = pl.BlockSpec(memory_space=pltpu.HBM)
    vmem = pl.BlockSpec(memory_space=pltpu.VMEM)
    return pl.pallas_call(
        update_kernel,
        in_specs=[vmem] + [hbm] * 5,
        out_specs=hbm,
        out_shape=jax.ShapeDtypeStruct((rows, MASK), jnp.float32),
        scratch_shapes=[
            pltpu.VMEM((2, BAND, BAND), jnp.float32),
            pltpu.VMEM(base.shape, jnp.float32),
            pltpu.VMEM((1, 2 * BAND), jnp.float32),
            pltpu.VMEM((CHUNKS, rows, WIDTH), jnp.float32),
            pltpu.VMEM(step_value.shape, jnp.bfloat16),
            pltpu.VMEM(phases.shape, jnp.float32),
            pltpu.VMEM((rows, HALF), jnp.float32),
            pltpu.VMEM((rows, HALF), jnp.float32),
            pltpu.VMEM((stacked, BAND), jnp.bfloat16),
            pltpu.VMEM((stacked, BAND), jnp.bfloat16),
            pltpu.VMEM((stacked, STEP), jnp.float32),
            pltpu.VMEM((stacked, STEP), jnp.float32),
            pltpu.SemaphoreType.DMA((2 * CHUNKS + 4,)),
        ],
        compiler_params=params(STREAM_LIMIT),
        name="mask_update",
    )(tiles, base, shifts, mask_params, step_value, phases)


def exchange(values, axes):
    return lax.all_to_all(values, axes, 0, 0, tiled=True)


def summed(parts, copies):
    total = jnp.sum(parts.astype(jnp.float32), 0).astype(parts.dtype)
    return jnp.broadcast_to(total[None], (copies,) + total.shape)


def sum_tiles(tiles):
    everyone = ("rows", "kern")
    return exchange(summed(exchange(tiles, everyone), DEVICES), everyone)


def local(mask_params, pupil_kernels, target_pattern):
    rows = mask_params.shape[0]
    grid_rows = target_pattern.shape[0]
    step_value = step_table()
    phases = jnp.asarray(wide_table(np.arange(STEPS) * STEP, MASK, HALF))
    mask_base = jnp.asarray(wide_table(np.arange(rows), MASK))
    mask_shifts = jnp.asarray(wide_table(np.arange(ROWS * KERN) * rows, MASK)[:, None, :])
    grid_base = jnp.asarray(wide_table(np.arange(grid_rows), GRID))
    grid_shifts = jnp.asarray(wide_table(np.arange(ROWS) * grid_rows, GRID)[:, None, :])
    column_map = jnp.asarray(coarse_map())

    tiles, rows_table, wanted = mask_spectrum(
        mask_params, jnp.asarray(step_value), phases, mask_base, mask_shifts, grid_base, grid_shifts, target_pattern
    )
    fields, powers = coarse_fields(sum_tiles(tiles), pupil_kernels, wanted, rows_table, column_map)
    adjoint = coarse_adjoint(exchange(powers, "kern"), jnp.asarray(interpolation()))
    gradient = spectrum_gradient(fields, exchange(adjoint, "kern"), pupil_kernels, rows_table, column_map)
    return mask_update(
        sum_tiles(gradient), mask_base, mask_shifts, mask_params, jnp.asarray(step_value.T), phases
    )


def solution(mesh):
    placed = (P(("rows", "kern"), None), P("kern", None, None, None, None), P("rows", "kern"))
    return jax.shard_map(
        local, mesh=mesh, in_specs=placed, out_specs=P(("rows", "kern"), None), check_vma=False
    )
```

time: 144 us -> 126 us (0.88)
  starting transfers between devices: 23.5 us -> 0 us
  blocking collectives: 73.5 us -> 96.5 us
  waiting for transfers between devices: 7.84 us -> 0 us
  Pallas kernels: 31.9 us -> 26.3 us
  local copies, waits for them, and re-layouts: 6.16 us -> 1.99 us
    all_to_all x4 -> x6, blocking collectives: 73.5 us -> 96.5 us  [exchange(): return lax.all_to_all(values, axes, 0, 0, tiled=True)]
    ppermute x14 -> x0, starting transfers between devices: 19.4 us -> none  [shifted(): lax.ppermute(values, 'kern', [(place, (place + shift) % KERN) for place i...]
    ppermute x14 -> x0, waiting for transfers between devices: 7.84 us -> none  [shifted(): lax.ppermute(values, 'kern', [(place, (place + shift) % KERN) for place i...]
    pallas_call x2, Pallas kernels: 21.6 us -> 17.3 us  [the longest x1 8.94 us: mask_spectrum(): pl.pallas_call(spectrum_kernel, in_specs=[pl.BlockSpec(memory_space=pltpu...]
    unnamed x30 -> x10, local copies, waits for them, and re-layouts: 6.08 us -> 1.91 us
    all_to_all x1 -> x0, starting transfers between devices: 4.14 us -> none  [exchange(): return lax.all_to_all(values, axes, 0, 0, tiled=True)]
  transfers between devices with their start and end apart: 15 -> 0, of which waited for: 5 -> 0; matrix products, arithmetic and copies ran while one was open for 0% -> 0% of each run, Pallas kernels for 0% -> 0%
where the time goes in v3:
time: 126 us; the launch traced here: 125 us
  blocking collectives  96.5 us (77%)
  Pallas kernels  26.3 us (21%)
  local copies, waits for them, and re-layouts  1.99 us (2%)
    all_to_all x6, blocking collectives, exchange(): return lax.all_to_all(values, axes, 0, 0, tiled=True)  96.5 us
    pallas_call x1, Pallas kernels, mask_spectrum(): pl.pallas_call(spectrum_kernel, in_specs=[pl.BlockSpec(memory_space=pltpu...  8.94 us
    pallas_call x1, Pallas kernels, mask_update(): pl.pallas_call(update_kernel, in_specs=[vmem] + [hbm] * 5, out_specs=hbm,...  8.37 us
    pallas_call x1, Pallas kernels, coarse_adjoint(): pl.pallas_call(adjoint_kernel, grid=(KERN,), in_specs=[whole_spec(parts.s...  3.9 us
    pallas_call x1, Pallas kernels, coarse_fields(): pl.pallas_call(field_kernel, grid=(members,), in_specs=[whole_spec(tiles....  2.58 us

profile of v3, /device:TPU:1, one launch (start us, length us, event | category | flops | bytes accessed | tf_op | source)
XLA Modules:
  0.0 125.2 jit_solution(14621264676940074786)
XLA Ops:
  0.0 0.0 copy-start.2
  0.0 0.0 copy-start
  0.0 8.9 %mask_spectrum.1 = (bf16[128,8,128]{2,1,0:T(8,128)(2,1)}, bf16[256,512]{1,0:T(8,128)(2,1)}, bf16[256,512]{1,0:T(8,128)(2,1)}) custom-call(f32[128,16384]{1,0:T(8,128)} %mask_ref.3, bf16[256,256]{1,0:T(8,128)(2,1)} %constant.28.clone.step_ref, f32[64,256]{1,0:T(8,128)} %constant.22.clone.phase_ref, f32[128,512]{1,0:T(8,128)} %constant.23.clone.base_ref, ...), custom_call_target="tpu_custom_call" | custom-call | tf_op jit(solution)/shard_map/mask_spectrum/pallas_call | solution.py:256
  9.0 22.6 %all_to_all.30 = bf16[128,8,128]{2,1,0:T(8,128)(2,1)S(1)} all-to-all(bf16[128,8,128]{2,1,0:T(8,128)(2,1)} %get-tuple-element.10), channel_id=1, replica_groups=mesh['rows'=16,'kern'=8] {'rows','kern'}, dimensions={0} | all-to-all | bytes 524288 | tf_op jit(solution)/shard_map/all_to_all | solution.py:599
  31.5 0.1 reduce_sum.24
  31.7 0.0 copy-start.1
  31.7 15.0 %all_to_all.31.tiles_ref = bf16[128,8,128]{2,1,0:T(8,128)(2,1)S(1)} all-to-all(bf16[128,8,128]{2,1,0:T(8,128)(2,1)S(1)} %broadcast_in_dim.4), channel_id=1, replica_groups=mesh['rows'=16,'kern'=8] {'rows','kern'}, dimensions={0} | all-to-all | bytes 524288 | tf_op jit(solution)/shard_map/all_to_all | solution.py:599
  46.7 0.0 copy-done.2
  46.7 0.0 copy-done
  46.7 0.0 copy-start.3
  46.7 0.9 copy-done.3
  47.7 0.0 copy-start.4
  47.7 0.9 copy-done.4
  48.6 2.6 %coarse_fields.1 = (f32[2,512,1024]{2,1,0:T(8,128)S(1)}, bf16[8,3,32,512]{3,2,1,0:T(8,128)(2,1)S(1)}) custom-call(bf16[128,8,128]{2,1,0:T(8,128)(2,1)S(1)} %all_to_all.31.tiles_ref, f32[2,2,2,256,256]{4,3,2,1,0:T(8,128)S(1)} %copy-done, bf16[256,512]{1,0:T(8,128)(2,1)S(1)} %copy-done.4, bf16[256,512]{1,0:T(8,128)(2,1)S(1)} %copy-done.3, ...), custom_call_target="tpu_custom_call" | custom-call | tf_op jit(solution)/shard_map/coarse_fields/pallas_call | solution.py:336
  51.2 14.4 %all_to_all.32.parts_ref = bf16[8,3,32,512]{3,2,1,0:T(8,128)(2,1)S(1)} all-to-all(bf16[8,3,32,512]{3,2,1,0:T(8,128)(2,1)S(1)} %get-tuple-element.14), channel_id=1, replica_groups=mesh['rows'=16,'kern'=8] {'kern'}, dimensions={0} | all-to-all | bytes 1572864 | tf_op jit(solution)/shard_map/all_to_all | solution.py:599
  65.6 0.0 copy-done.1
  65.6 3.9 %coarse_adjoint.1 = bf16[8,2,32,512]{3,2,1,0:T(8,128)(2,1)S(1)} custom-call(bf16[8,3,32,512]{3,2,1,0:T(8,128)(2,1)S(1)} %all_to_all.32.parts_ref, bf16[512,4096]{1,0:T(8,128)(2,1)S(1)} %copy-done.1), custom_call_target="tpu_custom_call" | custom-call | tf_op jit(solution)/shard_map/coarse_adjoint/pallas_call | solution.py:398
  69.6 10.4 %all_to_all.33.adjoint_ref = bf16[8,2,32,512]{3,2,1,0:T(8,128)(2,1)S(1)} all-to-all(bf16[8,2,32,512]{3,2,1,0:T(8,128)(2,1)S(1)} %coarse_adjoint.1), channel_id=1, replica_groups=mesh['rows'=16,'kern'=8] {'kern'}, dimensions={0} | all-to-all | bytes 1048576 | tf_op jit(solution)/shard_map/all_to_all | solution.py:599
  80.0 2.5 %spectrum_gradient.1 = bf16[128,8,128]{2,1,0:T(8,128)(2,1)S(1)} custom-call(f32[2,512,1024]{2,1,0:T(8,128)S(1)} %get-tuple-element.13.field_ref, bf16[8,2,32,512]{3,2,1,0:T(8,128)(2,1)S(1)} %all_to_all.33.adjoint_ref, f32[2,2,2,256,256]{4,3,2,1,0:T(8,128)S(1)} %copy-done, bf16[256,512]{1,0:T(8,128)(2,1)S(1)} %copy-done.3, bf16[512,1024]{1,0:T(8,128)(2,1)S(1)} %copy-done.2), custom_call_target="tpu_custom_call" | custom-call | tf_op jit(solution)/shard_map/spectrum_gradient/pallas_call | solution.py:454
  82.5 18.7 %all_to_all.34 = bf16[128,8,128]{2,1,0:T(8,128)(2,1)S(1)} all-to-all(bf16[128,8,128]{2,1,0:T(8,128)(2,1)S(1)} %spectrum_gradient.1), channel_id=1, replica_groups=mesh['rows'=16,'kern'=8] {'rows','kern'}, dimensions={0} | all-to-all | bytes 524288 | tf_op jit(solution)/shard_map/all_to_all | solution.py:599
  101.1 0.1 reduce_sum.25
  101.3 15.4 %all_to_all.35.tiles_ref = bf16[128,8,128]{2,1,0:T(8,128)(2,1)} all-to-all(bf16[128,8,128]{2,1,0:T(8,128)(2,1)S(1)} %broadcast_in_dim.5), channel_id=1, replica_groups=mesh['rows'=16,'kern'=8] {'rows','kern'}, dimensions={0} | all-to-all | bytes 524288 | tf_op jit(solution)/shard_map/all_to_all | solution.py:599
  116.7 8.4 %mask_update.1 = f32[128,16384]{1,0:T(8,128)} custom-call(bf16[128,8,128]{2,1,0:T(8,128)(2,1)} %all_to_all.35.tiles_ref, f32[128,512]{1,0:T(8,128)} %constant.23.clone.base_ref, f32[128,1,512]{2,1,0:T(1,128)} %constant.24.clone.shift_ref, f32[128,16384]{1,0:T(8,128)} %mask_ref.3, bf16[256,256]{1,0:T(8,128)(2,1)} %constant.30.clone.step_ref, ...), custom_call_target="tpu_custom_call" | custom-call | tf_op jit(solution)/shard_map/mask_update/pallas_call | solution.py:573
  (2 shorter events, 0.1 us)
Async XLA Ops:
  0.0 46.7 %copy-start.2 = (bf16[512,1024]{1,0:T(8,128)(2,1)S(1)}, bf16[512,1024]{1,0:T(8,128)(2,1)}, u32[]{:S(2)}) copy-start(bf16[512,1024]{1,0:T(8,128)(2,1)} %constant.27.clone.map_ref) | copy-start | bytes 3145732
  0.0 46.7 %copy-start = (f32[2,2,2,256,256]{4,3,2,1,0:T(8,128)S(1)}, f32[2,2,2,256,256]{4,3,2,1,0:T(8,128)}, u32[]{:S(2)}) copy-start(f32[2,2,2,256,256]{4,3,2,1,0:T(8,128)} %pupil_ref.3) | copy-start | bytes 6291460
  31.7 34.0 %copy-start.1 = (bf16[512,4096]{1,0:T(8,128)(2,1)S(1)}, bf16[512,4096]{1,0:T(8,128)(2,1)}, u32[]{:S(2)}) copy-start(bf16[512,4096]{1,0:T(8,128)(2,1)} %constant.29.clone.matrix_ref) | copy-start | bytes 12582916
  46.7 1.0 copy-start.3
  47.7 0.9 copy-start.4

commit v4 on v3

--- a/solution.py
+++ b/solution.py
@@ -18,7 +18,7 @@
 ROWS = 16
 KERN = 8
 DEVICES = ROWS * KERN
-WIDTH = 2048
+WIDTH = 1024
 CHUNKS = MASK // WIDTH
 PER = WIDTH // STEP
 
@@ -29,7 +29,6 @@
 
 VMEM_LIMIT = 24 * 1024 * 1024
 STREAM_LIMIT = 56 * 1024 * 1024
-HIGHEST = lax.Precision.HIGHEST
 
 
 def tables(positions, period, count=BAND):
@@ -49,6 +48,12 @@
 def step_table():
     cosine, sine = tables(np.arange(STEP), MASK, HALF)
     return bfloat(np.concatenate([cosine, -sine], 1) / MASK)
+
+
+def row_transform(rows):
+    table = wide_table(np.arange(rows), MASK).T
+    high = bfloat(table)
+    return np.concatenate([high, bfloat(table - high.astype(np.float32))], 0)
 
 
 def coarse_map():
@@ -108,21 +113,11 @@
     return lax.broadcasted_iota(jnp.int32, shape, 0), lax.broadcasted_iota(jnp.int32, shape, 1)
 
 
-def row_mirror():
-    row, column = iotas((BAND, BAND))
-    return jnp.where(row + column == BAND, 1.0, 0.0).astype(jnp.bfloat16)
-
-
 def conjugate_mirror():
     row, column = iotas((BAND, BAND))
     real = (row + column == HALF) & (row < HALF) & (column > 0) & (column < HALF)
     imag = (row + column == 2 * HALF + HALF) & (row >= HALF) & (column > HALF)
     return (jnp.where(real, 1.0, 0.0) - jnp.where(imag, 1.0, 0.0)).astype(jnp.bfloat16)
-
-
-def diagonal():
-    row, column = iotas((BAND, BAND))
-    return row == column
 
 
 def store_tiles(out_ref, real, imag):
@@ -145,11 +140,12 @@
 
 def spectrum_kernel(
     mask_ref, step_ref, phase_ref, base_ref, shift_ref, grid_base_ref, grid_shift_ref, target_ref,
-    out_ref, rows_ref, wanted_ref,
+    out_ref, grid_ref,
     held_ref, steps_ref, phases_ref, bases_ref, shifts_ref, grid_bases_ref, grid_shifts_ref, targets_ref,
     stack_a, stack_b, product_a, product_b, re_ref, im_ref, flat_ref, sems,
 ):
     rows = mask_ref.shape[0]
+    grid_rows = target_ref.shape[0]
     stacks = (stack_a, stack_b)
     products = (product_a, product_b)
     chunks = [
@@ -172,18 +168,20 @@
     ]
     chunks[0].start()
     small[0].start()
+    small[1].start()
     chunks[1].start()
-    for copy in small[1:] + chunks[2:]:
+    for copy in small[2:5] + chunks[2:] + small[5:]:
         copy.start()
 
     def transmit(i):
         chunks[i].wait()
-        total = jnp.zeros((rows, HALF), jnp.float32)
+        total = None
         for part in range(PER):
             value = jnp.tanh(held_ref[i, :, part * STEP : (part + 1) * STEP]).astype(jnp.bfloat16)
             stacks[i % 2][part * rows : (part + 1) * rows] = value
             wide = value.astype(jnp.float32)
-            total = total + (wide[:, :HALF] + wide[:, HALF:])
+            both = wide[:, :HALF] + wide[:, HALF:]
+            total = both if part == 0 else total + both
         flat_ref[...] = total if i == 0 else flat_ref[...] + total
 
     def gather(i):
@@ -214,38 +212,43 @@
             transmit(i + 1)
         if i > 0:
             gather(i - 1)
+        if i == 1:
+            for copy in small[2:5]:
+                copy.wait()
+            cosine, sine = turned_table(grid_bases_ref[...], grid_shifts_ref[...])
+            grid_ref[:grid_rows, :BAND] = cosine.astype(jnp.bfloat16)
+            grid_ref[:grid_rows, BAND:] = sine.astype(jnp.bfloat16)
+            grid_ref[grid_rows:] = targets_ref[...].astype(jnp.float32).astype(jnp.bfloat16)
     gather(CHUNKS - 1)
-    for copy in small[2:]:
+    for copy in small[5:]:
         copy.wait()
-    cosine, sine = turned_table(grid_bases_ref[...], grid_shifts_ref[...])
-    rows_ref[:, :BAND] = cosine.astype(jnp.bfloat16)
-    rows_ref[:, BAND:] = sine.astype(jnp.bfloat16)
-    wanted_ref[...] = targets_ref[...].astype(jnp.float32).astype(jnp.bfloat16)
-    table = jnp.concatenate(turned_table(bases_ref[...], shifts_ref[...]), 1)
-    product = dot_first(table, jnp.concatenate([re_ref[...], im_ref[...]], 1), HIGHEST)
+    _, lane = iotas((rows, HALF))
+    mirror = conjugate_mirror()
+    half_high, half_low = split(jnp.concatenate([re_ref[...], im_ref[...]], 1))
+    other = float_dot(half_high, mirror) + float_dot(half_low, mirror)
+    centre = jnp.sum(flat_ref[...], 1, keepdims=True) * (1.0 / MASK)
+    other_high, other_low = split(
+        jnp.concatenate([jnp.where(lane == 0, centre, other[:, :HALF]), other[:, HALF:]], 1)
+    )
+    high = jnp.concatenate([half_high, other_high], 1)
+    low = jnp.concatenate([half_low, other_low], 1)
+    product = float_dot(bases_ref[...], high)
+    product = product[: 2 * BAND] + (product[2 * BAND :] + float_dot(bases_ref[: 2 * BAND], low))
+    diagonal = jnp.equal(*iotas((BAND, BAND)))
+    turn_cos, turn_sin = [
+        jnp.sum(jnp.where(diagonal, shifts_ref[:, part * BAND : (part + 1) * BAND], 0.0), 1, keepdims=True)
+        for part in range(2)
+    ]
     by_cos = product[:BAND]
     by_sin = product[BAND:]
-    half_re = by_cos[:, :HALF] + by_sin[:, HALF:]
-    half_im = by_cos[:, HALF:] - by_sin[:, :HALF]
-    beyond_re = by_cos[:1, :HALF] - by_sin[:1, HALF:]
-    beyond_im = by_cos[:1, HALF:] + by_sin[:1, :HALF]
-    centre = jnp.sum(dot_first(flat_ref[...], table, HIGHEST), 0, keepdims=True) * (1.0 / MASK)
-    mirror = conjugate_mirror()
-    flip = row_mirror()
-    row, column = iotas((BAND, HALF))
-    whole = jnp.concatenate([half_re, half_im], 1)
-    ends = jnp.concatenate([beyond_re, beyond_im], 1)
-    other = 0.0
-    for piece, end in zip(split(whole), split(jnp.concatenate([ends] * 8, 0))):
-        turned = float_dot(flip, float_dot(piece, mirror).astype(jnp.bfloat16))
-        other = other + jnp.where(iotas((BAND, BAND))[0] == 0, float_dot(end, mirror)[:1], turned)
-    parts = []
-    for part, value in enumerate((centre[:, :BAND], -centre[:, BAND:])):
-        line = jnp.sum(jnp.where(diagonal(), value, 0.0), 1, keepdims=True)
-        parts.append(jnp.where(column == 0, line, other[:, part * HALF : (part + 1) * HALF]))
-    store_tiles(
-        out_ref, jnp.concatenate([half_re, parts[0]], 1), jnp.concatenate([half_im, parts[1]], 1)
-    )
+    real = []
+    imag = []
+    for at in (0, 2 * HALF):
+        part_re = by_cos[:, at : at + HALF] + by_sin[:, at + HALF : at + 2 * HALF]
+        part_im = by_cos[:, at + HALF : at + 2 * HALF] - by_sin[:, at : at + HALF]
+        real.append(turn_cos * part_re + turn_sin * part_im)
+        imag.append(turn_cos * part_im - turn_sin * part_re)
+    store_tiles(out_ref, jnp.concatenate(real, 1), jnp.concatenate(imag, 1))
 
 
 def mask_spectrum(mask_params, step_value, phases, base, shifts, grid_base, grid_shifts, target):
@@ -256,17 +259,16 @@
     return pl.pallas_call(
         spectrum_kernel,
         in_specs=[pl.BlockSpec(memory_space=pltpu.HBM)] * len(arguments),
-        out_specs=[pl.BlockSpec(memory_space=pltpu.VMEM)] * 3,
+        out_specs=[pl.BlockSpec(memory_space=pltpu.VMEM)] * 2,
         out_shape=[
             jax.ShapeDtypeStruct((DEVICES, 8, 128), jnp.bfloat16),
-            jax.ShapeDtypeStruct((grid_rows, 2 * BAND), jnp.bfloat16),
-            jax.ShapeDtypeStruct(target.shape, jnp.bfloat16),
+            jax.ShapeDtypeStruct((2 * grid_rows, 2 * BAND), jnp.bfloat16),
         ],
         scratch_shapes=[
             pltpu.VMEM((CHUNKS, rows, WIDTH), jnp.float32),
             pltpu.VMEM(step_value.shape, jnp.bfloat16),
             pltpu.VMEM(phases.shape, jnp.float32),
-            pltpu.VMEM(base.shape, jnp.float32),
+            pltpu.VMEM(base.shape, jnp.bfloat16),
             pltpu.VMEM((1, 2 * BAND), jnp.float32),
             pltpu.VMEM(grid_base.shape, jnp.float32),
             pltpu.VMEM((1, 2 * BAND), jnp.float32),
@@ -286,18 +288,18 @@
 
 
 def field_kernel(
-    tiles_ref, pupil_ref, wanted_ref, rows_ref, map_ref, field_ref, power_ref,
+    tiles_ref, pupil_ref, grid_ref, map_ref, field_ref, power_ref,
     spec_ref, partial_ref, sum_ref,
 ):
     index = pl.program_id(0)
-    rows = wanted_ref.shape[0]
+    rows = grid_ref.shape[0] // 2
     slab = rows // KERN
 
     @pl.when(index == 0)
     def _():
         load_tiles(tiles_ref, spec_ref)
         for owner in range(KERN):
-            power_ref[owner, 2] = wanted_ref[owner * slab : (owner + 1) * slab]
+            power_ref[owner, 2] = grid_ref[rows + owner * slab : rows + (owner + 1) * slab]
 
     spec_re = spec_ref[0]
     spec_im = spec_ref[1]
@@ -309,7 +311,7 @@
         block = jnp.concatenate(
             [jnp.concatenate([amp_re, amp_im], 1), jnp.concatenate([-amp_im, amp_re], 1)], 0
         )
-        partial_ref[corner * rows : (corner + 1) * rows] = float_dot(rows_ref[...], block).astype(
+        partial_ref[corner * rows : (corner + 1) * rows] = float_dot(grid_ref[:rows], block).astype(
             jnp.bfloat16
         )
     field_ref[0] = float_dot(partial_ref[...], map_ref[...])
@@ -330,17 +332,16 @@
                 power_ref[owner, corner] = (sum_ref[at : at + slab] + power).astype(jnp.bfloat16)
 
 
-def coarse_fields(tiles, pupils, wanted, rows_table, column_map):
+def coarse_fields(tiles, pupils, grid_table, column_map):
     members = pupils.shape[0]
-    rows = wanted.shape[0]
+    rows = grid_table.shape[0] // 2
     return pl.pallas_call(
         field_kernel,
         grid=(members,),
         in_specs=[
             whole_spec(tiles.shape),
             pl.BlockSpec((1, 2, 2, BAND, BAND), lambda i: (i, 0, 0, 0, 0)),
-            whole_spec(wanted.shape),
-            whole_spec(rows_table.shape),
+            whole_spec(grid_table.shape),
             whole_spec(column_map.shape),
         ],
         out_specs=[
@@ -358,63 +359,52 @@
         ],
         compiler_params=params(),
         name="coarse_fields",
-    )(tiles, pupils, wanted, rows_table, column_map)
-
-
-def adjoint_kernel(parts_ref, matrix_ref, out_ref, power_ref, acc_ref):
-    index = pl.program_id(0)
+    )(tiles, pupils, grid_table, column_map)
+
+
+def adjoint_kernel(parts_ref, matrix_ref, out_ref):
     rows = parts_ref.shape[2]
-
-    @pl.when(index == 0)
-    def _():
+    width = GRID // KERN
+    powers = []
+    for corner in range(2):
+        total = parts_ref[0, corner].astype(jnp.float32)
+        for owner in range(1, KERN):
+            total = total + parts_ref[owner, corner].astype(jnp.float32)
+        powers.append(total.astype(jnp.bfloat16))
+    power = jnp.concatenate(powers, 0)
+    folded = None
+    for slab in range(KERN):
+        columns = slice(slab * width, (slab + 1) * width)
+        fine = float_dot(power, matrix_ref[:, columns])
+        wanted = parts_ref[slab, 2].astype(jnp.float32)
+        corners = []
         for corner in range(2):
-            total = parts_ref[0, corner].astype(jnp.float32)
-            for owner in range(1, KERN):
-                total = total + parts_ref[owner, corner].astype(jnp.float32)
-            power_ref[corner * rows : (corner + 1) * rows] = total.astype(jnp.bfloat16)
-        acc_ref[...] = jnp.zeros_like(acc_ref)
-
-    fine = float_dot(power_ref[...], matrix_ref[...])
-    wanted = parts_ref[index, 2].astype(jnp.float32)
-    corners = []
-    for corner in range(2):
-        dose = dose_levels[corner]
-        resist = jax.nn.sigmoid(steepness * (dose * fine[corner * rows : (corner + 1) * rows] - threshold))
-        corners.append(
-            (2.0 * (resist - wanted) * resist * (1.0 - resist) * steepness * dose).astype(jnp.bfloat16)
-        )
-    acc_ref[...] += dot_last(jnp.concatenate(corners, 0), matrix_ref[...])
-
-    @pl.when(index == pl.num_programs(0) - 1)
-    def _():
-        folded = acc_ref[...].reshape(2, rows, COARSE).astype(jnp.bfloat16)
-        for owner in range(KERN):
-            out_ref[owner] = folded
+            dose = dose_levels[corner]
+            resist = jax.nn.sigmoid(steepness * (dose * fine[corner * rows : (corner + 1) * rows] - threshold))
+            corners.append(
+                (2.0 * (resist - wanted) * resist * (1.0 - resist) * steepness * dose).astype(jnp.bfloat16)
+            )
+        term = dot_last(jnp.concatenate(corners, 0), matrix_ref[:, columns])
+        folded = term if slab == 0 else folded + term
+    folded = folded.reshape(2, rows, COARSE).astype(jnp.bfloat16)
+    for owner in range(KERN):
+        out_ref[owner] = folded
 
 
 def coarse_adjoint(parts, matrix):
     rows = parts.shape[2]
-    width = GRID // KERN
     return pl.pallas_call(
         adjoint_kernel,
-        grid=(KERN,),
-        in_specs=[
-            whole_spec(parts.shape),
-            pl.BlockSpec((COARSE, width), lambda i: (0, i)),
-        ],
-        out_specs=whole_spec((KERN, 2, rows, COARSE)),
+        in_specs=[pl.BlockSpec(memory_space=pltpu.VMEM)] * 2,
+        out_specs=pl.BlockSpec(memory_space=pltpu.VMEM),
         out_shape=jax.ShapeDtypeStruct((KERN, 2, rows, COARSE), jnp.bfloat16),
-        scratch_shapes=[
-            pltpu.VMEM((2 * rows, COARSE), jnp.bfloat16),
-            pltpu.VMEM((2 * rows, COARSE), jnp.float32),
-        ],
         compiler_params=params(),
         name="coarse_adjoint",
     )(parts, matrix)
 
 
 def gradient_kernel(
-    field_ref, adjoint_ref, pupil_ref, rows_ref, map_ref, out_ref, weighted_ref, back_ref, acc_ref
+    field_ref, adjoint_ref, pupil_ref, grid_ref, map_ref, out_ref, weighted_ref, back_ref, acc_ref
 ):
     index = pl.program_id(0)
     slab = adjoint_ref.shape[2]
@@ -435,7 +425,7 @@
                 )
     back_ref[...] = dot_last(weighted_ref[...], map_ref[...]).astype(jnp.bfloat16)
     for corner in range(2):
-        grads = dot_first(rows_ref[...], back_ref[corner * rows : (corner + 1) * rows])
+        grads = dot_first(grid_ref[:rows], back_ref[corner * rows : (corner + 1) * rows])
         grad_re = grads[:BAND, :BAND] + grads[BAND:, BAND:]
         grad_im = grads[:BAND, BAND:] - grads[BAND:, :BAND]
         kernel_re = pupil_ref[0, corner, 0]
@@ -448,9 +438,9 @@
         store_tiles(out_ref, acc_ref[0], acc_ref[1])
 
 
-def spectrum_gradient(fields, adjoint, pupils, rows_table, column_map):
+def spectrum_gradient(fields, adjoint, pupils, grid_table, column_map):
     members = pupils.shape[0]
-    rows = rows_table.shape[0]
+    rows = grid_table.shape[0] // 2
     return pl.pallas_call(
         gradient_kernel,
         grid=(members,),
@@ -458,7 +448,7 @@
             pl.BlockSpec((1, 2 * rows, 2 * COARSE), lambda i: (i, 0, 0)),
             whole_spec(adjoint.shape),
             pl.BlockSpec((1, 2, 2, BAND, BAND), lambda i: (i, 0, 0, 0, 0)),
-            whole_spec(rows_table.shape),
+            whole_spec(grid_table.shape),
             whole_spec(column_map.shape),
         ],
         out_specs=whole_spec((DEVICES, 8, 128)),
@@ -470,7 +460,7 @@
         ],
         compiler_params=params(),
         name="spectrum_gradient",
-    )(fields, adjoint, pupils, rows_table, column_map)
+    )(fields, adjoint, pupils, grid_table, column_map)
 
 
 def update_kernel(
@@ -503,30 +493,21 @@
         copy.start()
 
     load_tiles(tiles_ref, spec_ref)
-    left = jnp.concatenate([spec_ref[0, :, :HALF], spec_ref[1, :, :HALF]], 1)
-    right = jnp.concatenate([spec_ref[0, :, HALF:], spec_ref[1, :, HALF:]], 1)
-    turned = float_dot(right.astype(jnp.bfloat16), conjugate_mirror())
-    half = split(left + float_dot(row_mirror(), turned.astype(jnp.bfloat16)))
-    beyond_re = turned[:1, :HALF]
-    beyond_im = turned[:1, HALF:]
-    centres = [
-        jnp.sum(jnp.where(diagonal(), spec_ref[part, :, HALF : HALF + 1], 0.0), 0, keepdims=True)
-        for part in range(2)
-    ]
+    gradient = jnp.concatenate([spec_ref[0], spec_ref[1]], 1).astype(jnp.bfloat16)
     small[0].wait()
     small[1].wait()
     cosine, sine = turned_table(bases_ref[...], shifts_ref[...])
-    high_cos, low_cos = split(cosine)
-    high_sin, low_sin = split(sine)
-    product = float_dot(jnp.concatenate([high_cos, low_cos, high_sin, low_sin], 0), half[0])
-    rest = float_dot(jnp.concatenate([high_cos, high_sin], 0), half[1])
-    by_cos = product[:rows] + (product[rows : 2 * rows] + rest[:rows])
-    by_sin = product[2 * rows : 3 * rows] + (product[3 * rows :] + rest[rows:])
-    edge_cos = cosine[:, :1]
-    edge_sin = -sine[:, :1]
-    re_ref[...] = by_cos[:, :HALF] - by_sin[:, HALF:] + (edge_cos * beyond_re - edge_sin * beyond_im)
-    im_ref[...] = by_sin[:, :HALF] + by_cos[:, HALF:] + (edge_sin * beyond_re + edge_cos * beyond_im)
-    centre = jnp.sum(cosine * centres[0] - sine * centres[1], 1, keepdims=True) * (1.0 / MASK)
+    product = float_dot(jnp.concatenate(split(cosine) + split(sine), 0), gradient)
+    by_cos = product[:rows] + product[rows : 2 * rows]
+    by_sin = product[2 * rows : 3 * rows] + product[3 * rows :]
+    col_re = by_cos[:, :BAND] - by_sin[:, BAND:]
+    col_im = by_sin[:, :BAND] + by_cos[:, BAND:]
+    centre = col_re[:, HALF : HALF + 1] * (1.0 / MASK)
+    mirror = conjugate_mirror()
+    high, low = split(jnp.concatenate([col_re[:, HALF:], col_im[:, HALF:]], 1))
+    other = float_dot(high, mirror) + float_dot(low, mirror)
+    re_ref[...] = col_re[:, :HALF] + other[:, :HALF]
+    im_ref[...] = col_im[:, :HALF] + other[:, HALF:]
 
     def turn(i):
         piece = 32
@@ -615,17 +596,18 @@
     step_value = step_table()
     phases = jnp.asarray(wide_table(np.arange(STEPS) * STEP, MASK, HALF))
     mask_base = jnp.asarray(wide_table(np.arange(rows), MASK))
+    mask_transform = jnp.asarray(row_transform(rows))
     mask_shifts = jnp.asarray(wide_table(np.arange(ROWS * KERN) * rows, MASK)[:, None, :])
     grid_base = jnp.asarray(wide_table(np.arange(grid_rows), GRID))
     grid_shifts = jnp.asarray(wide_table(np.arange(ROWS) * grid_rows, GRID)[:, None, :])
     column_map = jnp.asarray(coarse_map())
 
-    tiles, rows_table, wanted = mask_spectrum(
-        mask_params, jnp.asarray(step_value), phases, mask_base, mask_shifts, grid_base, grid_shifts, target_pattern
+    tiles, grid_table = mask_spectrum(
+        mask_params, jnp.asarray(step_value), phases, mask_transform, mask_shifts, grid_base, grid_shifts, target_pattern
     )
-    fields, powers = coarse_fields(sum_tiles(tiles), pupil_kernels, wanted, rows_table, column_map)
+    fields, powers = coarse_fields(sum_tiles(tiles), pupil_kernels, grid_table, column_map)
     adjoint = coarse_adjoint(exchange(powers, "kern"), jnp.asarray(interpolation()))
-    gradient = spectrum_gradient(fields, exchange(adjoint, "kern"), pupil_kernels, rows_table, column_map)
+    gradient = spectrum_gradient(fields, exchange(adjoint, "kern"), pupil_kernels, grid_table, column_map)
     return mask_update(
         sum_tiles(gradient), mask_base, mask_shifts, mask_params, jnp.asarray(step_value.T), phases
     )

time: 126 us -> 124 us (0.984)
    pallas_call x1, Pallas kernels: 3.9 us -> 2.61 us  [coarse_adjoint(): pl.pallas_call(adjoint_kernel, in_specs=[pl.BlockSpec(memory_space=pltpu....]
where the time goes in v4:
time: 124 us
  blocking collectives  96.5 us (78%)
  Pallas kernels  25.5 us (21%)
    all_to_all x6, blocking collectives, exchange(): return lax.all_to_all(values, axes, 0, 0, tiled=True)  96.5 us
    pallas_call x1, Pallas kernels, mask_update(): pl.pallas_call(update_kernel, in_specs=[vmem] + [hbm] * 5, out_specs=hbm,...  9.08 us
    pallas_call x1, Pallas kernels, mask_spectrum(): pl.pallas_call(spectrum_kernel, in_specs=[pl.BlockSpec(memory_space=pltpu...  8.72 us
    pallas_call x1, Pallas kernels, coarse_adjoint(): pl.pallas_call(adjoint_kernel, in_specs=[pl.BlockSpec(memory_space=pltpu....  2.61 us
    pallas_call x1, Pallas kernels, coarse_fields(): pl.pallas_call(field_kernel, grid=(members,), in_specs=[whole_spec(tiles....  2.58 us
    pallas_call x1, Pallas kernels, spectrum_gradient(): pl.pallas_call(gradient_kernel, grid=(members,), in_specs=[pl.BlockSpec((...  2.5 us

profile of v4, /device:TPU:1, one launch (start us, length us, event | category | flops | bytes accessed | tf_op | source)
XLA Modules:
  0.0 123.6 jit_solution(15405037887699036443)
XLA Ops:
  0.0 0.0 copy-start.2
  0.0 0.0 copy-start
  0.0 8.7 %mask_spectrum.1 = (bf16[128,8,128]{2,1,0:T(8,128)(2,1)}, bf16[512,512]{1,0:T(8,128)(2,1)}) custom-call(f32[128,16384]{1,0:T(8,128)} %mask_ref.3, bf16[256,256]{1,0:T(8,128)(2,1)} %constant.31.clone.step_ref, f32[64,256]{1,0:T(8,128)} %constant.24.clone.phase_ref, bf16[1024,128]{1,0:T(8,128)(2,1)} %constant.26.clone.base_ref, ...), custom_call_target="tpu_custom_call" | custom-call | tf_op jit(solution)/shard_map/mask_spectrum/pallas_call | solution.py:259
  8.7 22.6 %all_to_all.30 = bf16[128,8,128]{2,1,0:T(8,128)(2,1)S(1)} all-to-all(bf16[128,8,128]{2,1,0:T(8,128)(2,1)} %get-tuple-element.9), channel_id=1, replica_groups=mesh['rows'=16,'kern'=8] {'rows','kern'}, dimensions={0} | all-to-all | bytes 524288 | tf_op jit(solution)/shard_map/all_to_all | solution.py:580
  31.3 0.1 reduce_sum.24
  31.4 0.0 copy-start.1
  31.5 15.0 %all_to_all.31.tiles_ref = bf16[128,8,128]{2,1,0:T(8,128)(2,1)S(1)} all-to-all(bf16[128,8,128]{2,1,0:T(8,128)(2,1)S(1)} %broadcast_in_dim.4), channel_id=1, replica_groups=mesh['rows'=16,'kern'=8] {'rows','kern'}, dimensions={0} | all-to-all | bytes 524288 | tf_op jit(solution)/shard_map/all_to_all | solution.py:580
  46.5 0.0 copy-done.2
  46.5 0.0 copy-done
  46.5 0.0 copy-start.3
  46.5 1.0 copy-done.3
  47.5 2.6 %coarse_fields.1 = (f32[2,512,1024]{2,1,0:T(8,128)S(1)}, bf16[8,3,32,512]{3,2,1,0:T(8,128)(2,1)S(1)}) custom-call(bf16[128,8,128]{2,1,0:T(8,128)(2,1)S(1)} %all_to_all.31.tiles_ref, f32[2,2,2,256,256]{4,3,2,1,0:T(8,128)S(1)} %copy-done, bf16[512,512]{1,0:T(8,128)(2,1)S(1)} %copy-done.3, bf16[512,1024]{1,0:T(8,128)(2,1)S(1)} %copy-done.2), custom_call_target="tpu_custom_call" | custom-call | tf_op jit(solution)/shard_map/coarse_fields/pallas_call | solution.py:338
  50.1 14.4 %all_to_all.32.parts_ref = bf16[8,3,32,512]{3,2,1,0:T(8,128)(2,1)S(1)} all-to-all(bf16[8,3,32,512]{3,2,1,0:T(8,128)(2,1)S(1)} %get-tuple-element.12), channel_id=1, replica_groups=mesh['rows'=16,'kern'=8] {'kern'}, dimensions={0} | all-to-all | bytes 1572864 | tf_op jit(solution)/shard_map/all_to_all | solution.py:580
  64.6 0.0 copy-done.1
  64.6 2.6 %coarse_adjoint.1 = bf16[8,2,32,512]{3,2,1,0:T(8,128)(2,1)S(1)} custom-call(bf16[8,3,32,512]{3,2,1,0:T(8,128)(2,1)S(1)} %all_to_all.32.parts_ref, bf16[512,4096]{1,0:T(8,128)(2,1)S(1)} %copy-done.1), custom_call_target="tpu_custom_call" | custom-call | tf_op jit(solution)/shard_map/coarse_adjoint/pallas_call | solution.py:396
  67.2 10.4 %all_to_all.33.adjoint_ref = bf16[8,2,32,512]{3,2,1,0:T(8,128)(2,1)S(1)} all-to-all(bf16[8,2,32,512]{3,2,1,0:T(8,128)(2,1)S(1)} %coarse_adjoint.1), channel_id=1, replica_groups=mesh['rows'=16,'kern'=8] {'kern'}, dimensions={0} | all-to-all | bytes 1048576 | tf_op jit(solution)/shard_map/all_to_all | solution.py:580
  77.6 2.5 %spectrum_gradient.1 = bf16[128,8,128]{2,1,0:T(8,128)(2,1)S(1)} custom-call(f32[2,512,1024]{2,1,0:T(8,128)S(1)} %get-tuple-element.11.field_ref, bf16[8,2,32,512]{3,2,1,0:T(8,128)(2,1)S(1)} %all_to_all.33.adjoint_ref, f32[2,2,2,256,256]{4,3,2,1,0:T(8,128)S(1)} %copy-done, bf16[512,512]{1,0:T(8,128)(2,1)S(1)} %copy-done.3, bf16[512,1024]{1,0:T(8,128)(2,1)S(1)} %copy-done.2), custom_call_target="tpu_custom_call" | custom-call | tf_op jit(solution)/shard_map/spectrum_gradient/pallas_call | solution.py:444
  80.1 18.7 %all_to_all.34 = bf16[128,8,128]{2,1,0:T(8,128)(2,1)S(1)} all-to-all(bf16[128,8,128]{2,1,0:T(8,128)(2,1)S(1)} %spectrum_gradient.1), channel_id=1, replica_groups=mesh['rows'=16,'kern'=8] {'rows','kern'}, dimensions={0} | all-to-all | bytes 524288 | tf_op jit(solution)/shard_map/all_to_all | solution.py:580
  98.8 0.1 reduce_sum.25
  98.9 15.4 %all_to_all.35.tiles_ref = bf16[128,8,128]{2,1,0:T(8,128)(2,1)} all-to-all(bf16[128,8,128]{2,1,0:T(8,128)(2,1)S(1)} %broadcast_in_dim.5), channel_id=1, replica_groups=mesh['rows'=16,'kern'=8] {'rows','kern'}, dimensions={0} | all-to-all | bytes 524288 | tf_op jit(solution)/shard_map/all_to_all | solution.py:580
  114.4 9.1 %mask_update.1 = f32[128,16384]{1,0:T(8,128)} custom-call(bf16[128,8,128]{2,1,0:T(8,128)(2,1)} %all_to_all.35.tiles_ref, f32[128,512]{1,0:T(8,128)} %constant.25.clone.base_ref, f32[128,1,512]{2,1,0:T(1,128)} %constant.27.clone.shift_ref, f32[128,16384]{1,0:T(8,128)} %mask_ref.3, bf16[256,256]{1,0:T(8,128)(2,1)} %constant.33.clone.step_ref, ...), custom_call_target="tpu_custom_call" | custom-call | tf_op jit(solution)/shard_map/mask_update/pallas_call | solution.py:554
  (2 shorter events, 0.1 us)
Async XLA Ops:
  0.0 46.5 %copy-start.2 = (bf16[512,1024]{1,0:T(8,128)(2,1)S(1)}, bf16[512,1024]{1,0:T(8,128)(2,1)}, u32[]{:S(2)}) copy-start(bf16[512,1024]{1,0:T(8,128)(2,1)} %constant.30.clone.map_ref) | copy-start | bytes 3145732
  0.0 46.5 %copy-start = (f32[2,2,2,256,256]{4,3,2,1,0:T(8,128)S(1)}, f32[2,2,2,256,256]{4,3,2,1,0:T(8,128)}, u32[]{:S(2)}) copy-start(f32[2,2,2,256,256]{4,3,2,1,0:T(8,128)} %pupil_ref.3) | copy-start | bytes 6291460
  31.4 33.1 %copy-start.1 = (bf16[512,4096]{1,0:T(8,128)(2,1)S(1)}, bf16[512,4096]{1,0:T(8,128)(2,1)}, u32[]{:S(2)}) copy-start(bf16[512,4096]{1,0:T(8,128)(2,1)} %constant.32.clone.matrix_ref) | copy-start | bytes 12582916
  46.5 1.0 copy-start.3

commit v5 on v4

--- a/solution.py
+++ b/solution.py
@@ -18,9 +18,7 @@
 ROWS = 16
 KERN = 8
 DEVICES = ROWS * KERN
-WIDTH = 1024
-CHUNKS = MASK // WIDTH
-PER = WIDTH // STEP
+CHUNK = 16
 
 steepness = 4.0
 threshold = 0.75
@@ -82,10 +80,6 @@
     return cosine, sine
 
 
-def whole_spec(shape):
-    return pl.BlockSpec(shape, lambda i: (0,) * len(shape))
-
-
 def params(limit=VMEM_LIMIT):
     return pltpu.CompilerParams(vmem_limit_bytes=limit)
 
@@ -140,20 +134,21 @@
 
 def spectrum_kernel(
     mask_ref, step_ref, phase_ref, base_ref, shift_ref, grid_base_ref, grid_shift_ref, target_ref,
-    out_ref, grid_ref,
-    held_ref, steps_ref, phases_ref, bases_ref, shifts_ref, grid_bases_ref, grid_shifts_ref, targets_ref,
+    out_ref, grid_out_ref,
+    grid_ref, held_ref, steps_ref, phases_ref, bases_ref, shifts_ref, grid_bases_ref, grid_shifts_ref, targets_ref,
     stack_a, stack_b, product_a, product_b, re_ref, im_ref, flat_ref, sems,
 ):
     rows = mask_ref.shape[0]
     grid_rows = target_ref.shape[0]
     stacks = (stack_a, stack_b)
     products = (product_a, product_b)
+    count = rows // CHUNK
+    places = [pl.ds(i * CHUNK, CHUNK) for i in range(count)]
     chunks = [
-        pltpu.make_async_copy(mask_ref.at[:, pl.ds(i * WIDTH, WIDTH)], held_ref.at[i], sems.at[i])
-        for i in range(CHUNKS)
+        pltpu.make_async_copy(mask_ref.at[places[i]], held_ref.at[places[i]], sems.at[i]) for i in range(count)
     ]
     small = [
-        pltpu.make_async_copy(source, target, sems.at[CHUNKS + i])
+        pltpu.make_async_copy(source, target, sems.at[count + i])
         for i, (source, target) in enumerate(
             (
                 (step_ref, steps_ref),
@@ -166,6 +161,7 @@
             )
         )
     ]
+    grid_copy = pltpu.make_async_copy(grid_ref, grid_out_ref, sems.at[count + 7])
     chunks[0].start()
     small[0].start()
     small[1].start()
@@ -176,39 +172,35 @@
     def transmit(i):
         chunks[i].wait()
         total = None
-        for part in range(PER):
-            value = jnp.tanh(held_ref[i, :, part * STEP : (part + 1) * STEP]).astype(jnp.bfloat16)
-            stacks[i % 2][part * rows : (part + 1) * rows] = value
+        for step in range(STEPS):
+            value = jnp.tanh(held_ref[places[i], step * STEP : (step + 1) * STEP]).astype(jnp.bfloat16)
+            stacks[i % 2][step * CHUNK : (step + 1) * CHUNK] = value
             wide = value.astype(jnp.float32)
             both = wide[:, :HALF] + wide[:, HALF:]
-            total = both if part == 0 else total + both
-        flat_ref[...] = total if i == 0 else flat_ref[...] + total
+            total = both if step == 0 else total + both
+        flat_ref[places[i]] = total
 
     def gather(i):
-        piece = 32
-        for start in range(0, rows, piece):
-            total_re = None
-            for part in range(PER):
-                at = part * rows + start
-                step = i * PER + part
-                cosine = phases_ref[step : step + 1, :HALF]
-                sine = phases_ref[step : step + 1, HALF:]
-                first = products[i % 2][at : at + piece, :HALF]
-                second = products[i % 2][at : at + piece, HALF:]
-                turned_re = first * cosine + second * sine
-                turned_im = second * cosine - first * sine
-                total_re = turned_re if part == 0 else total_re + turned_re
-                total_im = turned_im if part == 0 else total_im + turned_im
-            here = slice(start, start + piece)
-            re_ref[here] = total_re if i == 0 else re_ref[here] + total_re
-            im_ref[here] = total_im if i == 0 else im_ref[here] + total_im
+        totals = [None] * 4
+        for step in range(STEPS):
+            cosine = phases_ref[step : step + 1, :HALF]
+            sine = phases_ref[step : step + 1, HALF:]
+            first = products[i % 2][step * CHUNK : (step + 1) * CHUNK, :HALF]
+            second = products[i % 2][step * CHUNK : (step + 1) * CHUNK, HALF:]
+            at = 2 * (step % 2)
+            for part, turned in enumerate(
+                (first * cosine + second * sine, second * cosine - first * sine)
+            ):
+                totals[at + part] = turned if step < 2 else totals[at + part] + turned
+        re_ref[places[i]] = totals[0] + totals[2]
+        im_ref[places[i]] = totals[1] + totals[3]
 
     transmit(0)
     small[0].wait()
     small[1].wait()
-    for i in range(CHUNKS):
+    for i in range(count):
         products[i % 2][...] = float_dot(stacks[i % 2][...], steps_ref[...])
-        if i + 1 < CHUNKS:
+        if i + 1 < count:
             transmit(i + 1)
         if i > 0:
             gather(i - 1)
@@ -219,7 +211,8 @@
             grid_ref[:grid_rows, :BAND] = cosine.astype(jnp.bfloat16)
             grid_ref[:grid_rows, BAND:] = sine.astype(jnp.bfloat16)
             grid_ref[grid_rows:] = targets_ref[...].astype(jnp.float32).astype(jnp.bfloat16)
-    gather(CHUNKS - 1)
+            grid_copy.start()
+    gather(count - 1)
     for copy in small[5:]:
         copy.wait()
     _, lane = iotas((rows, HALF))
@@ -249,23 +242,25 @@
         real.append(turn_cos * part_re + turn_sin * part_im)
         imag.append(turn_cos * part_im - turn_sin * part_re)
     store_tiles(out_ref, jnp.concatenate(real, 1), jnp.concatenate(imag, 1))
+    grid_copy.wait()
 
 
 def mask_spectrum(mask_params, step_value, phases, base, shifts, grid_base, grid_shifts, target):
     rows = mask_params.shape[0]
-    stacked = rows * PER
+    stacked = STEPS * CHUNK
     arguments = (mask_params, step_value, phases, base, shifts, grid_base, grid_shifts, target)
     grid_rows = grid_base.shape[0]
     return pl.pallas_call(
         spectrum_kernel,
         in_specs=[pl.BlockSpec(memory_space=pltpu.HBM)] * len(arguments),
-        out_specs=[pl.BlockSpec(memory_space=pltpu.VMEM)] * 2,
+        out_specs=[pl.BlockSpec(memory_space=pltpu.VMEM), pl.BlockSpec(memory_space=pltpu.HBM)],
         out_shape=[
             jax.ShapeDtypeStruct((DEVICES, 8, 128), jnp.bfloat16),
             jax.ShapeDtypeStruct((2 * grid_rows, 2 * BAND), jnp.bfloat16),
         ],
         scratch_shapes=[
-            pltpu.VMEM((CHUNKS, rows, WIDTH), jnp.float32),
+            pltpu.VMEM((2 * grid_rows, 2 * BAND), jnp.bfloat16),
+            pltpu.VMEM((rows, MASK), jnp.float32),
             pltpu.VMEM(step_value.shape, jnp.bfloat16),
             pltpu.VMEM(phases.shape, jnp.float32),
             pltpu.VMEM(base.shape, jnp.bfloat16),
@@ -280,82 +275,61 @@
             pltpu.VMEM((rows, HALF), jnp.float32),
             pltpu.VMEM((rows, HALF), jnp.float32),
             pltpu.VMEM((rows, HALF), jnp.float32),
-            pltpu.SemaphoreType.DMA((CHUNKS + 7,)),
+            pltpu.SemaphoreType.DMA((rows // CHUNK + 8,)),
         ],
         compiler_params=params(STREAM_LIMIT),
         name="mask_spectrum",
     )(*arguments)
 
 
-def field_kernel(
-    tiles_ref, pupil_ref, grid_ref, map_ref, field_ref, power_ref,
-    spec_ref, partial_ref, sum_ref,
-):
-    index = pl.program_id(0)
+def field_kernel(tiles_ref, pupil_ref, grid_ref, map_ref, field_ref, power_ref, spec_ref, partial_ref):
+    members = pupil_ref.shape[0]
     rows = grid_ref.shape[0] // 2
     slab = rows // KERN
-
-    @pl.when(index == 0)
-    def _():
-        load_tiles(tiles_ref, spec_ref)
-        for owner in range(KERN):
-            power_ref[owner, 2] = grid_ref[rows + owner * slab : rows + (owner + 1) * slab]
-
+    load_tiles(tiles_ref, spec_ref)
     spec_re = spec_ref[0]
     spec_im = spec_ref[1]
-    for corner in range(2):
-        kernel_re = pupil_ref[0, corner, 0]
-        kernel_im = pupil_ref[0, corner, 1]
-        amp_re = (kernel_re * spec_re - kernel_im * spec_im).astype(jnp.bfloat16)
-        amp_im = (kernel_re * spec_im + kernel_im * spec_re).astype(jnp.bfloat16)
-        block = jnp.concatenate(
-            [jnp.concatenate([amp_re, amp_im], 1), jnp.concatenate([-amp_im, amp_re], 1)], 0
-        )
-        partial_ref[corner * rows : (corner + 1) * rows] = float_dot(grid_ref[:rows], block).astype(
-            jnp.bfloat16
-        )
-    field_ref[0] = float_dot(partial_ref[...], map_ref[...])
-
-    for corner in range(2):
-        for owner in range(KERN):
+    for member in range(members):
+        for corner in range(2):
+            kernel_re = pupil_ref[member, corner, 0]
+            kernel_im = pupil_ref[member, corner, 1]
+            amp_re = (kernel_re * spec_re - kernel_im * spec_im).astype(jnp.bfloat16)
+            amp_im = (kernel_re * spec_im + kernel_im * spec_re).astype(jnp.bfloat16)
+            block = jnp.concatenate(
+                [jnp.concatenate([amp_re, amp_im], 1), jnp.concatenate([-amp_im, amp_re], 1)], 0
+            )
+            partial_ref[member, corner * rows : (corner + 1) * rows] = float_dot(grid_ref[:rows], block).astype(
+                jnp.bfloat16
+            )
+        field_ref[member] = float_dot(partial_ref[member], map_ref[...])
+    for owner in range(KERN):
+        power_ref[owner, 2] = grid_ref[rows + owner * slab : rows + (owner + 1) * slab]
+        for corner in range(2):
             at = corner * rows + owner * slab
-            real = field_ref[0, at : at + slab, :COARSE]
-            imag = field_ref[0, at : at + slab, COARSE:]
-            power = real * real + imag * imag
-
-            @pl.when(index == 0)
-            def _():
-                sum_ref[at : at + slab] = power
-
-            @pl.when(index == 1)
-            def _():
-                power_ref[owner, corner] = (sum_ref[at : at + slab] + power).astype(jnp.bfloat16)
+            power = None
+            for member in range(members):
+                real = field_ref[member, at : at + slab, :COARSE]
+                imag = field_ref[member, at : at + slab, COARSE:]
+                term = real * real + imag * imag
+                power = term if member == 0 else power + term
+            power_ref[owner, corner] = power.astype(jnp.bfloat16)
 
 
 def coarse_fields(tiles, pupils, grid_table, column_map):
     members = pupils.shape[0]
     rows = grid_table.shape[0] // 2
+    vmem = pl.BlockSpec(memory_space=pltpu.VMEM)
     return pl.pallas_call(
         field_kernel,
-        grid=(members,),
-        in_specs=[
-            whole_spec(tiles.shape),
-            pl.BlockSpec((1, 2, 2, BAND, BAND), lambda i: (i, 0, 0, 0, 0)),
-            whole_spec(grid_table.shape),
-            whole_spec(column_map.shape),
-        ],
-        out_specs=[
-            pl.BlockSpec((1, 2 * rows, 2 * COARSE), lambda i: (i, 0, 0)),
-            whole_spec((KERN, 3, rows // KERN, COARSE)),
-        ],
+        in_specs=[vmem] * 4,
+        out_specs=[vmem] * 2,
         out_shape=[
             jax.ShapeDtypeStruct((members, 2 * rows, 2 * COARSE), jnp.float32),
             jax.ShapeDtypeStruct((KERN, 3, rows // KERN, COARSE), jnp.bfloat16),
         ],
         scratch_shapes=[
             pltpu.VMEM((2, BAND, BAND), jnp.float32),
-            pltpu.VMEM((2 * rows, 2 * BAND), jnp.bfloat16),
-            pltpu.VMEM((2 * rows, COARSE), jnp.float32),
+            pltpu.VMEM((members, 2 * rows, 2 * BAND), jnp.bfloat16),
         ],
         compiler_params=params(),
         name="coarse_fields",
@@ -403,59 +377,47 @@
     )(parts, matrix)
 
 
-def gradient_kernel(
-    field_ref, adjoint_ref, pupil_ref, grid_ref, map_ref, out_ref, weighted_ref, back_ref, acc_ref
-):
-    index = pl.program_id(0)
+def gradient_kernel(field_ref, adjoint_ref, pupil_ref, grid_ref, map_ref, out_ref, weighted_ref, back_ref, acc_ref):
+    members = pupil_ref.shape[0]
     slab = adjoint_ref.shape[2]
     rows = slab * KERN
-
-    @pl.when(index == 0)
-    def _():
-        acc_ref[...] = jnp.zeros_like(acc_ref)
-
-    for corner in range(2):
-        for owner in range(KERN):
-            at = corner * rows + owner * slab
-            adjoint = 2.0 * adjoint_ref[owner, corner].astype(jnp.float32)
-            for half in range(2):
-                columns = slice(half * COARSE, (half + 1) * COARSE)
-                weighted_ref[at : at + slab, columns] = (field_ref[0, at : at + slab, columns] * adjoint).astype(
-                    jnp.bfloat16
-                )
-    back_ref[...] = dot_last(weighted_ref[...], map_ref[...]).astype(jnp.bfloat16)
-    for corner in range(2):
-        grads = dot_first(grid_ref[:rows], back_ref[corner * rows : (corner + 1) * rows])
-        grad_re = grads[:BAND, :BAND] + grads[BAND:, BAND:]
-        grad_im = grads[:BAND, BAND:] - grads[BAND:, :BAND]
-        kernel_re = pupil_ref[0, corner, 0]
-        kernel_im = pupil_ref[0, corner, 1]
-        acc_ref[0] += kernel_re * grad_re + kernel_im * grad_im
-        acc_ref[1] += kernel_re * grad_im - kernel_im * grad_re
-
-    @pl.when(index == pl.num_programs(0) - 1)
-    def _():
-        store_tiles(out_ref, acc_ref[0], acc_ref[1])
+    for member in range(members):
+        for corner in range(2):
+            for owner in range(KERN):
+                at = corner * rows + owner * slab
+                adjoint = 2.0 * adjoint_ref[owner, corner].astype(jnp.float32)
+                for half in range(2):
+                    columns = slice(half * COARSE, (half + 1) * COARSE)
+                    weighted_ref[member, at : at + slab, columns] = (
+                        field_ref[member, at : at + slab, columns] * adjoint
+                    ).astype(jnp.bfloat16)
+        back_ref[member] = dot_last(weighted_ref[member], map_ref[...]).astype(jnp.bfloat16)
+        for corner in range(2):
+            grads = dot_first(grid_ref[:rows], back_ref[member, corner * rows : (corner + 1) * rows])
+            grad_re = grads[:BAND, :BAND] + grads[BAND:, BAND:]
+            grad_im = grads[:BAND, BAND:] - grads[BAND:, :BAND]
+            kernel_re = pupil_ref[member, corner, 0]
+            kernel_im = pupil_ref[member, corner, 1]
+            term_re = kernel_re * grad_re + kernel_im * grad_im
+            term_im = kernel_re * grad_im - kernel_im * grad_re
+            first = member == 0 and corner == 0
+            acc_ref[0] = term_re if first else acc_ref[0] + term_re
+            acc_ref[1] = term_im if first else acc_ref[1] + term_im
+    store_tiles(out_ref, acc_ref[0], acc_ref[1])
 
 
 def spectrum_gradient(fields, adjoint, pupils, grid_table, column_map):
     members = pupils.shape[0]
     rows = grid_table.shape[0] // 2
+    vmem = pl.BlockSpec(memory_space=pltpu.VMEM)
     return pl.pallas_call(
         gradient_kernel,
-        grid=(members,),
-        in_specs=[
-            pl.BlockSpec((1, 2 * rows, 2 * COARSE), lambda i: (i, 0, 0)),
-            whole_spec(adjoint.shape),
-            pl.BlockSpec((1, 2, 2, BAND, BAND), lambda i: (i, 0, 0, 0, 0)),
-            whole_spec(grid_table.shape),
-            whole_spec(column_map.shape),
-        ],
-        out_specs=whole_spec((DEVICES, 8, 128)),
+        in_specs=[vmem] * 5,
+        out_specs=vmem,
         out_shape=jax.ShapeDtypeStruct((DEVICES, 8, 128), jnp.bfloat16),
         scratch_shapes=[
-            pltpu.VMEM((2 * rows, 2 * COARSE), jnp.bfloat16),
-            pltpu.VMEM((2 * rows, 2 * BAND), jnp.bfloat16),
+            pltpu.VMEM((members, 2 * rows, 2 * COARSE), jnp.bfloat16),
+            pltpu.VMEM((members, 2 * rows, 2 * BAND), jnp.bfloat16),
             pltpu.VMEM((2, BAND, BAND), jnp.float32),
         ],
         compiler_params=params(),
@@ -465,25 +427,27 @@
 
 def update_kernel(
     tiles_ref, base_ref, shift_ref, mask_ref, step_ref, phase_ref, out_ref,
-    spec_ref, bases_ref, shifts_ref, held_ref, steps_ref, phases_ref, re_ref, im_ref, stack_a, stack_b, product_a, product_b, sems,
+    tile_ref, spec_ref, bases_ref, shifts_ref, held_ref, steps_ref, phases_ref, re_ref, im_ref, flat_ref, stack_a, stack_b, product_a, product_b, sems,
 ):
     rows = mask_ref.shape[0]
     stacks = (stack_a, stack_b)
     products = (product_a, product_b)
-    columns = [pl.ds(i * WIDTH, WIDTH) for i in range(CHUNKS)]
+    count = rows // CHUNK
+    places = [pl.ds(i * CHUNK, CHUNK) for i in range(count)]
     chunks = [
-        pltpu.make_async_copy(mask_ref.at[:, columns[i]], held_ref.at[i], sems.at[i]) for i in range(CHUNKS)
+        pltpu.make_async_copy(mask_ref.at[places[i]], held_ref.at[places[i]], sems.at[i]) for i in range(count)
     ]
     results = [
-        pltpu.make_async_copy(held_ref.at[i], out_ref.at[:, columns[i]], sems.at[CHUNKS + i])
-        for i in range(CHUNKS)
+        pltpu.make_async_copy(held_ref.at[places[i]], out_ref.at[places[i]], sems.at[count + i])
+        for i in range(count)
     ]
     small = [
-        pltpu.make_async_copy(source, target, sems.at[2 * CHUNKS + i])
+        pltpu.make_async_copy(source, target, sems.at[2 * count + i])
         for i, (source, target) in enumerate(
             (
                 (base_ref, bases_ref),
                 (shift_ref.at[device_place()], shifts_ref),
+                (tiles_ref, tile_ref),
                 (phase_ref, phases_ref),
                 (step_ref, steps_ref),
             )
@@ -492,17 +456,18 @@
     for copy in small + chunks:
         copy.start()
 
-    load_tiles(tiles_ref, spec_ref)
-    gradient = jnp.concatenate([spec_ref[0], spec_ref[1]], 1).astype(jnp.bfloat16)
     small[0].wait()
     small[1].wait()
     cosine, sine = turned_table(bases_ref[...], shifts_ref[...])
+    small[2].wait()
+    load_tiles(tile_ref, spec_ref)
+    gradient = jnp.concatenate([spec_ref[0], spec_ref[1]], 1).astype(jnp.bfloat16)
     product = float_dot(jnp.concatenate(split(cosine) + split(sine), 0), gradient)
     by_cos = product[:rows] + product[rows : 2 * rows]
     by_sin = product[2 * rows : 3 * rows] + product[3 * rows :]
     col_re = by_cos[:, :BAND] - by_sin[:, BAND:]
     col_im = by_sin[:, :BAND] + by_cos[:, BAND:]
-    centre = col_re[:, HALF : HALF + 1] * (1.0 / MASK)
+    flat_ref[...] = jnp.broadcast_to(col_re[:, HALF : HALF + 1] * (1.0 / MASK), flat_ref.shape)
     mirror = conjugate_mirror()
     high, low = split(jnp.concatenate([col_re[:, HALF:], col_im[:, HALF:]], 1))
     other = float_dot(high, mirror) + float_dot(low, mirror)
@@ -510,66 +475,65 @@
     im_ref[...] = col_im[:, :HALF] + other[:, HALF:]
 
     def turn(i):
-        piece = 32
-        for start in range(0, rows, piece):
-            col_re = re_ref[start : start + piece]
-            col_im = im_ref[start : start + piece]
-            for part in range(PER):
-                step = i * PER + part
-                cosine = phases_ref[step : step + 1, :HALF]
-                sine = phases_ref[step : step + 1, HALF:]
-                at = part * rows + start
-                stacks[i % 2][at : at + piece, :HALF] = (col_re * cosine - col_im * sine).astype(jnp.bfloat16)
-                stacks[i % 2][at : at + piece, HALF:] = (col_re * sine + col_im * cosine).astype(jnp.bfloat16)
+        col_re = re_ref[places[i]]
+        col_im = im_ref[places[i]]
+        for step in range(STEPS):
+            cosine = phases_ref[step : step + 1, :HALF]
+            sine = phases_ref[step : step + 1, HALF:]
+            here = slice(step * CHUNK, (step + 1) * CHUNK)
+            stacks[i % 2][here, :HALF] = (col_re * cosine - col_im * sine).astype(jnp.bfloat16)
+            stacks[i % 2][here, HALF:] = (col_re * sine + col_im * cosine).astype(jnp.bfloat16)
 
     def finish(i):
-        for part in range(PER):
-            here = slice(part * STEP, (part + 1) * STEP)
-            mask = held_ref[i, :, here]
+        centre = flat_ref[places[i]]
+        for step in range(STEPS):
+            here = slice(step * STEP, (step + 1) * STEP)
+            mask = held_ref[places[i], here]
             transmit = jnp.tanh(mask)
-            pixel_grad = products[i % 2][part * rows : (part + 1) * rows] + centre
-            held_ref[i, :, here] = mask - step_size * pixel_grad * (1.0 - transmit * transmit)
+            pixel_grad = products[i % 2][step * CHUNK : (step + 1) * CHUNK] + centre
+            held_ref[places[i], here] = mask - step_size * pixel_grad * (1.0 - transmit * transmit)
         results[i].start()
 
-    small[2].wait()
+    small[3].wait()
     turn(0)
-    small[3].wait()
-    for i in range(CHUNKS):
+    small[4].wait()
+    for i in range(count):
         chunks[i].wait()
         products[i % 2][...] = float_dot(stacks[i % 2][...], steps_ref[...])
-        if i + 1 < CHUNKS:
+        if i + 1 < count:
             turn(i + 1)
         if i > 0:
             finish(i - 1)
-    finish(CHUNKS - 1)
+    finish(count - 1)
     for copy in results:
         copy.wait()
 
 
 def mask_update(tiles, base, shifts, mask_params, step_value, phases):
     rows = mask_params.shape[0]
-    stacked = rows * PER
+    stacked = STEPS * CHUNK
     hbm = pl.BlockSpec(memory_space=pltpu.HBM)
-    vmem = pl.BlockSpec(memory_space=pltpu.VMEM)
     return pl.pallas_call(
         update_kernel,
-        in_specs=[vmem] + [hbm] * 5,
+        in_specs=[hbm] * 6,
         out_specs=hbm,
         out_shape=jax.ShapeDtypeStruct((rows, MASK), jnp.float32),
         scratch_shapes=[
+            pltpu.VMEM(tiles.shape, jnp.bfloat16),
             pltpu.VMEM((2, BAND, BAND), jnp.float32),
             pltpu.VMEM(base.shape, jnp.float32),
             pltpu.VMEM((1, 2 * BAND), jnp.float32),
-            pltpu.VMEM((CHUNKS, rows, WIDTH), jnp.float32),
+            pltpu.VMEM((rows, MASK), jnp.float32),
             pltpu.VMEM(step_value.shape, jnp.bfloat16),
             pltpu.VMEM(phases.shape, jnp.float32),
             pltpu.VMEM((rows, HALF), jnp.float32),
             pltpu.VMEM((rows, HALF), jnp.float32),
+            pltpu.VMEM((rows, STEP), jnp.float32),
             pltpu.VMEM((stacked, BAND), jnp.bfloat16),
             pltpu.VMEM((stacked, BAND), jnp.bfloat16),
             pltpu.VMEM((stacked, STEP), jnp.float32),
             pltpu.VMEM((stacked, STEP), jnp.float32),
-            pltpu.SemaphoreType.DMA((2 * CHUNKS + 4,)),
+            pltpu.SemaphoreType.DMA((2 * (rows // CHUNK) + 5,)),
         ],
         compiler_params=params(STREAM_LIMIT),
         name="mask_update",

time: 124 us -> 120 us (0.968)
  Pallas kernels: 25.5 us -> 21.9 us
    pallas_call x3, Pallas kernels: 14.2 us -> 11.7 us  [the longest x1 7.44 us: mask_update(): pl.pallas_call(update_kernel, in_specs=[hbm] * 6, out_specs=hbm, out_shap...]
where the time goes in v5:
time: 120 us
  blocking collectives  96.5 us (80%)
  Pallas kernels  21.9 us (18%)
    all_to_all x6, blocking collectives, exchange(): return lax.all_to_all(values, axes, 0, 0, tiled=True)  96.5 us
    pallas_call x1, Pallas kernels, mask_spectrum(): pl.pallas_call(spectrum_kernel, in_specs=[pl.BlockSpec(memory_space=pltpu...  7.6 us
    pallas_call x1, Pallas kernels, mask_update(): pl.pallas_call(update_kernel, in_specs=[hbm] * 6, out_specs=hbm, out_shap...  7.44 us
    pallas_call x1, Pallas kernels, coarse_adjoint(): pl.pallas_call(adjoint_kernel, in_specs=[pl.BlockSpec(memory_space=pltpu....  2.61 us

profile of v5, /device:TPU:1, one launch (start us, length us, event | category | flops | bytes accessed | tf_op | source)
XLA Modules:
  0.0 120.0 jit_solution(16017213298612958543)
XLA Ops:
  0.0 0.0 copy-start.2
  0.0 0.0 copy-start
  0.0 7.6 %mask_spectrum.1 = (bf16[128,8,128]{2,1,0:T(8,128)(2,1)}, bf16[512,512]{1,0:T(8,128)(2,1)}) custom-call(f32[128,16384]{1,0:T(8,128)} %mask_ref.3, bf16[256,256]{1,0:T(8,128)(2,1)} %constant.31.clone.step_ref, f32[64,256]{1,0:T(8,128)} %constant.24.clone.phase_ref, bf16[1024,128]{1,0:T(8,128)(2,1)} %constant.26.clone.base_ref, ...), custom_call_target="tpu_custom_call" | custom-call | tf_op jit(solution)/shard_map/mask_spectrum/pallas_call | solution.py:253
  7.6 22.6 %all_to_all.30 = bf16[128,8,128]{2,1,0:T(8,128)(2,1)S(1)} all-to-all(bf16[128,8,128]{2,1,0:T(8,128)(2,1)} %get-tuple-element.9), channel_id=1, replica_groups=mesh['rows'=16,'kern'=8] {'rows','kern'}, dimensions={0} | all-to-all | bytes 524288 | tf_op jit(solution)/shard_map/all_to_all | solution.py:544
  30.2 0.1 reduce_sum.24
  30.3 0.0 copy-start.1
  30.4 15.0 %all_to_all.31.tiles_ref = bf16[128,8,128]{2,1,0:T(8,128)(2,1)S(1)} all-to-all(bf16[128,8,128]{2,1,0:T(8,128)(2,1)S(1)} %broadcast_in_dim.4), channel_id=1, replica_groups=mesh['rows'=16,'kern'=8] {'rows','kern'}, dimensions={0} | all-to-all | bytes 524288 | tf_op jit(solution)/shard_map/all_to_all | solution.py:544
  45.4 0.0 copy-done.2
  45.4 0.0 copy-done
  45.4 0.0 copy-start.3
  45.4 1.0 copy-done.3
  46.4 2.0 %coarse_fields.1 = (f32[2,512,1024]{2,1,0:T(8,128)S(1)}, bf16[8,3,32,512]{3,2,1,0:T(8,128)(2,1)S(1)}) custom-call(bf16[128,8,128]{2,1,0:T(8,128)(2,1)S(1)} %all_to_all.31.tiles_ref, f32[2,2,2,256,256]{4,3,2,1,0:T(8,128)S(1)} %copy-done, bf16[512,512]{1,0:T(8,128)(2,1)S(1)} %copy-done.3, bf16[512,1024]{1,0:T(8,128)(2,1)S(1)} %copy-done.2), custom_call_target="tpu_custom_call" | custom-call | tf_op jit(solution)/shard_map/coarse_fields/pallas_call | solution.py:322
  48.5 14.4 %all_to_all.32.parts_ref = bf16[8,3,32,512]{3,2,1,0:T(8,128)(2,1)S(1)} all-to-all(bf16[8,3,32,512]{3,2,1,0:T(8,128)(2,1)S(1)} %get-tuple-element.12), channel_id=1, replica_groups=mesh['rows'=16,'kern'=8] {'kern'}, dimensions={0} | all-to-all | bytes 1572864 | tf_op jit(solution)/shard_map/all_to_all | solution.py:544
  62.9 0.0 copy-done.1
  62.9 2.6 %coarse_adjoint.1 = bf16[8,2,32,512]{3,2,1,0:T(8,128)(2,1)S(1)} custom-call(bf16[8,3,32,512]{3,2,1,0:T(8,128)(2,1)S(1)} %all_to_all.32.parts_ref, bf16[512,4096]{1,0:T(8,128)(2,1)S(1)} %copy-done.1), custom_call_target="tpu_custom_call" | custom-call | tf_op jit(solution)/shard_map/coarse_adjoint/pallas_call | solution.py:370
  65.5 10.4 %all_to_all.33.adjoint_ref = bf16[8,2,32,512]{3,2,1,0:T(8,128)(2,1)S(1)} all-to-all(bf16[8,2,32,512]{3,2,1,0:T(8,128)(2,1)S(1)} %coarse_adjoint.1), channel_id=1, replica_groups=mesh['rows'=16,'kern'=8] {'kern'}, dimensions={0} | all-to-all | bytes 1048576 | tf_op jit(solution)/shard_map/all_to_all | solution.py:544
  75.9 2.2 %spectrum_gradient.1 = bf16[128,8,128]{2,1,0:T(8,128)(2,1)S(1)} custom-call(f32[2,512,1024]{2,1,0:T(8,128)S(1)} %get-tuple-element.11.field_ref, bf16[8,2,32,512]{3,2,1,0:T(8,128)(2,1)S(1)} %all_to_all.33.adjoint_ref, f32[2,2,2,256,256]{4,3,2,1,0:T(8,128)S(1)} %copy-done, bf16[512,512]{1,0:T(8,128)(2,1)S(1)} %copy-done.3, bf16[512,1024]{1,0:T(8,128)(2,1)S(1)} %copy-done.2), custom_call_target="tpu_custom_call" | custom-call | tf_op jit(solution)/shard_map/spectrum_gradient/pallas_call | solution.py:413
  78.1 18.6 %all_to_all.34 = bf16[128,8,128]{2,1,0:T(8,128)(2,1)S(1)} all-to-all(bf16[128,8,128]{2,1,0:T(8,128)(2,1)S(1)} %spectrum_gradient.1), channel_id=1, replica_groups=mesh['rows'=16,'kern'=8] {'rows','kern'}, dimensions={0} | all-to-all | bytes 524288 | tf_op jit(solution)/shard_map/all_to_all | solution.py:544
  96.8 0.1 reduce_sum.25
  97.0 15.4 %all_to_all.35.tiles_ref = bf16[128,8,128]{2,1,0:T(8,128)(2,1)} all-to-all(bf16[128,8,128]{2,1,0:T(8,128)(2,1)S(1)} %broadcast_in_dim.5), channel_id=1, replica_groups=mesh['rows'=16,'kern'=8] {'rows','kern'}, dimensions={0} | all-to-all | bytes 524288 | tf_op jit(solution)/shard_map/all_to_all | solution.py:544
  112.4 7.4 %mask_update.1 = f32[128,16384]{1,0:T(8,128)} custom-call(bf16[128,8,128]{2,1,0:T(8,128)(2,1)} %all_to_all.35.tiles_ref, f32[128,512]{1,0:T(8,128)} %constant.25.clone.base_ref, f32[128,1,512]{2,1,0:T(1,128)} %constant.27.clone.shift_ref, f32[128,16384]{1,0:T(8,128)} %mask_ref.3, bf16[256,256]{1,0:T(8,128)(2,1)} %constant.33.clone.step_ref, ...), custom_call_target="tpu_custom_call" | custom-call | tf_op jit(solution)/shard_map/mask_update/pallas_call | solution.py:516
  (2 shorter events, 0.1 us)
Async XLA Ops:
  0.0 45.4 %copy-start.2 = (bf16[512,1024]{1,0:T(8,128)(2,1)S(1)}, bf16[512,1024]{1,0:T(8,128)(2,1)}, u32[]{:S(2)}) copy-start(bf16[512,1024]{1,0:T(8,128)(2,1)} %constant.30.clone.map_ref) | copy-start | bytes 3145732
  0.0 45.4 %copy-start = (f32[2,2,2,256,256]{4,3,2,1,0:T(8,128)S(1)}, f32[2,2,2,256,256]{4,3,2,1,0:T(8,128)}, u32[]{:S(2)}) copy-start(f32[2,2,2,256,256]{4,3,2,1,0:T(8,128)} %pupil_ref.3) | copy-start | bytes 6291460
  30.3 32.6 %copy-start.1 = (bf16[512,4096]{1,0:T(8,128)(2,1)S(1)}, bf16[512,4096]{1,0:T(8,128)(2,1)}, u32[]{:S(2)}) copy-start(bf16[512,4096]{1,0:T(8,128)(2,1)} %constant.32.clone.matrix_ref) | copy-start | bytes 12582916
  45.4 1.0 copy-start.3

commit v6 on v5

--- a/solution.py
+++ b/solution.py
@@ -19,6 +19,7 @@
 KERN = 8
 DEVICES = ROWS * KERN
 CHUNK = 16
+QUARTERS = 4
 
 steepness = 4.0
 threshold = 0.75
@@ -169,20 +170,25 @@
     for copy in small[2:5] + chunks[2:] + small[5:]:
         copy.start()
 
-    def transmit(i):
-        chunks[i].wait()
+    def steps_of(quarter):
+        return range(quarter * STEPS // QUARTERS, (quarter + 1) * STEPS // QUARTERS)
+
+    def transmit(i, quarter):
         total = None
-        for step in range(STEPS):
-            value = jnp.tanh(held_ref[places[i], step * STEP : (step + 1) * STEP]).astype(jnp.bfloat16)
-            stacks[i % 2][step * CHUNK : (step + 1) * CHUNK] = value
-            wide = value.astype(jnp.float32)
-            both = wide[:, :HALF] + wide[:, HALF:]
-            total = both if step == 0 else total + both
-        flat_ref[places[i]] = total
-
-    def gather(i):
+        for step in steps_of(quarter):
+            value = jnp.tanh(held_ref[places[i], step * STEP : (step + 1) * STEP])
+            stacks[i % 2][step * CHUNK : (step + 1) * CHUNK] = value.astype(jnp.bfloat16)
+            both = value[:, :HALF] + value[:, HALF:]
+            total = both if total is None else total + both
+        flat_ref[places[i]] = total if quarter == 0 else flat_ref[places[i]] + total
+
+    def multiply(i, quarter):
+        here = slice(steps_of(quarter).start * CHUNK, steps_of(quarter).stop * CHUNK)
+        products[i % 2][here] = float_dot(stacks[i % 2][here], steps_ref[...])
+
+    def gather(i, quarter):
         totals = [None] * 4
-        for step in range(STEPS):
+        for step in steps_of(quarter):
             cosine = phases_ref[step : step + 1, :HALF]
             sine = phases_ref[step : step + 1, HALF:]
             first = products[i % 2][step * CHUNK : (step + 1) * CHUNK, :HALF]
@@ -191,19 +197,26 @@
             for part, turned in enumerate(
                 (first * cosine + second * sine, second * cosine - first * sine)
             ):
-                totals[at + part] = turned if step < 2 else totals[at + part] + turned
-        re_ref[places[i]] = totals[0] + totals[2]
-        im_ref[places[i]] = totals[1] + totals[3]
-
-    transmit(0)
+                totals[at + part] = turned if totals[at + part] is None else totals[at + part] + turned
+        total_re = totals[0] + totals[2]
+        total_im = totals[1] + totals[3]
+        re_ref[places[i]] = total_re if quarter == 0 else re_ref[places[i]] + total_re
+        im_ref[places[i]] = total_im if quarter == 0 else im_ref[places[i]] + total_im
+
+    chunks[0].wait()
+    for quarter in range(QUARTERS):
+        transmit(0, quarter)
     small[0].wait()
     small[1].wait()
     for i in range(count):
-        products[i % 2][...] = float_dot(stacks[i % 2][...], steps_ref[...])
         if i + 1 < count:
-            transmit(i + 1)
-        if i > 0:
-            gather(i - 1)
+            chunks[i + 1].wait()
+        for quarter in range(QUARTERS):
+            multiply(i, quarter)
+            if i + 1 < count:
+                transmit(i + 1, quarter)
+            if i > 0:
+                gather(i - 1, quarter)
         if i == 1:
             for copy in small[2:5]:
                 copy.wait()
@@ -212,7 +225,8 @@
             grid_ref[:grid_rows, BAND:] = sine.astype(jnp.bfloat16)
             grid_ref[grid_rows:] = targets_ref[...].astype(jnp.float32).astype(jnp.bfloat16)
             grid_copy.start()
-    gather(count - 1)
+    for quarter in range(QUARTERS):
+        gather(count - 1, quarter)
     for copy in small[5:]:
         copy.wait()
     _, lane = iotas((rows, HALF))
@@ -474,37 +488,48 @@
     re_ref[...] = col_re[:, :HALF] + other[:, :HALF]
     im_ref[...] = col_im[:, :HALF] + other[:, HALF:]
 
-    def turn(i):
+    def steps_of(quarter):
+        return range(quarter * STEPS // QUARTERS, (quarter + 1) * STEPS // QUARTERS)
+
+    def turn(i, quarter):
         col_re = re_ref[places[i]]
         col_im = im_ref[places[i]]
-        for step in range(STEPS):
+        for step in steps_of(quarter):
             cosine = phases_ref[step : step + 1, :HALF]
             sine = phases_ref[step : step + 1, HALF:]
             here = slice(step * CHUNK, (step + 1) * CHUNK)
             stacks[i % 2][here, :HALF] = (col_re * cosine - col_im * sine).astype(jnp.bfloat16)
             stacks[i % 2][here, HALF:] = (col_re * sine + col_im * cosine).astype(jnp.bfloat16)
 
-    def finish(i):
+    def multiply(i, quarter):
+        here = slice(steps_of(quarter).start * CHUNK, steps_of(quarter).stop * CHUNK)
+        products[i % 2][here] = float_dot(stacks[i % 2][here], steps_ref[...])
+
+    def finish(i, quarter):
         centre = flat_ref[places[i]]
-        for step in range(STEPS):
+        for step in steps_of(quarter):
             here = slice(step * STEP, (step + 1) * STEP)
             mask = held_ref[places[i], here]
             transmit = jnp.tanh(mask)
             pixel_grad = products[i % 2][step * CHUNK : (step + 1) * CHUNK] + centre
             held_ref[places[i], here] = mask - step_size * pixel_grad * (1.0 - transmit * transmit)
-        results[i].start()
 
     small[3].wait()
-    turn(0)
+    for quarter in range(QUARTERS):
+        turn(0, quarter)
     small[4].wait()
-    for i in range(count):
-        chunks[i].wait()
-        products[i % 2][...] = float_dot(stacks[i % 2][...], steps_ref[...])
-        if i + 1 < count:
-            turn(i + 1)
+    for i in range(count + 1):
         if i > 0:
-            finish(i - 1)
-    finish(count - 1)
+            chunks[i - 1].wait()
+        for quarter in range(QUARTERS):
+            if i < count:
+                multiply(i, quarter)
+            if i + 1 < count:
+                turn(i + 1, quarter)
+            if i > 0:
+                finish(i - 1, quarter)
+        if i > 0:
+            results[i - 1].start()
     for copy in results:
         copy.wait()
 

time: 120 us -> 119 us (level)
  no operation moved by 1% of the time
where the time goes in v6:
time: 119 us
  blocking collectives  96.7 us (81%)
  Pallas kernels  20.9 us (18%)
    all_to_all x6, blocking collectives, exchange(): return lax.all_to_all(values, axes, 0, 0, tiled=True)  96.7 us
    pallas_call x1, Pallas kernels, mask_spectrum(): pl.pallas_call(spectrum_kernel, in_specs=[pl.BlockSpec(memory_space=pltpu...  7.09 us
    pallas_call x1, Pallas kernels, mask_update(): pl.pallas_call(update_kernel, in_specs=[hbm] * 6, out_specs=hbm, out_shap...  6.95 us
    pallas_call x1, Pallas kernels, coarse_adjoint(): pl.pallas_call(adjoint_kernel, in_specs=[pl.BlockSpec(memory_space=pltpu....  2.61 us

profile of v6, /device:TPU:1, one launch (start us, length us, event | category | flops | bytes accessed | tf_op | source)
XLA Modules:
  0.0 119.2 jit_solution(11688017866038903214)
XLA Ops:
  0.0 0.0 copy-start.2
  0.0 0.0 copy-start
  0.0 7.1 %mask_spectrum.1 = (bf16[128,8,128]{2,1,0:T(8,128)(2,1)}, bf16[512,512]{1,0:T(8,128)(2,1)}) custom-call(f32[128,16384]{1,0:T(8,128)} %mask_ref.3, bf16[256,256]{1,0:T(8,128)(2,1)} %constant.31.clone.step_ref, f32[64,256]{1,0:T(8,128)} %constant.24.clone.phase_ref, bf16[1024,128]{1,0:T(8,128)(2,1)} %constant.26.clone.base_ref, ...), custom_call_target="tpu_custom_call" | custom-call | tf_op jit(solution)/shard_map/mask_spectrum/pallas_call | solution.py:267
  7.1 22.6 %all_to_all.30 = bf16[128,8,128]{2,1,0:T(8,128)(2,1)S(1)} all-to-all(bf16[128,8,128]{2,1,0:T(8,128)(2,1)} %get-tuple-element.9), channel_id=1, replica_groups=mesh['rows'=16,'kern'=8] {'rows','kern'}, dimensions={0} | all-to-all | bytes 524288 | tf_op jit(solution)/shard_map/all_to_all | solution.py:569
  29.7 0.1 reduce_sum.24
  29.8 0.0 copy-start.1
  29.8 15.0 %all_to_all.31.tiles_ref = bf16[128,8,128]{2,1,0:T(8,128)(2,1)S(1)} all-to-all(bf16[128,8,128]{2,1,0:T(8,128)(2,1)S(1)} %broadcast_in_dim.4), channel_id=1, replica_groups=mesh['rows'=16,'kern'=8] {'rows','kern'}, dimensions={0} | all-to-all | bytes 524288 | tf_op jit(solution)/shard_map/all_to_all | solution.py:569
  44.9 0.0 copy-done.2
  44.9 0.0 copy-done
  44.9 0.0 copy-start.3
  44.9 1.0 copy-done.3
  45.9 2.0 %coarse_fields.1 = (f32[2,512,1024]{2,1,0:T(8,128)S(1)}, bf16[8,3,32,512]{3,2,1,0:T(8,128)(2,1)S(1)}) custom-call(bf16[128,8,128]{2,1,0:T(8,128)(2,1)S(1)} %all_to_all.31.tiles_ref, f32[2,2,2,256,256]{4,3,2,1,0:T(8,128)S(1)} %copy-done, bf16[512,512]{1,0:T(8,128)(2,1)S(1)} %copy-done.3, bf16[512,1024]{1,0:T(8,128)(2,1)S(1)} %copy-done.2), custom_call_target="tpu_custom_call" | custom-call | tf_op jit(solution)/shard_map/coarse_fields/pallas_call | solution.py:336
  47.9 14.4 %all_to_all.32.parts_ref = bf16[8,3,32,512]{3,2,1,0:T(8,128)(2,1)S(1)} all-to-all(bf16[8,3,32,512]{3,2,1,0:T(8,128)(2,1)S(1)} %get-tuple-element.12), channel_id=1, replica_groups=mesh['rows'=16,'kern'=8] {'kern'}, dimensions={0} | all-to-all | bytes 1572864 | tf_op jit(solution)/shard_map/all_to_all | solution.py:569
  62.4 0.0 copy-done.1
  62.4 2.6 %coarse_adjoint.1 = bf16[8,2,32,512]{3,2,1,0:T(8,128)(2,1)S(1)} custom-call(bf16[8,3,32,512]{3,2,1,0:T(8,128)(2,1)S(1)} %all_to_all.32.parts_ref, bf16[512,4096]{1,0:T(8,128)(2,1)S(1)} %copy-done.1), custom_call_target="tpu_custom_call" | custom-call | tf_op jit(solution)/shard_map/coarse_adjoint/pallas_call | solution.py:384
  65.0 10.4 %all_to_all.33.adjoint_ref = bf16[8,2,32,512]{3,2,1,0:T(8,128)(2,1)S(1)} all-to-all(bf16[8,2,32,512]{3,2,1,0:T(8,128)(2,1)S(1)} %coarse_adjoint.1), channel_id=1, replica_groups=mesh['rows'=16,'kern'=8] {'kern'}, dimensions={0} | all-to-all | bytes 1048576 | tf_op jit(solution)/shard_map/all_to_all | solution.py:569
  75.4 2.2 %spectrum_gradient.1 = bf16[128,8,128]{2,1,0:T(8,128)(2,1)S(1)} custom-call(f32[2,512,1024]{2,1,0:T(8,128)S(1)} %get-tuple-element.11.field_ref, bf16[8,2,32,512]{3,2,1,0:T(8,128)(2,1)S(1)} %all_to_all.33.adjoint_ref, f32[2,2,2,256,256]{4,3,2,1,0:T(8,128)S(1)} %copy-done, bf16[512,512]{1,0:T(8,128)(2,1)S(1)} %copy-done.3, bf16[512,1024]{1,0:T(8,128)(2,1)S(1)} %copy-done.2), custom_call_target="tpu_custom_call" | custom-call | tf_op jit(solution)/shard_map/spectrum_gradient/pallas_call | solution.py:427
  77.6 18.6 %all_to_all.34 = bf16[128,8,128]{2,1,0:T(8,128)(2,1)S(1)} all-to-all(bf16[128,8,128]{2,1,0:T(8,128)(2,1)S(1)} %spectrum_gradient.1), channel_id=1, replica_groups=mesh['rows'=16,'kern'=8] {'rows','kern'}, dimensions={0} | all-to-all | bytes 524288 | tf_op jit(solution)/shard_map/all_to_all | solution.py:569
  96.3 0.1 reduce_sum.25
  96.5 15.6 %all_to_all.35.tiles_ref = bf16[128,8,128]{2,1,0:T(8,128)(2,1)} all-to-all(bf16[128,8,128]{2,1,0:T(8,128)(2,1)S(1)} %broadcast_in_dim.5), channel_id=1, replica_groups=mesh['rows'=16,'kern'=8] {'rows','kern'}, dimensions={0} | all-to-all | bytes 524288 | tf_op jit(solution)/shard_map/all_to_all | solution.py:569
  112.0 6.9 %mask_update.1 = f32[128,16384]{1,0:T(8,128)} custom-call(bf16[128,8,128]{2,1,0:T(8,128)(2,1)} %all_to_all.35.tiles_ref, f32[128,512]{1,0:T(8,128)} %constant.25.clone.base_ref, f32[128,1,512]{2,1,0:T(1,128)} %constant.27.clone.shift_ref, f32[128,16384]{1,0:T(8,128)} %mask_ref.3, bf16[256,256]{1,0:T(8,128)(2,1)} %constant.33.clone.step_ref, ...), custom_call_target="tpu_custom_call" | custom-call | tf_op jit(solution)/shard_map/mask_update/pallas_call | solution.py:541
  (2 shorter events, 0.1 us)
Async XLA Ops:
  0.0 44.9 %copy-start.2 = (bf16[512,1024]{1,0:T(8,128)(2,1)S(1)}, bf16[512,1024]{1,0:T(8,128)(2,1)}, u32[]{:S(2)}) copy-start(bf16[512,1024]{1,0:T(8,128)(2,1)} %constant.30.clone.map_ref) | copy-start | bytes 3145732
  0.0 44.9 %copy-start = (f32[2,2,2,256,256]{4,3,2,1,0:T(8,128)S(1)}, f32[2,2,2,256,256]{4,3,2,1,0:T(8,128)}, u32[]{:S(2)}) copy-start(f32[2,2,2,256,256]{4,3,2,1,0:T(8,128)} %pupil_ref.3) | copy-start | bytes 6291460
  29.8 32.6 %copy-start.1 = (bf16[512,4096]{1,0:T(8,128)(2,1)S(1)}, bf16[512,4096]{1,0:T(8,128)(2,1)}, u32[]{:S(2)}) copy-start(bf16[512,4096]{1,0:T(8,128)(2,1)} %constant.32.clone.matrix_ref) | copy-start | bytes 12582916
  44.9 1.0 copy-start.3

commit v7 on v6

--- a/solution.py
+++ b/solution.py
@@ -28,6 +28,7 @@
 
 VMEM_LIMIT = 24 * 1024 * 1024
 STREAM_LIMIT = 56 * 1024 * 1024
+FIRST_LIMIT = 53 * 1024 * 1024
 
 
 def tables(positions, period, count=BAND):
@@ -291,7 +292,7 @@
             pltpu.VMEM((rows, HALF), jnp.float32),
             pltpu.SemaphoreType.DMA((rows // CHUNK + 8,)),
         ],
-        compiler_params=params(STREAM_LIMIT),
+        compiler_params=params(FIRST_LIMIT),
         name="mask_spectrum",
     )(*arguments)
 

time: 119 us -> 122 us (1.025)
  local copies, waits for them, and re-layouts: 1.13 us -> 4.67 us
    unnamed x8 -> x16, local copies, waits for them, and re-layouts: 1.05 us -> 4.59 us
where the time goes in v7:
time: 122 us
  blocking collectives  96.4 us (79%)
  Pallas kernels  20.2 us (17%)
  local copies, waits for them, and re-layouts  4.67 us (4%)
    all_to_all x6, blocking collectives, exchange(): return lax.all_to_all(values, axes, 0, 0, tiled=True)  96.4 us
    pallas_call x1, Pallas kernels, mask_update(): pl.pallas_call(update_kernel, in_specs=[hbm] * 6, out_specs=hbm, out_shap...  6.96 us
    pallas_call x1, Pallas kernels, mask_spectrum(): pl.pallas_call(spectrum_kernel, in_specs=[pl.BlockSpec(memory_space=pltpu...  6.35 us
    unnamed x16, local copies, waits for them, and re-layouts  4.59 us
    pallas_call x1, Pallas kernels, coarse_adjoint(): pl.pallas_call(adjoint_kernel, in_specs=[pl.BlockSpec(memory_space=pltpu....  2.61 us

profile of v7, /device:TPU:1, one launch (start us, length us, event | category | flops | bytes accessed | tf_op | source)
XLA Modules:
  0.0 121.7 jit_solution(13074659752522884035)
XLA Ops:
  0.0 0.0 copy-start.2
  0.0 0.0 copy-start.4
  0.0 0.9 copy-done.4
  0.9 0.0 copy-start.5
  0.9 0.9 copy-done.5
  1.9 0.0 copy-start.6
  1.9 0.9 copy-done.6
  2.8 0.0 copy-start.7
  2.8 0.8 copy-done.7
  3.5 0.0 copy-start
  3.5 6.3 %mask_spectrum.1 = (bf16[128,8,128]{2,1,0:T(8,128)(2,1)S(1)}, bf16[512,512]{1,0:T(8,128)(2,1)}) custom-call(f32[128,16384]{1,0:T(8,128)} %mask_ref.3, bf16[256,256]{1,0:T(8,128)(2,1)S(1)} %copy-done.6, f32[64,256]{1,0:T(8,128)S(1)} %copy-done.4, bf16[1024,128]{1,0:T(8,128)(2,1)S(1)} %copy-done.5, f32[128,1,512]{2,1,0:T(1,128)} %constant.27.clone.shift_ref, ...), custom_call_target="tpu_custom_call" | custom-call | tf_op jit(solution)/shard_map/mask_spectrum/pallas_call | solution.py:268
  9.9 22.3 %all_to_all.30 = bf16[128,8,128]{2,1,0:T(8,128)(2,1)S(1)} all-to-all(bf16[128,8,128]{2,1,0:T(8,128)(2,1)S(1)} %get-tuple-element.9), channel_id=1, replica_groups=mesh['rows'=16,'kern'=8] {'rows','kern'}, dimensions={0} | all-to-all | bytes 524288 | tf_op jit(solution)/shard_map/all_to_all | solution.py:570
  32.3 0.1 reduce_sum.24
  32.4 0.0 copy-start.1
  32.4 15.0 %all_to_all.31.tiles_ref = bf16[128,8,128]{2,1,0:T(8,128)(2,1)S(1)} all-to-all(bf16[128,8,128]{2,1,0:T(8,128)(2,1)S(1)} %broadcast_in_dim.4), channel_id=1, replica_groups=mesh['rows'=16,'kern'=8] {'rows','kern'}, dimensions={0} | all-to-all | bytes 524288 | tf_op jit(solution)/shard_map/all_to_all | solution.py:570
  47.5 0.0 copy-done.2
  47.5 0.0 copy-done
  47.5 0.0 copy-start.3
  47.5 1.0 copy-done.3
  48.5 2.0 %coarse_fields.1 = (f32[2,512,1024]{2,1,0:T(8,128)S(1)}, bf16[8,3,32,512]{3,2,1,0:T(8,128)(2,1)S(1)}) custom-call(bf16[128,8,128]{2,1,0:T(8,128)(2,1)S(1)} %all_to_all.31.tiles_ref, f32[2,2,2,256,256]{4,3,2,1,0:T(8,128)S(1)} %copy-done, bf16[512,512]{1,0:T(8,128)(2,1)S(1)} %copy-done.3, bf16[512,1024]{1,0:T(8,128)(2,1)S(1)} %copy-done.2), custom_call_target="tpu_custom_call" | custom-call | tf_op jit(solution)/shard_map/coarse_fields/pallas_call | solution.py:337
  50.5 14.4 %all_to_all.32.parts_ref = bf16[8,3,32,512]{3,2,1,0:T(8,128)(2,1)S(1)} all-to-all(bf16[8,3,32,512]{3,2,1,0:T(8,128)(2,1)S(1)} %get-tuple-element.12), channel_id=1, replica_groups=mesh['rows'=16,'kern'=8] {'kern'}, dimensions={0} | all-to-all | bytes 1572864 | tf_op jit(solution)/shard_map/all_to_all | solution.py:570
  65.0 0.0 copy-done.1
  65.0 2.6 %coarse_adjoint.1 = bf16[8,2,32,512]{3,2,1,0:T(8,128)(2,1)S(1)} custom-call(bf16[8,3,32,512]{3,2,1,0:T(8,128)(2,1)S(1)} %all_to_all.32.parts_ref, bf16[512,4096]{1,0:T(8,128)(2,1)S(1)} %copy-done.1), custom_call_target="tpu_custom_call" | custom-call | tf_op jit(solution)/shard_map/coarse_adjoint/pallas_call | solution.py:385
  67.6 10.4 %all_to_all.33.adjoint_ref = bf16[8,2,32,512]{3,2,1,0:T(8,128)(2,1)S(1)} all-to-all(bf16[8,2,32,512]{3,2,1,0:T(8,128)(2,1)S(1)} %coarse_adjoint.1), channel_id=1, replica_groups=mesh['rows'=16,'kern'=8] {'kern'}, dimensions={0} | all-to-all | bytes 1048576 | tf_op jit(solution)/shard_map/all_to_all | solution.py:570
  78.0 2.2 %spectrum_gradient.1 = bf16[128,8,128]{2,1,0:T(8,128)(2,1)S(1)} custom-call(f32[2,512,1024]{2,1,0:T(8,128)S(1)} %get-tuple-element.11.field_ref, bf16[8,2,32,512]{3,2,1,0:T(8,128)(2,1)S(1)} %all_to_all.33.adjoint_ref, f32[2,2,2,256,256]{4,3,2,1,0:T(8,128)S(1)} %copy-done, bf16[512,512]{1,0:T(8,128)(2,1)S(1)} %copy-done.3, bf16[512,1024]{1,0:T(8,128)(2,1)S(1)} %copy-done.2), custom_call_target="tpu_custom_call" | custom-call | tf_op jit(solution)/shard_map/spectrum_gradient/pallas_call | solution.py:428
  80.2 18.6 %all_to_all.34 = bf16[128,8,128]{2,1,0:T(8,128)(2,1)S(1)} all-to-all(bf16[128,8,128]{2,1,0:T(8,128)(2,1)S(1)} %spectrum_gradient.1), channel_id=1, replica_groups=mesh['rows'=16,'kern'=8] {'rows','kern'}, dimensions={0} | all-to-all | bytes 524288 | tf_op jit(solution)/shard_map/all_to_all | solution.py:570
  98.8 0.1 reduce_sum.25
  99.0 15.6 %all_to_all.35.tiles_ref = bf16[128,8,128]{2,1,0:T(8,128)(2,1)} all-to-all(bf16[128,8,128]{2,1,0:T(8,128)(2,1)S(1)} %broadcast_in_dim.5), channel_id=1, replica_groups=mesh['rows'=16,'kern'=8] {'rows','kern'}, dimensions={0} | all-to-all | bytes 524288 | tf_op jit(solution)/shard_map/all_to_all | solution.py:570
  114.6 7.0 %mask_update.1 = f32[128,16384]{1,0:T(8,128)} custom-call(bf16[128,8,128]{2,1,0:T(8,128)(2,1)} %all_to_all.35.tiles_ref, f32[128,512]{1,0:T(8,128)} %constant.25.clone.base_ref, f32[128,1,512]{2,1,0:T(1,128)} %constant.27.clone.shift_ref, f32[128,16384]{1,0:T(8,128)} %mask_ref.3, bf16[256,256]{1,0:T(8,128)(2,1)} %constant.33.clone.step_ref, ...), custom_call_target="tpu_custom_call" | custom-call | tf_op jit(solution)/shard_map/mask_update/pallas_call | solution.py:542
  (2 shorter events, 0.1 us)
Async XLA Ops:
  0.0 47.5 %copy-start.2 = (bf16[512,1024]{1,0:T(8,128)(2,1)S(1)}, bf16[512,1024]{1,0:T(8,128)(2,1)}, u32[]{:S(2)}) copy-start(bf16[512,1024]{1,0:T(8,128)(2,1)} %constant.30.clone.map_ref) | copy-start | bytes 3145732
  0.0 0.9 copy-start.4
  0.9 0.9 copy-start.5
  1.9 0.9 copy-start.6
  2.8 0.8 copy-start.7
  3.5 43.9 %copy-start = (f32[2,2,2,256,256]{4,3,2,1,0:T(8,128)S(1)}, f32[2,2,2,256,256]{4,3,2,1,0:T(8,128)}, u32[]{:S(2)}) copy-start(f32[2,2,2,256,256]{4,3,2,1,0:T(8,128)} %pupil_ref.3) | copy-start | bytes 6291460
  32.4 32.6 %copy-start.1 = (bf16[512,4096]{1,0:T(8,128)(2,1)S(1)}, bf16[512,4096]{1,0:T(8,128)(2,1)}, u32[]{:S(2)}) copy-start(bf16[512,4096]{1,0:T(8,128)(2,1)} %constant.32.clone.matrix_ref) | copy-start | bytes 12582916
  47.5 1.0 copy-start.3

commit v8 on v6

--- a/solution.py
+++ b/solution.py
@@ -27,7 +27,7 @@
 dose_levels = (1.0, 1.15)
 
 VMEM_LIMIT = 24 * 1024 * 1024
-STREAM_LIMIT = 56 * 1024 * 1024
+STREAM_LIMIT = 53 * 1024 * 1024
 
 
 def tables(positions, period, count=BAND):
@@ -53,6 +53,37 @@
     table = wide_table(np.arange(rows), MASK).T
     high = bfloat(table)
     return np.concatenate([high, bfloat(table - high.astype(np.float32))], 0)
+
+
+TABLE_ROWS = {"grid": GRID, "base": 128, "shift": DEVICES, "phase": STEPS, "step": STEP, "transform": STEP}
+
+
+def constant_table(rows):
+    step = step_table().astype(np.float32)
+    transform = row_transform(rows).astype(np.float32)
+    parts = {
+        "grid": wide_table(np.arange(GRID), GRID),
+        "base": wide_table(np.arange(rows), MASK),
+        "shift": wide_table(np.arange(DEVICES) * rows, MASK),
+        "phase": np.pad(wide_table(np.arange(STEPS) * STEP, MASK, HALF), ((0, 0), (0, BAND))),
+        "step": np.concatenate([step, step.T], 1),
+        "transform": np.concatenate(np.split(transform, 4, 0), 1),
+    }
+    return np.concatenate([parts[name] for name in TABLE_ROWS], 0)
+
+
+def table_rows(name, start=0, count=None):
+    names = list(TABLE_ROWS)
+    first = sum(TABLE_ROWS[before] for before in names[: names.index(name)])
+    return pl.ds(pl.multiple_of(first + start, 8), TABLE_ROWS[name] if count is None else count)
+
+
+def shift_group():
+    return table_rows("shift", 8 * (device_place() // 8), 8)
+
+
+def own_shift(shifts_ref):
+    return shifts_ref[pl.ds(lax.rem(device_place(), 8), 1), :]
 
 
 def coarse_map():
@@ -134,9 +165,8 @@
 
 
 def spectrum_kernel(
-    mask_ref, step_ref, phase_ref, base_ref, shift_ref, grid_base_ref, grid_shift_ref, target_ref,
-    out_ref, grid_out_ref,
-    grid_ref, held_ref, steps_ref, phases_ref, bases_ref, shifts_ref, grid_bases_ref, grid_shifts_ref, targets_ref,
+    mask_ref, constant_ref, target_ref, out_ref, grid_out_ref,
+    grid_ref, held_ref, steps_ref, phases_ref, bases_ref, shifts_ref, grid_rows_ref, targets_ref,
     stack_a, stack_b, product_a, product_b, re_ref, im_ref, flat_ref, sems,
 ):
     rows = mask_ref.shape[0]
@@ -152,22 +182,21 @@
         pltpu.make_async_copy(source, target, sems.at[count + i])
         for i, (source, target) in enumerate(
             (
-                (step_ref, steps_ref),
-                (phase_ref, phases_ref),
-                (grid_base_ref, grid_bases_ref),
-                (grid_shift_ref.at[lax.axis_index("rows")], grid_shifts_ref),
+                (constant_ref.at[table_rows("step")], steps_ref),
+                (constant_ref.at[table_rows("phase")], phases_ref),
+                (constant_ref.at[table_rows("grid", lax.axis_index("rows") * grid_rows, grid_rows)], grid_rows_ref),
                 (target_ref, targets_ref),
-                (base_ref, bases_ref),
-                (shift_ref.at[device_place()], shifts_ref),
+                (constant_ref.at[table_rows("transform")], bases_ref),
+                (constant_ref.at[shift_group()], shifts_ref),
             )
         )
     ]
-    grid_copy = pltpu.make_async_copy(grid_ref, grid_out_ref, sems.at[count + 7])
+    grid_copy = pltpu.make_async_copy(grid_ref, grid_out_ref, sems.at[count + 6])
     chunks[0].start()
     small[0].start()
     small[1].start()
     chunks[1].start()
-    for copy in small[2:5] + chunks[2:] + small[5:]:
+    for copy in small[2:4] + chunks[2:] + small[4:]:
         copy.start()
 
     def steps_of(quarter):
@@ -184,13 +213,13 @@
 
     def multiply(i, quarter):
         here = slice(steps_of(quarter).start * CHUNK, steps_of(quarter).stop * CHUNK)
-        products[i % 2][here] = float_dot(stacks[i % 2][here], steps_ref[...])
+        products[i % 2][here] = float_dot(stacks[i % 2][here], step_value)
 
     def gather(i, quarter):
         totals = [None] * 4
         for step in steps_of(quarter):
             cosine = phases_ref[step : step + 1, :HALF]
-            sine = phases_ref[step : step + 1, HALF:]
+            sine = phases_ref[step : step + 1, HALF:BAND]
             first = products[i % 2][step * CHUNK : (step + 1) * CHUNK, :HALF]
             second = products[i % 2][step * CHUNK : (step + 1) * CHUNK, HALF:]
             at = 2 * (step % 2)
@@ -208,6 +237,7 @@
         transmit(0, quarter)
     small[0].wait()
     small[1].wait()
+    step_value = steps_ref[:, :BAND].astype(jnp.bfloat16)
     for i in range(count):
         if i + 1 < count:
             chunks[i + 1].wait()
@@ -218,16 +248,14 @@
             if i > 0:
                 gather(i - 1, quarter)
         if i == 1:
-            for copy in small[2:5]:
+            for copy in small[2:4]:
                 copy.wait()
-            cosine, sine = turned_table(grid_bases_ref[...], grid_shifts_ref[...])
-            grid_ref[:grid_rows, :BAND] = cosine.astype(jnp.bfloat16)
-            grid_ref[:grid_rows, BAND:] = sine.astype(jnp.bfloat16)
+            grid_ref[:grid_rows] = grid_rows_ref[...].astype(jnp.bfloat16)
             grid_ref[grid_rows:] = targets_ref[...].astype(jnp.float32).astype(jnp.bfloat16)
             grid_copy.start()
     for quarter in range(QUARTERS):
         gather(count - 1, quarter)
-    for copy in small[5:]:
+    for copy in small[4:]:
         copy.wait()
     _, lane = iotas((rows, HALF))
     mirror = conjugate_mirror()
@@ -239,11 +267,14 @@
     )
     high = jnp.concatenate([half_high, other_high], 1)
     low = jnp.concatenate([half_low, other_low], 1)
-    product = float_dot(bases_ref[...], high)
-    product = product[: 2 * BAND] + (product[2 * BAND :] + float_dot(bases_ref[: 2 * BAND], low))
+    transform = [bases_ref[:, at * rows : (at + 1) * rows].astype(jnp.bfloat16) for at in range(4)]
+    product = float_dot(jnp.concatenate(transform, 0), high)
+    rest = float_dot(jnp.concatenate(transform[:2], 0), low)
+    product = product[: 2 * BAND] + (product[2 * BAND :] + rest)
     diagonal = jnp.equal(*iotas((BAND, BAND)))
+    shift = own_shift(shifts_ref)
     turn_cos, turn_sin = [
-        jnp.sum(jnp.where(diagonal, shifts_ref[:, part * BAND : (part + 1) * BAND], 0.0), 1, keepdims=True)
+        jnp.sum(jnp.where(diagonal, shift[:, part * BAND : (part + 1) * BAND], 0.0), 1, keepdims=True)
         for part in range(2)
     ]
     by_cos = product[:BAND]
@@ -259,11 +290,11 @@
     grid_copy.wait()
 
 
-def mask_spectrum(mask_params, step_value, phases, base, shifts, grid_base, grid_shifts, target):
+def mask_spectrum(mask_params, constants, target):
     rows = mask_params.shape[0]
     stacked = STEPS * CHUNK
-    arguments = (mask_params, step_value, phases, base, shifts, grid_base, grid_shifts, target)
-    grid_rows = grid_base.shape[0]
+    arguments = (mask_params, constants, target)
+    grid_rows = target.shape[0]
     return pl.pallas_call(
         spectrum_kernel,
         in_specs=[pl.BlockSpec(memory_space=pltpu.HBM)] * len(arguments),
@@ -275,12 +306,11 @@
         scratch_shapes=[
             pltpu.VMEM((2 * grid_rows, 2 * BAND), jnp.bfloat16),
             pltpu.VMEM((rows, MASK), jnp.float32),
-            pltpu.VMEM(step_value.shape, jnp.bfloat16),
-            pltpu.VMEM(phases.shape, jnp.float32),
-            pltpu.VMEM(base.shape, jnp.bfloat16),
-            pltpu.VMEM((1, 2 * BAND), jnp.float32),
-            pltpu.VMEM(grid_base.shape, jnp.float32),
-            pltpu.VMEM((1, 2 * BAND), jnp.float32),
+            pltpu.VMEM((STEP, 2 * BAND), jnp.float32),
+            pltpu.VMEM((STEPS, 2 * BAND), jnp.float32),
+            pltpu.VMEM((STEP, 2 * BAND), jnp.float32),
+            pltpu.VMEM((8, 2 * BAND), jnp.float32),
+            pltpu.VMEM((grid_rows, 2 * BAND), jnp.float32),
             pltpu.VMEM(target.shape, jnp.int32),
             pltpu.VMEM((stacked, STEP), jnp.bfloat16),
             pltpu.VMEM((stacked, STEP), jnp.bfloat16),
@@ -289,7 +319,7 @@
             pltpu.VMEM((rows, HALF), jnp.float32),
             pltpu.VMEM((rows, HALF), jnp.float32),
             pltpu.VMEM((rows, HALF), jnp.float32),
-            pltpu.SemaphoreType.DMA((rows // CHUNK + 8,)),
+            pltpu.SemaphoreType.DMA((rows // CHUNK + 7,)),
         ],
         compiler_params=params(STREAM_LIMIT),
         name="mask_spectrum",
@@ -440,7 +470,7 @@
 
 
 def update_kernel(
-    tiles_ref, base_ref, shift_ref, mask_ref, step_ref, phase_ref, out_ref,
+    tiles_ref, constant_ref, mask_ref, out_ref,
     tile_ref, spec_ref, bases_ref, shifts_ref, held_ref, steps_ref, phases_ref, re_ref, im_ref, flat_ref, stack_a, stack_b, product_a, product_b, sems,
 ):
     rows = mask_ref.shape[0]
@@ -459,11 +489,11 @@
         pltpu.make_async_copy(source, target, sems.at[2 * count + i])
         for i, (source, target) in enumerate(
             (
-                (base_ref, bases_ref),
-                (shift_ref.at[device_place()], shifts_ref),
+                (constant_ref.at[table_rows("base")], bases_ref),
+                (constant_ref.at[shift_group()], shifts_ref),
                 (tiles_ref, tile_ref),
-                (phase_ref, phases_ref),
-                (step_ref, steps_ref),
+                (constant_ref.at[table_rows("phase")], phases_ref),
+                (constant_ref.at[table_rows("step")], steps_ref),
             )
         )
     ]
@@ -472,7 +502,7 @@
 
     small[0].wait()
     small[1].wait()
-    cosine, sine = turned_table(bases_ref[...], shifts_ref[...])
+    cosine, sine = turned_table(bases_ref[...], own_shift(shifts_ref))
     small[2].wait()
     load_tiles(tile_ref, spec_ref)
     gradient = jnp.concatenate([spec_ref[0], spec_ref[1]], 1).astype(jnp.bfloat16)
@@ -496,14 +526,14 @@
         col_im = im_ref[places[i]]
         for step in steps_of(quarter):
             cosine = phases_ref[step : step + 1, :HALF]
-            sine = phases_ref[step : step + 1, HALF:]
+            sine = phases_ref[step : step + 1, HALF:BAND]
             here = slice(step * CHUNK, (step + 1) * CHUNK)
             stacks[i % 2][here, :HALF] = (col_re * cosine - col_im * sine).astype(jnp.bfloat16)
             stacks[i % 2][here, HALF:] = (col_re * sine + col_im * cosine).astype(jnp.bfloat16)
 
     def multiply(i, quarter):
         here = slice(steps_of(quarter).start * CHUNK, steps_of(quarter).stop * CHUNK)
-        products[i % 2][here] = float_dot(stacks[i % 2][here], steps_ref[...])
+        products[i % 2][here] = float_dot(stacks[i % 2][here], step_value)
 
     def finish(i, quarter):
         centre = flat_ref[places[i]]
@@ -518,6 +548,7 @@
     for quarter in range(QUARTERS):
         turn(0, quarter)
     small[4].wait()
+    step_value = steps_ref[:, BAND:].astype(jnp.bfloat16)
     for i in range(count + 1):
         if i > 0:
             chunks[i - 1].wait()
@@ -534,23 +565,23 @@
         copy.wait()
 
 
-def mask_update(tiles, base, shifts, mask_params, step_value, phases):
+def mask_update(tiles, constants, mask_params):
     rows = mask_params.shape[0]
     stacked = STEPS * CHUNK
     hbm = pl.BlockSpec(memory_space=pltpu.HBM)
     return pl.pallas_call(
         update_kernel,
-        in_specs=[hbm] * 6,
+        in_specs=[hbm] * 3,
         out_specs=hbm,
         out_shape=jax.ShapeDtypeStruct((rows, MASK), jnp.float32),
         scratch_shapes=[
             pltpu.VMEM(tiles.shape, jnp.bfloat16),
             pltpu.VMEM((2, BAND, BAND), jnp.float32),
-            pltpu.VMEM(base.shape, jnp.float32),
-            pltpu.VMEM((1, 2 * BAND), jnp.float32),
+            pltpu.VMEM((rows, 2 * BAND), jnp.float32),
+            pltpu.VMEM((8, 2 * BAND), jnp.float32),
             pltpu.VMEM((rows, MASK), jnp.float32),
-            pltpu.VMEM(step_value.shape, jnp.bfloat16),
-            pltpu.VMEM(phases.shape, jnp.float32),
+            pltpu.VMEM((STEP, 2 * BAND), jnp.float32),
+            pltpu.VMEM((STEPS, 2 * BAND), jnp.float32),
             pltpu.VMEM((rows, HALF), jnp.float32),
             pltpu.VMEM((rows, HALF), jnp.float32),
             pltpu.VMEM((rows, STEP), jnp.float32),
@@ -562,7 +593,7 @@
         ],
         compiler_params=params(STREAM_LIMIT),
         name="mask_update",
-    )(tiles, base, shifts, mask_params, step_value, phases)
+    )(tiles, constants, mask_params)
 
 
 def exchange(values, axes):
@@ -574,32 +605,38 @@
     return jnp.broadcast_to(total[None], (copies,) + total.shape)
 
 
-def sum_tiles(tiles):
-    everyone = ("rows", "kern")
-    return exchange(summed(exchange(tiles, everyone), DEVICES), everyone)
+def total_kernel(parts_ref, out_ref):
+    total = jnp.sum(parts_ref[...].astype(jnp.float32), 0).astype(out_ref.dtype)
+    for owner in range(DEVICES):
+        out_ref[owner] = total
+
+
+def total_tiles(parts):
+    vmem = pl.BlockSpec(memory_space=pltpu.VMEM)
+    return pl.pallas_call(
+        total_kernel,
+        in_specs=[vmem],
+        out_specs=vmem,
+        out_shape=jax.ShapeDtypeStruct(parts.shape, parts.dtype),
+        compiler_params=params(),
+        cost_estimate=pl.CostEstimate(flops=10**10, bytes_accessed=2 * parts.size, transcendentals=0),
+        name="total_tiles",
+    )(parts)
 
 
 def local(mask_params, pupil_kernels, target_pattern):
     rows = mask_params.shape[0]
-    grid_rows = target_pattern.shape[0]
-    step_value = step_table()
-    phases = jnp.asarray(wide_table(np.arange(STEPS) * STEP, MASK, HALF))
-    mask_base = jnp.asarray(wide_table(np.arange(rows), MASK))
-    mask_transform = jnp.asarray(row_transform(rows))
-    mask_shifts = jnp.asarray(wide_table(np.arange(ROWS * KERN) * rows, MASK)[:, None, :])
-    grid_base = jnp.asarray(wide_table(np.arange(grid_rows), GRID))
-    grid_shifts = jnp.asarray(wide_table(np.arange(ROWS) * grid_rows, GRID)[:, None, :])
+    constants = jnp.asarray(constant_table(rows))
     column_map = jnp.asarray(coarse_map())
 
-    tiles, grid_table = mask_spectrum(
-        mask_params, jnp.asarray(step_value), phases, mask_transform, mask_shifts, grid_base, grid_shifts, target_pattern
-    )
-    fields, powers = coarse_fields(sum_tiles(tiles), pupil_kernels, grid_table, column_map)
+    everyone = ("rows", "kern")
+    tiles, grid_table = mask_spectrum(mask_params, constants, target_pattern)
+    spectrum = exchange(total_tiles(exchange(tiles, everyone)), everyone)
+    fields, powers = coarse_fields(spectrum, pupil_kernels, grid_table, column_map)
     adjoint = coarse_adjoint(exchange(powers, "kern"), jnp.asarray(interpolation()))
     gradient = spectrum_gradient(fields, exchange(adjoint, "kern"), pupil_kernels, grid_table, column_map)
-    return mask_update(
-        sum_tiles(gradient), mask_base, mask_shifts, mask_params, jnp.asarray(step_value.T), phases
-    )
+    gradient = exchange(summed(exchange(gradient, everyone), DEVICES), everyone)
+    return mask_update(gradient, constants, mask_params)
 
 
 def solution(mesh):

time: 119 us -> 116 us (0.975)
  Pallas kernels: 20.9 us -> 19.7 us
    pallas_call x1, Pallas kernels: 7.09 us -> 5.79 us  [mask_spectrum(): pl.pallas_call(spectrum_kernel, in_specs=[pl.BlockSpec(memory_space=pltpu...]
    pallas_call x1 -> x2, Pallas kernels: 6.95 us -> 7.04 us  [the longest x1 6.89 us: mask_update(): pl.pallas_call(update_kernel, in_specs=[hbm] * 3, out_specs=hbm, out_shap...]
where the time goes in v8:
time: 116 us
  blocking collectives  95.9 us (83%)
  Pallas kernels  19.7 us (17%)
    all_to_all x6, blocking collectives, exchange(): return lax.all_to_all(values, axes, 0, 0, tiled=True)  95.9 us
    pallas_call x1, Pallas kernels, mask_update(): pl.pallas_call(update_kernel, in_specs=[hbm] * 3, out_specs=hbm, out_shap...  6.89 us
    pallas_call x1, Pallas kernels, mask_spectrum(): pl.pallas_call(spectrum_kernel, in_specs=[pl.BlockSpec(memory_space=pltpu...  5.79 us
    pallas_call x1, Pallas kernels, coarse_adjoint(): pl.pallas_call(adjoint_kernel, in_specs=[pl.BlockSpec(memory_space=pltpu....  2.61 us

profile of v8, /device:TPU:1, one launch (start us, length us, event | category | flops | bytes accessed | tf_op | source)
XLA Modules:
  0.0 116.0 jit_solution(7330940878633634193)
XLA Ops:
  0.0 5.8 %mask_spectrum.1 = (bf16[128,8,128]{2,1,0:T(8,128)(2,1)S(1)}, bf16[512,512]{1,0:T(8,128)(2,1)S(1)}) custom-call(f32[128,16384]{1,0:T(8,128)} %mask_ref.3, f32[4928,512]{1,0:T(8,128)} %constant.9.clone.constant_ref, s32[256,512]{1,0:T(8,128)} %target_ref.1), custom_call_target="tpu_custom_call" | custom-call | tf_op jit(solution)/shard_map/mask_spectrum/pallas_call | solution.py:298
  5.8 22.3 %all_to_all.30.parts_ref = bf16[128,8,128]{2,1,0:T(8,128)(2,1)S(1)} all-to-all(bf16[128,8,128]{2,1,0:T(8,128)(2,1)S(1)} %get-tuple-element.9), channel_id=1, replica_groups=mesh['rows'=16,'kern'=8] {'rows','kern'}, dimensions={0} | all-to-all | bytes 524288 | tf_op jit(solution)/shard_map/all_to_all | solution.py:600
  28.2 0.0 copy-start
  28.2 0.0 copy-start.2
  28.2 0.2 total_tiles.1
  28.3 0.0 copy-start.1
  28.3 15.0 %all_to_all.31.tiles_ref = bf16[128,8,128]{2,1,0:T(8,128)(2,1)S(1)} all-to-all(bf16[128,8,128]{2,1,0:T(8,128)(2,1)S(1)} %total_tiles.1), channel_id=1, replica_groups=mesh['rows'=16,'kern'=8] {'rows','kern'}, dimensions={0} | all-to-all | bytes 524288 | tf_op jit(solution)/shard_map/all_to_all | solution.py:600
  43.3 0.0 copy-done
  43.3 0.0 copy-done.2
  43.3 2.0 %coarse_fields.1 = (f32[2,512,1024]{2,1,0:T(8,128)S(1)}, bf16[8,3,32,512]{3,2,1,0:T(8,128)(2,1)S(1)}) custom-call(bf16[128,8,128]{2,1,0:T(8,128)(2,1)S(1)} %all_to_all.31.tiles_ref, f32[2,2,2,256,256]{4,3,2,1,0:T(8,128)S(1)} %copy-done, bf16[512,512]{1,0:T(8,128)(2,1)S(1)} %get-tuple-element.10.grid_ref, bf16[512,1024]{1,0:T(8,128)(2,1)S(1)} %copy-done.2), custom_call_target="tpu_custom_call" | custom-call | tf_op jit(solution)/shard_map/coarse_fields/pallas_call | solution.py:366
  45.4 14.4 %all_to_all.32.parts_ref = bf16[8,3,32,512]{3,2,1,0:T(8,128)(2,1)S(1)} all-to-all(bf16[8,3,32,512]{3,2,1,0:T(8,128)(2,1)S(1)} %get-tuple-element.12), channel_id=1, replica_groups=mesh['rows'=16,'kern'=8] {'kern'}, dimensions={0} | all-to-all | bytes 1572864 | tf_op jit(solution)/shard_map/all_to_all | solution.py:600
  59.8 0.0 copy-done.1
  59.8 2.6 %coarse_adjoint.1 = bf16[8,2,32,512]{3,2,1,0:T(8,128)(2,1)S(1)} custom-call(bf16[8,3,32,512]{3,2,1,0:T(8,128)(2,1)S(1)} %all_to_all.32.parts_ref, bf16[512,4096]{1,0:T(8,128)(2,1)S(1)} %copy-done.1), custom_call_target="tpu_custom_call" | custom-call | tf_op jit(solution)/shard_map/coarse_adjoint/pallas_call | solution.py:414
  62.4 10.4 %all_to_all.33.adjoint_ref = bf16[8,2,32,512]{3,2,1,0:T(8,128)(2,1)S(1)} all-to-all(bf16[8,2,32,512]{3,2,1,0:T(8,128)(2,1)S(1)} %coarse_adjoint.1), channel_id=1, replica_groups=mesh['rows'=16,'kern'=8] {'kern'}, dimensions={0} | all-to-all | bytes 1048576 | tf_op jit(solution)/shard_map/all_to_all | solution.py:600
  72.8 2.2 %spectrum_gradient.1 = bf16[128,8,128]{2,1,0:T(8,128)(2,1)S(1)} custom-call(f32[2,512,1024]{2,1,0:T(8,128)S(1)} %get-tuple-element.11.field_ref, bf16[8,2,32,512]{3,2,1,0:T(8,128)(2,1)S(1)} %all_to_all.33.adjoint_ref, f32[2,2,2,256,256]{4,3,2,1,0:T(8,128)S(1)} %copy-done, bf16[512,512]{1,0:T(8,128)(2,1)S(1)} %get-tuple-element.10.grid_ref, ...), custom_call_target="tpu_custom_call" | custom-call | tf_op jit(solution)/shard_map/spectrum_gradient/pallas_call | solution.py:457
  75.0 18.7 %all_to_all.34 = bf16[128,8,128]{2,1,0:T(8,128)(2,1)S(1)} all-to-all(bf16[128,8,128]{2,1,0:T(8,128)(2,1)S(1)} %spectrum_gradient.1), channel_id=1, replica_groups=mesh['rows'=16,'kern'=8] {'rows','kern'}, dimensions={0} | all-to-all | bytes 524288 | tf_op jit(solution)/shard_map/all_to_all | solution.py:600
  93.7 0.1 reduce_sum.12
  93.9 15.0 %all_to_all.35.tiles_ref = bf16[128,8,128]{2,1,0:T(8,128)(2,1)S(1)} all-to-all(bf16[128,8,128]{2,1,0:T(8,128)(2,1)S(1)} %broadcast_in_dim.2), channel_id=1, replica_groups=mesh['rows'=16,'kern'=8] {'rows','kern'}, dimensions={0} | all-to-all | bytes 524288 | tf_op jit(solution)/shard_map/all_to_all | solution.py:600
  108.9 6.9 %mask_update.1 = f32[128,16384]{1,0:T(8,128)} custom-call(bf16[128,8,128]{2,1,0:T(8,128)(2,1)S(1)} %all_to_all.35.tiles_ref, f32[4928,512]{1,0:T(8,128)} %constant.9.clone.constant_ref, f32[128,16384]{1,0:T(8,128)} %mask_ref.3), custom_call_target="tpu_custom_call" | custom-call | tf_op jit(solution)/shard_map/mask_update/pallas_call | solution.py:572
  (1 shorter events, 0.0 us)
Async XLA Ops:
  28.2 15.2 %copy-start = (f32[2,2,2,256,256]{4,3,2,1,0:T(8,128)S(1)}, f32[2,2,2,256,256]{4,3,2,1,0:T(8,128)}, u32[]{:S(2)}) copy-start(f32[2,2,2,256,256]{4,3,2,1,0:T(8,128)} %pupil_ref.3) | copy-start | bytes 6291460
  28.2 15.2 %copy-start.2 = (bf16[512,1024]{1,0:T(8,128)(2,1)S(1)}, bf16[512,1024]{1,0:T(8,128)(2,1)}, u32[]{:S(2)}) copy-start(bf16[512,1024]{1,0:T(8,128)(2,1)} %constant.10.clone.map_ref) | copy-start | bytes 3145732
  28.3 31.5 %copy-start.1 = (bf16[512,4096]{1,0:T(8,128)(2,1)S(1)}, bf16[512,4096]{1,0:T(8,128)(2,1)}, u32[]{:S(2)}) copy-start(bf16[512,4096]{1,0:T(8,128)(2,1)} %constant.11.clone.matrix_ref) | copy-start | bytes 12582916

commit v9 on v8

--- a/solution.py
+++ b/solution.py
@@ -182,8 +182,8 @@
         pltpu.make_async_copy(source, target, sems.at[count + i])
         for i, (source, target) in enumerate(
             (
-                (constant_ref.at[table_rows("step")], steps_ref),
-                (constant_ref.at[table_rows("phase")], phases_ref),
+                (constant_ref.at[table_rows("step"), pl.ds(0, BAND)], steps_ref),
+                (constant_ref.at[table_rows("phase"), pl.ds(0, BAND)], phases_ref),
                 (constant_ref.at[table_rows("grid", lax.axis_index("rows") * grid_rows, grid_rows)], grid_rows_ref),
                 (target_ref, targets_ref),
                 (constant_ref.at[table_rows("transform")], bases_ref),
@@ -237,7 +237,7 @@
         transmit(0, quarter)
     small[0].wait()
     small[1].wait()
-    step_value = steps_ref[:, :BAND].astype(jnp.bfloat16)
+    step_value = steps_ref[...].astype(jnp.bfloat16)
     for i in range(count):
         if i + 1 < count:
             chunks[i + 1].wait()
@@ -306,8 +306,8 @@
         scratch_shapes=[
             pltpu.VMEM((2 * grid_rows, 2 * BAND), jnp.bfloat16),
             pltpu.VMEM((rows, MASK), jnp.float32),
-            pltpu.VMEM((STEP, 2 * BAND), jnp.float32),
-            pltpu.VMEM((STEPS, 2 * BAND), jnp.float32),
+            pltpu.VMEM((STEP, BAND), jnp.float32),
+            pltpu.VMEM((STEPS, BAND), jnp.float32),
             pltpu.VMEM((STEP, 2 * BAND), jnp.float32),
             pltpu.VMEM((8, 2 * BAND), jnp.float32),
             pltpu.VMEM((grid_rows, 2 * BAND), jnp.float32),
@@ -333,18 +333,17 @@
     load_tiles(tiles_ref, spec_ref)
     spec_re = spec_ref[0]
     spec_im = spec_ref[1]
+    table = jnp.concatenate([grid_ref[:rows, :BAND], grid_ref[:rows, BAND:]], 0)
     for member in range(members):
         for corner in range(2):
             kernel_re = pupil_ref[member, corner, 0]
             kernel_im = pupil_ref[member, corner, 1]
             amp_re = (kernel_re * spec_re - kernel_im * spec_im).astype(jnp.bfloat16)
             amp_im = (kernel_re * spec_im + kernel_im * spec_re).astype(jnp.bfloat16)
-            block = jnp.concatenate(
-                [jnp.concatenate([amp_re, amp_im], 1), jnp.concatenate([-amp_im, amp_re], 1)], 0
-            )
-            partial_ref[member, corner * rows : (corner + 1) * rows] = float_dot(grid_ref[:rows], block).astype(
-                jnp.bfloat16
-            )
+            product = float_dot(table, jnp.concatenate([amp_re, amp_im], 1))
+            here = slice(corner * rows, (corner + 1) * rows)
+            partial_ref[member, here, :BAND] = (product[:rows, :BAND] - product[rows:, BAND:]).astype(jnp.bfloat16)
+            partial_ref[member, here, BAND:] = (product[:rows, BAND:] + product[rows:, :BAND]).astype(jnp.bfloat16)
         field_ref[member] = float_dot(partial_ref[member], map_ref[...])
     for owner in range(KERN):
         power_ref[owner, 2] = grid_ref[rows + owner * slab : rows + (owner + 1) * slab]
@@ -425,6 +424,7 @@
     members = pupil_ref.shape[0]
     slab = adjoint_ref.shape[2]
     rows = slab * KERN
+    table = grid_ref[:rows].T
     for member in range(members):
         for corner in range(2):
             for owner in range(KERN):
@@ -437,7 +437,7 @@
                     ).astype(jnp.bfloat16)
         back_ref[member] = dot_last(weighted_ref[member], map_ref[...]).astype(jnp.bfloat16)
         for corner in range(2):
-            grads = dot_first(grid_ref[:rows], back_ref[member, corner * rows : (corner + 1) * rows])
+            grads = float_dot(table, back_ref[member, corner * rows : (corner + 1) * rows])
             grad_re = grads[:BAND, :BAND] + grads[BAND:, BAND:]
             grad_im = grads[:BAND, BAND:] - grads[BAND:, :BAND]
             kernel_re = pupil_ref[member, corner, 0]
@@ -492,8 +492,8 @@
                 (constant_ref.at[table_rows("base")], bases_ref),
                 (constant_ref.at[shift_group()], shifts_ref),
                 (tiles_ref, tile_ref),
-                (constant_ref.at[table_rows("phase")], phases_ref),
-                (constant_ref.at[table_rows("step")], steps_ref),
+                (constant_ref.at[table_rows("phase"), pl.ds(0, BAND)], phases_ref),
+                (constant_ref.at[table_rows("step"), pl.ds(BAND, BAND)], steps_ref),
             )
         )
     ]
@@ -548,7 +548,7 @@
     for quarter in range(QUARTERS):
         turn(0, quarter)
     small[4].wait()
-    step_value = steps_ref[:, BAND:].astype(jnp.bfloat16)
+    step_value = steps_ref[...].astype(jnp.bfloat16)
     for i in range(count + 1):
         if i > 0:
             chunks[i - 1].wait()
@@ -580,8 +580,8 @@
             pltpu.VMEM((rows, 2 * BAND), jnp.float32),
             pltpu.VMEM((8, 2 * BAND), jnp.float32),
             pltpu.VMEM((rows, MASK), jnp.float32),
-            pltpu.VMEM((STEP, 2 * BAND), jnp.float32),
-            pltpu.VMEM((STEPS, 2 * BAND), jnp.float32),
+            pltpu.VMEM((STEP, BAND), jnp.float32),
+            pltpu.VMEM((STEPS, BAND), jnp.float32),
             pltpu.VMEM((rows, HALF), jnp.float32),
             pltpu.VMEM((rows, HALF), jnp.float32),
             pltpu.VMEM((rows, STEP), jnp.float32),
@@ -629,7 +629,7 @@
     constants = jnp.asarray(constant_table(rows))
     column_map = jnp.asarray(coarse_map())
 
-    everyone = ("rows", "kern")
+    everyone = ("kern", "rows")
     tiles, grid_table = mask_spectrum(mask_params, constants, target_pattern)
     spectrum = exchange(total_tiles(exchange(tiles, everyone)), everyone)
     fields, powers = coarse_fields(spectrum, pupil_kernels, grid_table, column_map)

time: 116 us -> 116 us (level)
  no operation moved by 1% of the time
where the time goes in v9:
time: 116 us
  blocking collectives  95.8 us (83%)
  Pallas kernels  19.7 us (17%)
    all_to_all x6, blocking collectives, exchange(): return lax.all_to_all(values, axes, 0, 0, tiled=True)  95.8 us
    pallas_call x1, Pallas kernels, mask_update(): pl.pallas_call(update_kernel, in_specs=[hbm] * 3, out_specs=hbm, out_shap...  6.89 us
    pallas_call x1, Pallas kernels, mask_spectrum(): pl.pallas_call(spectrum_kernel, in_specs=[pl.BlockSpec(memory_space=pltpu...  5.69 us
    pallas_call x1, Pallas kernels, coarse_adjoint(): pl.pallas_call(adjoint_kernel, in_specs=[pl.BlockSpec(memory_space=pltpu....  2.61 us

profile of v9, /device:TPU:1, one launch (start us, length us, event | category | flops | bytes accessed | tf_op | source)
XLA Modules:
  0.0 115.9 jit_solution(4958836238891690191)
XLA Ops:
  0.0 5.7 %mask_spectrum.1 = (bf16[128,8,128]{2,1,0:T(8,128)(2,1)S(1)}, bf16[512,512]{1,0:T(8,128)(2,1)S(1)}) custom-call(f32[128,16384]{1,0:T(8,128)} %mask_ref.3, f32[4928,512]{1,0:T(8,128)} %constant.9.clone.constant_ref, s32[256,512]{1,0:T(8,128)} %target_ref.1), custom_call_target="tpu_custom_call" | custom-call | tf_op jit(solution)/shard_map/mask_spectrum/pallas_call | solution.py:298
  5.7 22.6 %all_to_all.30.parts_ref = bf16[128,8,128]{2,1,0:T(8,128)(2,1)S(1)} all-to-all(bf16[128,8,128]{2,1,0:T(8,128)(2,1)S(1)} %get-tuple-element.9), channel_id=1, replica_groups=mesh['rows'=16,'kern'=8] {'kern','rows'}, dimensions={0} | all-to-all | bytes 524288 | tf_op jit(solution)/shard_map/all_to_all | solution.py:600
  28.3 0.0 copy-start
  28.3 0.0 copy-start.2
  28.3 0.2 total_tiles.1
  28.4 0.0 copy-start.1
  28.4 15.1 %all_to_all.31.tiles_ref = bf16[128,8,128]{2,1,0:T(8,128)(2,1)S(1)} all-to-all(bf16[128,8,128]{2,1,0:T(8,128)(2,1)S(1)} %total_tiles.1), channel_id=1, replica_groups=mesh['rows'=16,'kern'=8] {'kern','rows'}, dimensions={0} | all-to-all | bytes 524288 | tf_op jit(solution)/shard_map/all_to_all | solution.py:600
  43.5 0.0 copy-done
  43.5 0.0 copy-done.2
  43.5 2.2 %coarse_fields.1 = (f32[2,512,1024]{2,1,0:T(8,128)S(1)}, bf16[8,3,32,512]{3,2,1,0:T(8,128)(2,1)S(1)}) custom-call(bf16[128,8,128]{2,1,0:T(8,128)(2,1)S(1)} %all_to_all.31.tiles_ref, f32[2,2,2,256,256]{4,3,2,1,0:T(8,128)S(1)} %copy-done, bf16[512,512]{1,0:T(8,128)(2,1)S(1)} %get-tuple-element.10.grid_ref, bf16[512,1024]{1,0:T(8,128)(2,1)S(1)} %copy-done.2), custom_call_target="tpu_custom_call" | custom-call | tf_op jit(solution)/shard_map/coarse_fields/pallas_call | solution.py:365
  45.7 14.4 %all_to_all.32.parts_ref = bf16[8,3,32,512]{3,2,1,0:T(8,128)(2,1)S(1)} all-to-all(bf16[8,3,32,512]{3,2,1,0:T(8,128)(2,1)S(1)} %get-tuple-element.12), channel_id=1, replica_groups=mesh['rows'=16,'kern'=8] {'kern'}, dimensions={0} | all-to-all | bytes 1572864 | tf_op jit(solution)/shard_map/all_to_all | solution.py:600
  60.1 0.0 copy-done.1
  60.2 2.6 %coarse_adjoint.1 = bf16[8,2,32,512]{3,2,1,0:T(8,128)(2,1)S(1)} custom-call(bf16[8,3,32,512]{3,2,1,0:T(8,128)(2,1)S(1)} %all_to_all.32.parts_ref, bf16[512,4096]{1,0:T(8,128)(2,1)S(1)} %copy-done.1), custom_call_target="tpu_custom_call" | custom-call | tf_op jit(solution)/shard_map/coarse_adjoint/pallas_call | solution.py:413
  62.8 11.5 %all_to_all.33.adjoint_ref = bf16[8,2,32,512]{3,2,1,0:T(8,128)(2,1)S(1)} all-to-all(bf16[8,2,32,512]{3,2,1,0:T(8,128)(2,1)S(1)} %coarse_adjoint.1), channel_id=1, replica_groups=mesh['rows'=16,'kern'=8] {'kern'}, dimensions={0} | all-to-all | bytes 1048576 | tf_op jit(solution)/shard_map/all_to_all | solution.py:600
  74.3 2.2 %spectrum_gradient.1 = bf16[128,8,128]{2,1,0:T(8,128)(2,1)S(1)} custom-call(f32[2,512,1024]{2,1,0:T(8,128)S(1)} %get-tuple-element.11.field_ref, bf16[8,2,32,512]{3,2,1,0:T(8,128)(2,1)S(1)} %all_to_all.33.adjoint_ref, f32[2,2,2,256,256]{4,3,2,1,0:T(8,128)S(1)} %copy-done, bf16[512,512]{1,0:T(8,128)(2,1)S(1)} %get-tuple-element.10.grid_ref, ...), custom_call_target="tpu_custom_call" | custom-call | tf_op jit(solution)/shard_map/spectrum_gradient/pallas_call | solution.py:457
  76.5 17.1 %all_to_all.34 = bf16[128,8,128]{2,1,0:T(8,128)(2,1)S(1)} all-to-all(bf16[128,8,128]{2,1,0:T(8,128)(2,1)S(1)} %spectrum_gradient.1), channel_id=1, replica_groups=mesh['rows'=16,'kern'=8] {'kern','rows'}, dimensions={0} | all-to-all | bytes 524288 | tf_op jit(solution)/shard_map/all_to_all | solution.py:600
  93.6 0.1 reduce_sum.12
  93.8 15.0 %all_to_all.35.tiles_ref = bf16[128,8,128]{2,1,0:T(8,128)(2,1)S(1)} all-to-all(bf16[128,8,128]{2,1,0:T(8,128)(2,1)S(1)} %broadcast_in_dim.2), channel_id=1, replica_groups=mesh['rows'=16,'kern'=8] {'kern','rows'}, dimensions={0} | all-to-all | bytes 524288 | tf_op jit(solution)/shard_map/all_to_all | solution.py:600
  108.8 6.9 %mask_update.1 = f32[128,16384]{1,0:T(8,128)} custom-call(bf16[128,8,128]{2,1,0:T(8,128)(2,1)S(1)} %all_to_all.35.tiles_ref, f32[4928,512]{1,0:T(8,128)} %constant.9.clone.constant_ref, f32[128,16384]{1,0:T(8,128)} %mask_ref.3), custom_call_target="tpu_custom_call" | custom-call | tf_op jit(solution)/shard_map/mask_update/pallas_call | solution.py:572
  (1 shorter events, 0.0 us)
Async XLA Ops:
  28.3 15.3 %copy-start = (f32[2,2,2,256,256]{4,3,2,1,0:T(8,128)S(1)}, f32[2,2,2,256,256]{4,3,2,1,0:T(8,128)}, u32[]{:S(2)}) copy-start(f32[2,2,2,256,256]{4,3,2,1,0:T(8,128)} %pupil_ref.3) | copy-start | bytes 6291460
  28.3 15.3 %copy-start.2 = (bf16[512,1024]{1,0:T(8,128)(2,1)S(1)}, bf16[512,1024]{1,0:T(8,128)(2,1)}, u32[]{:S(2)}) copy-start(bf16[512,1024]{1,0:T(8,128)(2,1)} %constant.10.clone.map_ref) | copy-start | bytes 3145732
  28.4 31.7 %copy-start.1 = (bf16[512,4096]{1,0:T(8,128)(2,1)S(1)}, bf16[512,4096]{1,0:T(8,128)(2,1)}, u32[]{:S(2)}) copy-start(bf16[512,4096]{1,0:T(8,128)(2,1)} %constant.11.clone.matrix_ref) | copy-start | bytes 12582916

commit v10 on v9

--- a/solution.py
+++ b/solution.py
@@ -20,6 +20,7 @@
 DEVICES = ROWS * KERN
 CHUNK = 16
 QUARTERS = 4
+QUARTER = MASK // QUARTERS
 
 steepness = 4.0
 threshold = 0.75
@@ -175,8 +176,17 @@
     products = (product_a, product_b)
     count = rows // CHUNK
     places = [pl.ds(i * CHUNK, CHUNK) for i in range(count)]
-    chunks = [
-        pltpu.make_async_copy(mask_ref.at[places[i]], held_ref.at[places[i]], sems.at[i]) for i in range(count)
+    chunks = [None] + [
+        pltpu.make_async_copy(mask_ref.at[places[i]], held_ref.at[places[i]], sems.at[i]) for i in range(1, count)
+    ]
+    columns = [pl.ds(quarter * QUARTER, QUARTER) for quarter in range(QUARTERS)]
+    heads = [
+        pltpu.make_async_copy(
+            mask_ref.at[places[0], columns[quarter]],
+            held_ref.at[places[0], columns[quarter]],
+            sems.at[count + 7 + quarter],
+        )
+        for quarter in range(QUARTERS)
     ]
     small = [
         pltpu.make_async_copy(source, target, sems.at[count + i])
@@ -192,7 +202,8 @@
         )
     ]
     grid_copy = pltpu.make_async_copy(grid_ref, grid_out_ref, sems.at[count + 6])
-    chunks[0].start()
+    for copy in heads:
+        copy.start()
     small[0].start()
     small[1].start()
     chunks[1].start()
@@ -232,8 +243,8 @@
         re_ref[places[i]] = total_re if quarter == 0 else re_ref[places[i]] + total_re
         im_ref[places[i]] = total_im if quarter == 0 else im_ref[places[i]] + total_im
 
-    chunks[0].wait()
     for quarter in range(QUARTERS):
+        heads[quarter].wait()
         transmit(0, quarter)
     small[0].wait()
     small[1].wait()
@@ -319,7 +330,7 @@
             pltpu.VMEM((rows, HALF), jnp.float32),
             pltpu.VMEM((rows, HALF), jnp.float32),
             pltpu.VMEM((rows, HALF), jnp.float32),
-            pltpu.SemaphoreType.DMA((rows // CHUNK + 7,)),
+            pltpu.SemaphoreType.DMA((rows // CHUNK + 7 + QUARTERS,)),
         ],
         compiler_params=params(STREAM_LIMIT),
         name="mask_spectrum",
@@ -333,17 +344,18 @@
     load_tiles(tiles_ref, spec_ref)
     spec_re = spec_ref[0]
     spec_im = spec_ref[1]
-    table = jnp.concatenate([grid_ref[:rows, :BAND], grid_ref[:rows, BAND:]], 0)
     for member in range(members):
         for corner in range(2):
             kernel_re = pupil_ref[member, corner, 0]
             kernel_im = pupil_ref[member, corner, 1]
             amp_re = (kernel_re * spec_re - kernel_im * spec_im).astype(jnp.bfloat16)
             amp_im = (kernel_re * spec_im + kernel_im * spec_re).astype(jnp.bfloat16)
-            product = float_dot(table, jnp.concatenate([amp_re, amp_im], 1))
-            here = slice(corner * rows, (corner + 1) * rows)
-            partial_ref[member, here, :BAND] = (product[:rows, :BAND] - product[rows:, BAND:]).astype(jnp.bfloat16)
-            partial_ref[member, here, BAND:] = (product[:rows, BAND:] + product[rows:, :BAND]).astype(jnp.bfloat16)
+            block = jnp.concatenate(
+                [jnp.concatenate([amp_re, amp_im], 1), jnp.concatenate([-amp_im, amp_re], 1)], 0
+            )
+            partial_ref[member, corner * rows : (corner + 1) * rows] = float_dot(grid_ref[:rows], block).astype(
+                jnp.bfloat16
+            )
         field_ref[member] = float_dot(partial_ref[member], map_ref[...])
     for owner in range(KERN):
         power_ref[owner, 2] = grid_ref[rows + owner * slab : rows + (owner + 1) * slab]
@@ -481,12 +493,18 @@
     chunks = [
         pltpu.make_async_copy(mask_ref.at[places[i]], held_ref.at[places[i]], sems.at[i]) for i in range(count)
     ]
+    columns = [pl.ds(quarter * QUARTER, QUARTER) for quarter in range(QUARTERS)]
     results = [
-        pltpu.make_async_copy(held_ref.at[places[i]], out_ref.at[places[i]], sems.at[count + i])
+        pltpu.make_async_copy(
+            held_ref.at[places[i], columns[quarter]],
+            out_ref.at[places[i], columns[quarter]],
+            sems.at[count + 5 + QUARTERS * i + quarter],
+        )
         for i in range(count)
+        for quarter in range(QUARTERS)
     ]
     small = [
-        pltpu.make_async_copy(source, target, sems.at[2 * count + i])
+        pltpu.make_async_copy(source, target, sems.at[count + i])
         for i, (source, target) in enumerate(
             (
                 (constant_ref.at[table_rows("base")], bases_ref),
@@ -559,8 +577,7 @@
                 turn(i + 1, quarter)
             if i > 0:
                 finish(i - 1, quarter)
-        if i > 0:
-            results[i - 1].start()
+                results[QUARTERS * (i - 1) + quarter].start()
     for copy in results:
         copy.wait()
 
@@ -589,7 +606,7 @@
             pltpu.VMEM((stacked, BAND), jnp.bfloat16),
             pltpu.VMEM((stacked, STEP), jnp.float32),
             pltpu.VMEM((stacked, STEP), jnp.float32),
-            pltpu.SemaphoreType.DMA((2 * (rows // CHUNK) + 5,)),
+            pltpu.SemaphoreType.DMA(((QUARTERS + 1) * (rows // CHUNK) + 5,)),
         ],
         compiler_params=params(STREAM_LIMIT),
         name="mask_update",

time: 116 us -> 116 us (level)
  no operation moved by 1% of the time
where the time goes in v10:
time: 116 us
  blocking collectives  95.8 us (83%)
  Pallas kernels  19.6 us (17%)
    all_to_all x6, blocking collectives, exchange(): return lax.all_to_all(values, axes, 0, 0, tiled=True)  95.8 us
    pallas_call x1, Pallas kernels, mask_update(): pl.pallas_call(update_kernel, in_specs=[hbm] * 3, out_specs=hbm, out_shap...  6.88 us
    pallas_call x1, Pallas kernels, mask_spectrum(): pl.pallas_call(spectrum_kernel, in_specs=[pl.BlockSpec(memory_space=pltpu...  5.74 us
    pallas_call x1, Pallas kernels, coarse_adjoint(): pl.pallas_call(adjoint_kernel, in_specs=[pl.BlockSpec(memory_space=pltpu....  2.61 us

profile of v10, /device:TPU:1, one launch (start us, length us, event | category | flops | bytes accessed | tf_op | source)
XLA Modules:
  0.0 115.8 jit_solution(4414339823838400930)
XLA Ops:
  0.0 5.7 %mask_spectrum.1 = (bf16[128,8,128]{2,1,0:T(8,128)(2,1)S(1)}, bf16[512,512]{1,0:T(8,128)(2,1)S(1)}) custom-call(f32[128,16384]{1,0:T(8,128)} %mask_ref.3, f32[4928,512]{1,0:T(8,128)} %constant.9.clone.constant_ref, s32[256,512]{1,0:T(8,128)} %target_ref.1), custom_call_target="tpu_custom_call" | custom-call | tf_op jit(solution)/shard_map/mask_spectrum/pallas_call | solution.py:309
  5.7 22.6 %all_to_all.30.parts_ref = bf16[128,8,128]{2,1,0:T(8,128)(2,1)S(1)} all-to-all(bf16[128,8,128]{2,1,0:T(8,128)(2,1)S(1)} %get-tuple-element.9), channel_id=1, replica_groups=mesh['rows'=16,'kern'=8] {'kern','rows'}, dimensions={0} | all-to-all | bytes 524288 | tf_op jit(solution)/shard_map/all_to_all | solution.py:617
  28.3 0.0 copy-start
  28.3 0.0 copy-start.2
  28.3 0.2 total_tiles.1
  28.5 0.0 copy-start.1
  28.5 15.1 %all_to_all.31.tiles_ref = bf16[128,8,128]{2,1,0:T(8,128)(2,1)S(1)} all-to-all(bf16[128,8,128]{2,1,0:T(8,128)(2,1)S(1)} %total_tiles.1), channel_id=1, replica_groups=mesh['rows'=16,'kern'=8] {'kern','rows'}, dimensions={0} | all-to-all | bytes 524288 | tf_op jit(solution)/shard_map/all_to_all | solution.py:617
  43.6 0.0 copy-done
  43.6 0.0 copy-done.2
  43.6 2.0 %coarse_fields.1 = (f32[2,512,1024]{2,1,0:T(8,128)S(1)}, bf16[8,3,32,512]{3,2,1,0:T(8,128)(2,1)S(1)}) custom-call(bf16[128,8,128]{2,1,0:T(8,128)(2,1)S(1)} %all_to_all.31.tiles_ref, f32[2,2,2,256,256]{4,3,2,1,0:T(8,128)S(1)} %copy-done, bf16[512,512]{1,0:T(8,128)(2,1)S(1)} %get-tuple-element.10.grid_ref, bf16[512,1024]{1,0:T(8,128)(2,1)S(1)} %copy-done.2), custom_call_target="tpu_custom_call" | custom-call | tf_op jit(solution)/shard_map/coarse_fields/pallas_call | solution.py:377
  45.6 14.4 %all_to_all.32.parts_ref = bf16[8,3,32,512]{3,2,1,0:T(8,128)(2,1)S(1)} all-to-all(bf16[8,3,32,512]{3,2,1,0:T(8,128)(2,1)S(1)} %get-tuple-element.12), channel_id=1, replica_groups=mesh['rows'=16,'kern'=8] {'kern'}, dimensions={0} | all-to-all | bytes 1572864 | tf_op jit(solution)/shard_map/all_to_all | solution.py:617
  60.0 0.0 copy-done.1
  60.0 2.6 %coarse_adjoint.1 = bf16[8,2,32,512]{3,2,1,0:T(8,128)(2,1)S(1)} custom-call(bf16[8,3,32,512]{3,2,1,0:T(8,128)(2,1)S(1)} %all_to_all.32.parts_ref, bf16[512,4096]{1,0:T(8,128)(2,1)S(1)} %copy-done.1), custom_call_target="tpu_custom_call" | custom-call | tf_op jit(solution)/shard_map/coarse_adjoint/pallas_call | solution.py:425
  62.7 11.0 %all_to_all.33.adjoint_ref = bf16[8,2,32,512]{3,2,1,0:T(8,128)(2,1)S(1)} all-to-all(bf16[8,2,32,512]{3,2,1,0:T(8,128)(2,1)S(1)} %coarse_adjoint.1), channel_id=1, replica_groups=mesh['rows'=16,'kern'=8] {'kern'}, dimensions={0} | all-to-all | bytes 1048576 | tf_op jit(solution)/shard_map/all_to_all | solution.py:617
  73.7 2.2 %spectrum_gradient.1 = bf16[128,8,128]{2,1,0:T(8,128)(2,1)S(1)} custom-call(f32[2,512,1024]{2,1,0:T(8,128)S(1)} %get-tuple-element.11.field_ref, bf16[8,2,32,512]{3,2,1,0:T(8,128)(2,1)S(1)} %all_to_all.33.adjoint_ref, f32[2,2,2,256,256]{4,3,2,1,0:T(8,128)S(1)} %copy-done, bf16[512,512]{1,0:T(8,128)(2,1)S(1)} %get-tuple-element.10.grid_ref, ...), custom_call_target="tpu_custom_call" | custom-call | tf_op jit(solution)/shard_map/spectrum_gradient/pallas_call | solution.py:469
  75.9 17.6 %all_to_all.34 = bf16[128,8,128]{2,1,0:T(8,128)(2,1)S(1)} all-to-all(bf16[128,8,128]{2,1,0:T(8,128)(2,1)S(1)} %spectrum_gradient.1), channel_id=1, replica_groups=mesh['rows'=16,'kern'=8] {'kern','rows'}, dimensions={0} | all-to-all | bytes 524288 | tf_op jit(solution)/shard_map/all_to_all | solution.py:617
  93.5 0.1 reduce_sum.12
  93.7 15.0 %all_to_all.35.tiles_ref = bf16[128,8,128]{2,1,0:T(8,128)(2,1)S(1)} all-to-all(bf16[128,8,128]{2,1,0:T(8,128)(2,1)S(1)} %broadcast_in_dim.2), channel_id=1, replica_groups=mesh['rows'=16,'kern'=8] {'kern','rows'}, dimensions={0} | all-to-all | bytes 524288 | tf_op jit(solution)/shard_map/all_to_all | solution.py:617
  108.7 6.9 %mask_update.1 = f32[128,16384]{1,0:T(8,128)} custom-call(bf16[128,8,128]{2,1,0:T(8,128)(2,1)S(1)} %all_to_all.35.tiles_ref, f32[4928,512]{1,0:T(8,128)} %constant.9.clone.constant_ref, f32[128,16384]{1,0:T(8,128)} %mask_ref.3), custom_call_target="tpu_custom_call" | custom-call | tf_op jit(solution)/shard_map/mask_update/pallas_call | solution.py:589
  (1 shorter events, 0.0 us)
Async XLA Ops:
  28.3 15.3 %copy-start = (f32[2,2,2,256,256]{4,3,2,1,0:T(8,128)S(1)}, f32[2,2,2,256,256]{4,3,2,1,0:T(8,128)}, u32[]{:S(2)}) copy-start(f32[2,2,2,256,256]{4,3,2,1,0:T(8,128)} %pupil_ref.3) | copy-start | bytes 6291460
  28.3 15.3 %copy-start.2 = (bf16[512,1024]{1,0:T(8,128)(2,1)S(1)}, bf16[512,1024]{1,0:T(8,128)(2,1)}, u32[]{:S(2)}) copy-start(bf16[512,1024]{1,0:T(8,128)(2,1)} %constant.10.clone.map_ref) | copy-start | bytes 3145732
  28.5 31.6 %copy-start.1 = (bf16[512,4096]{1,0:T(8,128)(2,1)S(1)}, bf16[512,4096]{1,0:T(8,128)(2,1)}, u32[]{:S(2)}) copy-start(bf16[512,4096]{1,0:T(8,128)(2,1)} %constant.11.clone.matrix_ref) | copy-start | bytes 12582916

commit v11 on v10

--- a/solution.py
+++ b/solution.py
@@ -447,7 +447,7 @@
                     weighted_ref[member, at : at + slab, columns] = (
                         field_ref[member, at : at + slab, columns] * adjoint
                     ).astype(jnp.bfloat16)
-        back_ref[member] = dot_last(weighted_ref[member], map_ref[...]).astype(jnp.bfloat16)
+        back_ref[member] = float_dot(weighted_ref[member], map_ref[...]).astype(jnp.bfloat16)
         for corner in range(2):
             grads = float_dot(table, back_ref[member, corner * rows : (corner + 1) * rows])
             grad_re = grads[:BAND, :BAND] + grads[BAND:, BAND:]
@@ -531,8 +531,8 @@
     col_im = by_sin[:, :BAND] + by_cos[:, BAND:]
     flat_ref[...] = jnp.broadcast_to(col_re[:, HALF : HALF + 1] * (1.0 / MASK), flat_ref.shape)
     mirror = conjugate_mirror()
-    high, low = split(jnp.concatenate([col_re[:, HALF:], col_im[:, HALF:]], 1))
-    other = float_dot(high, mirror) + float_dot(low, mirror)
+    right = jnp.concatenate([col_re[:, HALF:], col_im[:, HALF:]], 1).astype(jnp.bfloat16)
+    other = float_dot(right, mirror)
     re_ref[...] = col_re[:, :HALF] + other[:, :HALF]
     im_ref[...] = col_im[:, :HALF] + other[:, HALF:]
 
@@ -651,7 +651,8 @@
     spectrum = exchange(total_tiles(exchange(tiles, everyone)), everyone)
     fields, powers = coarse_fields(spectrum, pupil_kernels, grid_table, column_map)
     adjoint = coarse_adjoint(exchange(powers, "kern"), jnp.asarray(interpolation()))
-    gradient = spectrum_gradient(fields, exchange(adjoint, "kern"), pupil_kernels, grid_table, column_map)
+    column_back = jnp.asarray(coarse_map().T.copy())
+    gradient = spectrum_gradient(fields, exchange(adjoint, "kern"), pupil_kernels, grid_table, column_back)
     gradient = exchange(summed(exchange(gradient, everyone), DEVICES), everyone)
     return mask_update(gradient, constants, mask_params)
 

time: 116 us -> 116 us (level)
  no operation moved by 1% of the time
where the time goes in v11:
time: 116 us
  blocking collectives  95.7 us (82%)
  Pallas kernels  19.7 us (17%)
    all_to_all x6, blocking collectives, exchange(): return lax.all_to_all(values, axes, 0, 0, tiled=True)  95.7 us
    pallas_call x1, Pallas kernels, mask_update(): pl.pallas_call(update_kernel, in_specs=[hbm] * 3, out_specs=hbm, out_shap...  6.95 us
    pallas_call x1, Pallas kernels, mask_spectrum(): pl.pallas_call(spectrum_kernel, in_specs=[pl.BlockSpec(memory_space=pltpu...  5.74 us
    pallas_call x1, Pallas kernels, coarse_adjoint(): pl.pallas_call(adjoint_kernel, in_specs=[pl.BlockSpec(memory_space=pltpu....  2.61 us

profile of v11, /device:TPU:1, one launch (start us, length us, event | category | flops | bytes accessed | tf_op | source)
XLA Modules:
  0.0 115.8 jit_solution(6824611198387913704)
XLA Ops:
  0.0 5.7 %mask_spectrum.1 = (bf16[128,8,128]{2,1,0:T(8,128)(2,1)S(1)}, bf16[512,512]{1,0:T(8,128)(2,1)S(1)}) custom-call(f32[128,16384]{1,0:T(8,128)} %mask_ref.3, f32[4928,512]{1,0:T(8,128)} %constant.11.clone.constant_ref, s32[256,512]{1,0:T(8,128)} %target_ref.1), custom_call_target="tpu_custom_call" | custom-call | tf_op jit(solution)/shard_map/mask_spectrum/pallas_call | solution.py:309
  5.7 22.6 %all_to_all.30.parts_ref = bf16[128,8,128]{2,1,0:T(8,128)(2,1)S(1)} all-to-all(bf16[128,8,128]{2,1,0:T(8,128)(2,1)S(1)} %get-tuple-element.9), channel_id=1, replica_groups=mesh['rows'=16,'kern'=8] {'kern','rows'}, dimensions={0} | all-to-all | bytes 524288 | tf_op jit(solution)/shard_map/all_to_all | solution.py:617
  28.3 0.0 copy-start
  28.3 0.0 copy-start.3
  28.3 0.2 total_tiles.1
  28.5 0.0 copy-start.1
  28.5 0.0 copy-start.2
  28.5 15.1 %all_to_all.31.tiles_ref = bf16[128,8,128]{2,1,0:T(8,128)(2,1)S(1)} all-to-all(bf16[128,8,128]{2,1,0:T(8,128)(2,1)S(1)} %total_tiles.1), channel_id=1, replica_groups=mesh['rows'=16,'kern'=8] {'kern','rows'}, dimensions={0} | all-to-all | bytes 524288 | tf_op jit(solution)/shard_map/all_to_all | solution.py:617
  43.6 0.0 copy-done
  43.6 0.0 copy-done.3
  43.6 2.0 %coarse_fields.1 = (f32[2,512,1024]{2,1,0:T(8,128)S(1)}, bf16[8,3,32,512]{3,2,1,0:T(8,128)(2,1)S(1)}) custom-call(bf16[128,8,128]{2,1,0:T(8,128)(2,1)S(1)} %all_to_all.31.tiles_ref, f32[2,2,2,256,256]{4,3,2,1,0:T(8,128)S(1)} %copy-done, bf16[512,512]{1,0:T(8,128)(2,1)S(1)} %get-tuple-element.10.grid_ref, bf16[512,1024]{1,0:T(8,128)(2,1)S(1)} %copy-done.3), custom_call_target="tpu_custom_call" | custom-call | tf_op jit(solution)/shard_map/coarse_fields/pallas_call | solution.py:377
  45.6 14.4 %all_to_all.32.parts_ref = bf16[8,3,32,512]{3,2,1,0:T(8,128)(2,1)S(1)} all-to-all(bf16[8,3,32,512]{3,2,1,0:T(8,128)(2,1)S(1)} %get-tuple-element.12), channel_id=1, replica_groups=mesh['rows'=16,'kern'=8] {'kern'}, dimensions={0} | all-to-all | bytes 1572864 | tf_op jit(solution)/shard_map/all_to_all | solution.py:617
  60.1 0.0 copy-done.1
  60.1 2.6 %coarse_adjoint.1 = bf16[8,2,32,512]{3,2,1,0:T(8,128)(2,1)S(1)} custom-call(bf16[8,3,32,512]{3,2,1,0:T(8,128)(2,1)S(1)} %all_to_all.32.parts_ref, bf16[512,4096]{1,0:T(8,128)(2,1)S(1)} %copy-done.1), custom_call_target="tpu_custom_call" | custom-call | tf_op jit(solution)/shard_map/coarse_adjoint/pallas_call | solution.py:425
  62.7 11.5 %all_to_all.33.adjoint_ref = bf16[8,2,32,512]{3,2,1,0:T(8,128)(2,1)S(1)} all-to-all(bf16[8,2,32,512]{3,2,1,0:T(8,128)(2,1)S(1)} %coarse_adjoint.1), channel_id=1, replica_groups=mesh['rows'=16,'kern'=8] {'kern'}, dimensions={0} | all-to-all | bytes 1048576 | tf_op jit(solution)/shard_map/all_to_all | solution.py:617
  74.2 0.0 copy-done.2
  74.2 2.2 %spectrum_gradient.1 = bf16[128,8,128]{2,1,0:T(8,128)(2,1)S(1)} custom-call(f32[2,512,1024]{2,1,0:T(8,128)S(1)} %get-tuple-element.11.field_ref, bf16[8,2,32,512]{3,2,1,0:T(8,128)(2,1)S(1)} %all_to_all.33.adjoint_ref, f32[2,2,2,256,256]{4,3,2,1,0:T(8,128)S(1)} %copy-done, bf16[512,512]{1,0:T(8,128)(2,1)S(1)} %get-tuple-element.10.grid_ref, ...), custom_call_target="tpu_custom_call" | custom-call | tf_op jit(solution)/shard_map/spectrum_gradient/pallas_call | solution.py:469
  76.4 17.1 %all_to_all.34 = bf16[128,8,128]{2,1,0:T(8,128)(2,1)S(1)} all-to-all(bf16[128,8,128]{2,1,0:T(8,128)(2,1)S(1)} %spectrum_gradient.1), channel_id=1, replica_groups=mesh['rows'=16,'kern'=8] {'kern','rows'}, dimensions={0} | all-to-all | bytes 524288 | tf_op jit(solution)/shard_map/all_to_all | solution.py:617
  93.5 0.1 reduce_sum.12
  93.7 15.0 %all_to_all.35.tiles_ref = bf16[128,8,128]{2,1,0:T(8,128)(2,1)S(1)} all-to-all(bf16[128,8,128]{2,1,0:T(8,128)(2,1)S(1)} %broadcast_in_dim.2), channel_id=1, replica_groups=mesh['rows'=16,'kern'=8] {'kern','rows'}, dimensions={0} | all-to-all | bytes 524288 | tf_op jit(solution)/shard_map/all_to_all | solution.py:617
  108.7 7.0 %mask_update.1 = f32[128,16384]{1,0:T(8,128)} custom-call(bf16[128,8,128]{2,1,0:T(8,128)(2,1)S(1)} %all_to_all.35.tiles_ref, f32[4928,512]{1,0:T(8,128)} %constant.11.clone.constant_ref, f32[128,16384]{1,0:T(8,128)} %mask_ref.3), custom_call_target="tpu_custom_call" | custom-call | tf_op jit(solution)/shard_map/mask_update/pallas_call | solution.py:589
  (1 shorter events, 0.0 us)
Async XLA Ops:
  28.3 15.3 %copy-start = (f32[2,2,2,256,256]{4,3,2,1,0:T(8,128)S(1)}, f32[2,2,2,256,256]{4,3,2,1,0:T(8,128)}, u32[]{:S(2)}) copy-start(f32[2,2,2,256,256]{4,3,2,1,0:T(8,128)} %pupil_ref.3) | copy-start | bytes 6291460
  28.3 15.3 %copy-start.3 = (bf16[512,1024]{1,0:T(8,128)(2,1)S(1)}, bf16[512,1024]{1,0:T(8,128)(2,1)}, u32[]{:S(2)}) copy-start(bf16[512,1024]{1,0:T(8,128)(2,1)} %constant.12.clone.map_ref) | copy-start | bytes 3145732
  28.5 31.6 %copy-start.1 = (bf16[512,4096]{1,0:T(8,128)(2,1)S(1)}, bf16[512,4096]{1,0:T(8,128)(2,1)}, u32[]{:S(2)}) copy-start(bf16[512,4096]{1,0:T(8,128)(2,1)} %constant.13.clone.matrix_ref) | copy-start | bytes 12582916
  28.5 45.7 %copy-start.2 = (bf16[1024,512]{1,0:T(8,128)(2,1)S(1)}, bf16[1024,512]{1,0:T(8,128)(2,1)}, u32[]{:S(2)}) copy-start(bf16[1024,512]{1,0:T(8,128)(2,1)} %constant.14.clone.map_ref) | copy-start | bytes 3145732

commit v12 on v10

--- a/solution.py
+++ b/solution.py
@@ -19,7 +19,7 @@
 KERN = 8
 DEVICES = ROWS * KERN
 CHUNK = 16
-QUARTERS = 4
+QUARTERS = 2
 QUARTER = MASK // QUARTERS
 
 steepness = 4.0

time: 116 us -> 116 us (level)
  no operation moved by 1% of the time
where the time goes in v12:
time: 116 us
  blocking collectives  95.8 us (83%)
  Pallas kernels  19.6 us (17%)
    all_to_all x6, blocking collectives, exchange(): return lax.all_to_all(values, axes, 0, 0, tiled=True)  95.8 us
    pallas_call x1, Pallas kernels, mask_update(): pl.pallas_call(update_kernel, in_specs=[hbm] * 3, out_specs=hbm, out_shap...  6.89 us
    pallas_call x1, Pallas kernels, mask_spectrum(): pl.pallas_call(spectrum_kernel, in_specs=[pl.BlockSpec(memory_space=pltpu...  5.67 us
    pallas_call x1, Pallas kernels, coarse_adjoint(): pl.pallas_call(adjoint_kernel, in_specs=[pl.BlockSpec(memory_space=pltpu....  2.61 us

profile of v12, /device:TPU:1, one launch (start us, length us, event | category | flops | bytes accessed | tf_op | source)
XLA Modules:
  0.0 115.7 jit_solution(17725666597272184243)
XLA Ops:
  0.0 5.7 %mask_spectrum.1 = (bf16[128,8,128]{2,1,0:T(8,128)(2,1)S(1)}, bf16[512,512]{1,0:T(8,128)(2,1)S(1)}) custom-call(f32[128,16384]{1,0:T(8,128)} %mask_ref.3, f32[4928,512]{1,0:T(8,128)} %constant.9.clone.constant_ref, s32[256,512]{1,0:T(8,128)} %target_ref.1), custom_call_target="tpu_custom_call" | custom-call | tf_op jit(solution)/shard_map/mask_spectrum/pallas_call | solution.py:309
  5.7 22.6 %all_to_all.30.parts_ref = bf16[128,8,128]{2,1,0:T(8,128)(2,1)S(1)} all-to-all(bf16[128,8,128]{2,1,0:T(8,128)(2,1)S(1)} %get-tuple-element.9), channel_id=1, replica_groups=mesh['rows'=16,'kern'=8] {'kern','rows'}, dimensions={0} | all-to-all | bytes 524288 | tf_op jit(solution)/shard_map/all_to_all | solution.py:617
  28.3 0.0 copy-start
  28.3 0.0 copy-start.2
  28.3 0.2 total_tiles.1
  28.4 0.0 copy-start.1
  28.4 15.1 %all_to_all.31.tiles_ref = bf16[128,8,128]{2,1,0:T(8,128)(2,1)S(1)} all-to-all(bf16[128,8,128]{2,1,0:T(8,128)(2,1)S(1)} %total_tiles.1), channel_id=1, replica_groups=mesh['rows'=16,'kern'=8] {'kern','rows'}, dimensions={0} | all-to-all | bytes 524288 | tf_op jit(solution)/shard_map/all_to_all | solution.py:617
  43.5 0.0 copy-done
  43.5 0.0 copy-done.2
  43.5 2.0 %coarse_fields.1 = (f32[2,512,1024]{2,1,0:T(8,128)S(1)}, bf16[8,3,32,512]{3,2,1,0:T(8,128)(2,1)S(1)}) custom-call(bf16[128,8,128]{2,1,0:T(8,128)(2,1)S(1)} %all_to_all.31.tiles_ref, f32[2,2,2,256,256]{4,3,2,1,0:T(8,128)S(1)} %copy-done, bf16[512,512]{1,0:T(8,128)(2,1)S(1)} %get-tuple-element.10.grid_ref, bf16[512,1024]{1,0:T(8,128)(2,1)S(1)} %copy-done.2), custom_call_target="tpu_custom_call" | custom-call | tf_op jit(solution)/shard_map/coarse_fields/pallas_call | solution.py:377
  45.6 14.4 %all_to_all.32.parts_ref = bf16[8,3,32,512]{3,2,1,0:T(8,128)(2,1)S(1)} all-to-all(bf16[8,3,32,512]{3,2,1,0:T(8,128)(2,1)S(1)} %get-tuple-element.12), channel_id=1, replica_groups=mesh['rows'=16,'kern'=8] {'kern'}, dimensions={0} | all-to-all | bytes 1572864 | tf_op jit(solution)/shard_map/all_to_all | solution.py:617
  60.0 0.0 copy-done.1
  60.0 2.6 %coarse_adjoint.1 = bf16[8,2,32,512]{3,2,1,0:T(8,128)(2,1)S(1)} custom-call(bf16[8,3,32,512]{3,2,1,0:T(8,128)(2,1)S(1)} %all_to_all.32.parts_ref, bf16[512,4096]{1,0:T(8,128)(2,1)S(1)} %copy-done.1), custom_call_target="tpu_custom_call" | custom-call | tf_op jit(solution)/shard_map/coarse_adjoint/pallas_call | solution.py:425
  62.6 11.5 %all_to_all.33.adjoint_ref = bf16[8,2,32,512]{3,2,1,0:T(8,128)(2,1)S(1)} all-to-all(bf16[8,2,32,512]{3,2,1,0:T(8,128)(2,1)S(1)} %coarse_adjoint.1), channel_id=1, replica_groups=mesh['rows'=16,'kern'=8] {'kern'}, dimensions={0} | all-to-all | bytes 1048576 | tf_op jit(solution)/shard_map/all_to_all | solution.py:617
  74.1 2.2 %spectrum_gradient.1 = bf16[128,8,128]{2,1,0:T(8,128)(2,1)S(1)} custom-call(f32[2,512,1024]{2,1,0:T(8,128)S(1)} %get-tuple-element.11.field_ref, bf16[8,2,32,512]{3,2,1,0:T(8,128)(2,1)S(1)} %all_to_all.33.adjoint_ref, f32[2,2,2,256,256]{4,3,2,1,0:T(8,128)S(1)} %copy-done, bf16[512,512]{1,0:T(8,128)(2,1)S(1)} %get-tuple-element.10.grid_ref, ...), custom_call_target="tpu_custom_call" | custom-call | tf_op jit(solution)/shard_map/spectrum_gradient/pallas_call | solution.py:469
  76.4 17.1 %all_to_all.34 = bf16[128,8,128]{2,1,0:T(8,128)(2,1)S(1)} all-to-all(bf16[128,8,128]{2,1,0:T(8,128)(2,1)S(1)} %spectrum_gradient.1), channel_id=1, replica_groups=mesh['rows'=16,'kern'=8] {'kern','rows'}, dimensions={0} | all-to-all | bytes 524288 | tf_op jit(solution)/shard_map/all_to_all | solution.py:617
  93.4 0.1 reduce_sum.12
  93.6 15.0 %all_to_all.35.tiles_ref = bf16[128,8,128]{2,1,0:T(8,128)(2,1)S(1)} all-to-all(bf16[128,8,128]{2,1,0:T(8,128)(2,1)S(1)} %broadcast_in_dim.2), channel_id=1, replica_groups=mesh['rows'=16,'kern'=8] {'kern','rows'}, dimensions={0} | all-to-all | bytes 524288 | tf_op jit(solution)/shard_map/all_to_all | solution.py:617
  108.7 6.9 %mask_update.1 = f32[128,16384]{1,0:T(8,128)} custom-call(bf16[128,8,128]{2,1,0:T(8,128)(2,1)S(1)} %all_to_all.35.tiles_ref, f32[4928,512]{1,0:T(8,128)} %constant.9.clone.constant_ref, f32[128,16384]{1,0:T(8,128)} %mask_ref.3), custom_call_target="tpu_custom_call" | custom-call | tf_op jit(solution)/shard_map/mask_update/pallas_call | solution.py:589
  (1 shorter events, 0.0 us)
Async XLA Ops:
  28.3 15.3 %copy-start = (f32[2,2,2,256,256]{4,3,2,1,0:T(8,128)S(1)}, f32[2,2,2,256,256]{4,3,2,1,0:T(8,128)}, u32[]{:S(2)}) copy-start(f32[2,2,2,256,256]{4,3,2,1,0:T(8,128)} %pupil_ref.3) | copy-start | bytes 6291460
  28.3 15.3 %copy-start.2 = (bf16[512,1024]{1,0:T(8,128)(2,1)S(1)}, bf16[512,1024]{1,0:T(8,128)(2,1)}, u32[]{:S(2)}) copy-start(bf16[512,1024]{1,0:T(8,128)(2,1)} %constant.10.clone.map_ref) | copy-start | bytes 3145732
  28.4 31.6 %copy-start.1 = (bf16[512,4096]{1,0:T(8,128)(2,1)S(1)}, bf16[512,4096]{1,0:T(8,128)(2,1)}, u32[]{:S(2)}) copy-start(bf16[512,4096]{1,0:T(8,128)(2,1)} %constant.11.clone.matrix_ref) | copy-start | bytes 12582916
